TPU v7x, 128 devices: a whole 4x4x4 slice. The times are simulated.
128 devices in a mesh: gx: 8 (over x, core), gy: 16 (over y, z).
Axes of the slice: x: 4, y: 4, z: 4, core: 2. Of those that a mesh axis runs over, the one named last changes fastest.
Arguments:
- tokens: bfloat16 [1024, 18432], P(None, ('gx', 'gy')), may hold values from -6 to 6
- w_query: bfloat16 [18432, 12288], P('gx', 'gy'), may hold values from -0.046875 to 0.046875
- w_keyvalue: bfloat16 [18432, 512], P('gx'), may hold values from -0.21875 to 0.21875
- w_output: bfloat16 [12288, 18432], P('gy', 'gx'), may hold values from -0.0546875 to 0.0546875
- key_cache: bfloat16 [1024, 1024, 256], P(('gx', 'gy')), may hold values from -400 to 400
- value_cache: bfloat16 [1024, 1024, 256], P(('gx', 'gy')), may hold values from -6 to 6
Outputs:
- layer_out: bfloat16 [1024, 18432], P(None, ('gx', 'gy'))
- new_keyvalue: bfloat16 [1024, 512], P(('gx', 'gy'))
All inputs are finite; a program needn't handle non-finite values.
Results may differ from a plain program's by a relative error of at most 0.02.
Values may be sent and summed in bfloat16 or wider, within the bound.
No kernel may reach another device: no remote copies, remote signals or barrier semaphores. Data moves between devices by JAX's collectives and lax.ppermute only.
A program may use at most 128 MiB of HBM per device.

v0:
```python
import jax
import jax.numpy as jnp
from jax import lax
from jax.sharding import PartitionSpec as P


def shards(tokens, w_query, w_keyvalue, w_output, key_cache, value_cache):
    n_gx = lax.axis_size("gx")
    n_gy = lax.axis_size("gy")
    column = lax.axis_index("gy")
    head_size = key_cache.shape[2]
    rows_dev = key_cache.shape[0]
    features = lax.all_gather(tokens, "gy", axis=1, tiled=True)
    query_part = jnp.dot(features, w_query, preferred_element_type=jnp.float32)
    grouped = features.reshape(n_gx, n_gy, rows_dev, features.shape[1])
    owned = lax.dynamic_index_in_dim(grouped, column, 1, keepdims=False)
    owned = owned.reshape(n_gx * rows_dev, features.shape[1])
    keyvalue_part = jnp.dot(owned, w_keyvalue, preferred_element_type=jnp.float32)
    query_rows, keyvalue_rows = (
        lax.psum_scatter(query_part, "gx", scatter_dimension=0, tiled=True),
        lax.psum_scatter(keyvalue_part, "gx", scatter_dimension=0, tiled=True),
    )
    query_rows = query_rows.astype(jnp.bfloat16)
    new_keyvalue = keyvalue_rows.astype(jnp.bfloat16)
    queries = lax.all_to_all(query_rows, "gy", split_axis=0, concat_axis=1, tiled=True)
    queries = queries.reshape(rows_dev, -1, head_size)
    new_key = new_keyvalue[:, :head_size]
    new_value = new_keyvalue[:, head_size:]
    score_scale = 1.0 / head_size**0.5
    scores = (
        jnp.einsum("bhe,bte->bht", queries, key_cache, preferred_element_type=jnp.float32)
        * score_scale
    )
    score_new = (
        jnp.einsum("bhe,be->bh", queries, new_key, preferred_element_type=jnp.float32) * score_scale
    )
    highest = jnp.maximum(jnp.max(scores, axis=2), score_new)
    raised = jnp.exp(scores - highest[:, :, None])
    raised_new = jnp.exp(score_new - highest)
    denominator = jnp.sum(raised, axis=2) + raised_new
    probs = (raised / denominator[:, :, None]).astype(jnp.bfloat16)
    prob_new = (raised_new / denominator).astype(jnp.bfloat16)
    mixed = jnp.einsum("bht,bte->bhe", probs, value_cache, preferred_element_type=jnp.float32)
    mixed = (
        mixed + prob_new.astype(jnp.float32)[:, :, None] * new_value.astype(jnp.float32)[:, None, :]
    )
    attended = mixed.astype(jnp.bfloat16).reshape(rows_dev, -1)
    by_heads = lax.all_to_all(attended, "gy", split_axis=1, concat_axis=0, tiled=True)
    partials = jnp.dot(
        lax.all_gather(by_heads, "gx", axis=0, tiled=True),
        w_output,
        preferred_element_type=jnp.float32,
    )
    layer_out = lax.psum_scatter(
        partials.astype(jnp.bfloat16), "gy", scatter_dimension=1, tiled=True
    )
    return (layer_out, new_keyvalue)


def solution(mesh):
    return jax.shard_map(
        shards,
        mesh=mesh,
        in_specs=(
            P(None, ("gx", "gy")),
            P("gx", "gy"),
            P("gx", None),
            P("gy", "gx"),
            P(("gx", "gy"), None, None),
            P(("gx", "gy"), None, None),
        ),
        out_specs=(P(None, ("gx", "gy")), P(("gx", "gy"), None)),
        check_vma=False,
    )
```

profile of v0, /device:TPU:0, one launch (start us, length us, event | category | flops | bytes accessed | tf_op | source)
XLA Modules:
  0.0 297.9 jit_solution(6924533608604405180)
XLA Ops:
  7.2 0.0 copy-start
  7.2 0.0 all-gather.3.cloned.1.call-start
  7.2 0.7 all-gather.3.cloned.1.call-update
  7.9 0.0 reduce-scatter.6.cloned.1.call-start
  8.0 58.8 %all-gather.3.cloned.1.call-done = bf16[1024,2304]{0,1:T(8,128)(2,1)} async-done(((bf16[1024,144]{0,1:T(8,128)(2,1)}), bf16[1024,2304]{0,1:T(8,128)(2,1)}) %all-gather.3.cloned.1.call-update) | async-done | bytes 4718608 | tf_op jit(solution)/shard_map/all_gather | solution.py:13
  66.8 6.8 %copy.13 = bf16[1024,2304]{1,0:T(8,128)(2,1)} copy(bf16[1024,2304]{0,1:T(8,128)(2,1)} %all-gather.3.cloned.1.call-done) | data formatting | bytes 9437184 | tf_op jit(solution)/shard_map/all_gather | solution.py:13
  73.6 3.0 fusion.4
  76.5 0.0 reduce-scatter.6.cloned.1.call-update
  76.6 0.0 reduce-scatter.4.cloned.1.call-start
  76.6 9.0 %fusion.13 = f32[1024,768]{1,0:T(8,128)} fusion(bf16[1024,2304]{0,1:T(8,128)(2,1)} %all-gather.3.cloned.1.call-done, bf16[2304,768]{1,0:T(8,128)(2,1)} %param.7), kind=kOutput, calls=%fused_computation.24 | convolution fusion | flops 3623878656 | bytes 11403264 | tf_op jit(solution)/shard_map/dot_general | solution.py:14
  85.6 0.0 reduce-scatter.4.cloned.1.call-update
  85.7 20.8 %reduce-scatter.6.cloned.1.call-done = f32[8,512]{1,0:T(8,128)} async-done(((f32[64,512]{1,0:T(8,128)}), f32[8,512]{1,0:T(8,128)}) %reduce-scatter.6.cloned.1.call-update) | async-done | bytes 16400 | tf_op jit(solution)/shard_map/reduce_scatter | solution.py:21
  106.5 0.7 convert_element_type.25
  107.2 0.0 copy-start.1
  107.2 36.5 %reduce-scatter.4.cloned.1.call-done = f32[128,768]{1,0:T(8,128)} async-done(((f32[1024,768]{1,0:T(8,128)}), f32[128,768]{1,0:T(8,128)}) %reduce-scatter.4.cloned.1.call-update) | async-done | bytes 393232 | tf_op jit(solution)/shard_map/reduce_scatter | solution.py:20
  143.7 1.7 convert_bitcast_fusion
  145.4 7.0 %all-to-all-start = ((bf16[16,8,768]{2,1,0:T(8,128)(2,1)}), bf16[16,8,768]{2,1,0:T(8,128)(2,1)}, u32[]{:S(2)}, u32[]{:S(2)}) async-start(bf16[16,8,768]{2,1,0:T(8,128)(2,1)} %convert_bitcast_fusion), calls=%async_computation.1 | async-start | bytes 393216 | tf_op jit(solution)/shard_map/all_to_all | solution.py:25
  152.4 0.0 all-gather.5.cloned.1.call-start
  152.5 0.6 slice_convert_fusion
  153.1 7.5 %all-to-all-done = bf16[16,8,768]{2,1,0:T(8,128)(2,1)} async-done(((bf16[16,8,768]{2,1,0:T(8,128)(2,1)}), bf16[16,8,768]{2,1,0:T(8,128)(2,1)}, u32[]{:S(2)}, u32[]{:S(2)}) %all-to-all-start) | async-done | bytes 196640 | tf_op jit(solution)/shard_map/all_to_all | solution.py:25
  160.5 1.6 copy.12
  162.2 1.7 reshape.27
  163.9 1.1 fusion.7
  164.9 0.0 copy-start.2
  164.9 3.9 %fusion.12 = (f32[8,48]{1,0:T(8,128)S(1)}, f32[8,48,1024]{2,1,0:T(8,128)S(1)}) fusion(bf16[8,48,256]{2,1,0:T(8,128)(2,1)} %reshape.27, bf16[8,1024,256]{2,1,0:T(8,128)(2,1)} %param.10), kind=kOutput, calls=%fused_computation.23 | convolution fusion | flops 202112640 | bytes 5965312 | tf_op jit(solution)/shard_map/bhe,bte->bht/dot_general | solution.py:31
  168.8 0.0 copy-done.1
  168.9 0.4 fusion
  169.3 0.0 copy-done.2
  169.3 1.5 fusion.1
  170.8 1.7 all_to_all.29
  172.5 1.0 copy.14
  173.5 11.7 %all_to_all.35 = bf16[8,16,768]{2,0,1:T(8,128)(2,1)} all-to-all(bf16[8,16,768]{2,0,1:T(8,128)(2,1)S(1)} %copy.14), channel_id=1, replica_groups=mesh['gx'=8,'gy'=16] {'gy'}, dimensions={1} | all-to-all | bytes 393216 | tf_op jit(solution)/shard_map/all_to_all | solution.py:48
  185.2 0.0 all-gather.5.cloned.1.call-update
  185.2 0.0 reduce-scatter.8.cloned.1.call-start
  185.3 20.1 %all-gather.5.cloned.1.call-done = bf16[1024,768]{1,0:T(8,128)(2,1)} async-done(((bf16[128,768]{1,0:T(8,128)(2,1)}), bf16[1024,768]{1,0:T(8,128)(2,1)}) %all-gather.5.cloned.1.call-update) | async-done | bytes 1572880 | tf_op jit(solution)/shard_map/all_gather | solution.py:50
  205.4 0.0 copy-done
  205.4 7.0 %convolution_convert_fusion = bf16[1024,2304]{0,1:T(8,128)(2,1)} fusion(bf16[1024,768]{1,0:T(8,128)(2,1)} %all-gather.5.cloned.1.call-done, bf16[768,2304]{1,0:T(8,128)(2,1)S(1)} %copy-done), kind=kOutput, calls=%fused_computation | convolution fusion | flops 3626237952 | bytes 9830400 | tf_op jit(solution)/shard_map/dot_general | solution.py:49
  212.4 0.0 reduce-scatter.8.cloned.1.call-update
  212.4 79.0 %reduce-scatter.8.cloned.1.call-done = bf16[1024,144]{0,1:T(8,128)(2,1)} async-done(((bf16[1024,2304]{0,1:T(8,128)(2,1)}), bf16[1024,144]{0,1:T(8,128)(2,1)}) %reduce-scatter.8.cloned.1.call-update) | async-done | bytes 294928 | tf_op jit(solution)/shard_map/reduce_scatter | solution.py:54
  (2 shorter events, 0.0 us)
Async XLA Ops:
  7.2 198.3 %copy-start = (bf16[768,2304]{1,0:T(8,128)(2,1)S(1)}, bf16[768,2304]{1,0:T(8,128)(2,1)}, u32[]{:S(2)}) copy-start(bf16[768,2304]{1,0:T(8,128)(2,1)} %param.9) | copy-start | bytes 10616836
  7.2 59.6 %all-gather.3.cloned.1.call-start = ((), (), s32[]{:S(2)}) async-start(), calls=%async_computation.5 | async-start | bytes 5013504 | tf_op jit(solution)/shard_map/all_gather | solution.py:13
  7.9 98.6 %reduce-scatter.6.cloned.1.call-start = ((), (), s32[]{:S(2)}) async-start(), calls=%async_computation.7 | async-start | bytes 147456 | tf_op jit(solution)/shard_map/reduce_scatter | solution.py:21
  76.6 67.1 %reduce-scatter.4.cloned.1.call-start = ((), (), s32[]{:S(2)}) async-start(), calls=%async_computation.6 | async-start | bytes 3538944 | tf_op jit(solution)/shard_map/reduce_scatter | solution.py:20
  107.2 61.6 %copy-start.1 = (bf16[8,512]{1,0:T(8,128)(2,1)}, bf16[8,512]{1,0:T(8,128)(2,1)S(1)}, u32[]{:S(2)}) copy-start(bf16[8,512]{1,0:T(8,128)(2,1)S(1)} %convert_element_type.25) | copy-start | bytes 24580
  145.4 15.2 %all-to-all-start = ((bf16[16,8,768]{2,1,0:T(8,128)(2,1)}), bf16[16,8,768]{2,1,0:T(8,128)(2,1)}, u32[]{:S(2)}, u32[]{:S(2)}) async-start(bf16[16,8,768]{2,1,0:T(8,128)(2,1)} %convert_bitcast_fusion), calls=%async_computation.1 | async-start | bytes 393216 | tf_op jit(solution)/shard_map/all_to_all | solution.py:25
  152.4 53.0 %all-gather.5.cloned.1.call-start = ((), (), s32[]{:S(2)}) async-start(), calls=%async_computation.8 | async-start | bytes 1769472 | tf_op jit(solution)/shard_map/all_gather | solution.py:50
  164.9 4.3 %copy-start.2 = (bf16[8,1024,256]{2,1,0:T(8,128)(2,1)S(1)}, bf16[8,1024,256]{2,1,0:T(8,128)(2,1)}, u32[]{:S(2)}) copy-start(bf16[8,1024,256]{2,1,0:T(8,128)(2,1)} %param.11) | copy-start | bytes 12582916
  185.2 106.2 %reduce-scatter.8.cloned.1.call-start = ((), (), s32[]{:S(2)}) async-start(), calls=%async_computation.9 | async-start | bytes 5013504 | tf_op jit(solution)/shard_map/reduce_scatter | solution.py:54
Sparse Core Ops, SparseCore 0:
  10.2 56.5 all-gather.2
  76.7 29.7 reduce-scatter.5
  109.0 34.5 reduce-scatter.3
  185.4 20.0 all-gather.4
  212.5 78.8 reduce-scatter.7
where the time goes:
time: 299 us; the launch traced here: 298 us
  waiting for transfers between devices  224 us (75%)
  matrix products  25.4 us (8%)
  between operations  13.8 us (5%)
  local copies, waits for them, and re-layouts  12.8 us (4%)
  blocking collectives  11.7 us (4%)
  starting transfers between devices  7.24 us (2%)
  other arithmetic  3.41 us (1%)
    reduce_scatter x1, waiting for transfers between devices, shards(): lax.psum_scatter(partials.astype(jnp.bfloat16), 'gy', scatter_dimension=1...  79 us
    all_gather x1, waiting for transfers between devices, shards(): features = lax.all_gather(tokens, 'gy', axis=1, tiled=True)  58.8 us
    reduce_scatter x1, waiting for transfers between devices, shards(): lax.psum_scatter(query_part, 'gx', scatter_dimension=0, tiled=True)  36.5 us
    reduce_scatter x1, waiting for transfers between devices, shards(): lax.psum_scatter(keyvalue_part, 'gx', scatter_dimension=0, tiled=True)  20.8 us
    all_gather x1, waiting for transfers between devices, shards(): lax.all_gather(by_heads, 'gx', axis=0, tiled=True)  20.1 us
    all_to_all x1, blocking collectives, shards(): lax.all_to_all(attended, 'gy', split_axis=1, concat_axis=0, tiled=True)  11.7 us
    dot_general x1, matrix products, shards(): query_part = jnp.dot(features, w_query, preferred_element_type=jnp.float32)  9.03 us
    all_to_all x1, waiting for transfers between devices, shards(): lax.all_to_all(query_rows, 'gy', split_axis=0, concat_axis=1, tiled=True)  7.49 us
  transfers between devices with their start and end apart: 6, of which 6 were waited for; matrix products, arithmetic and copies ran while one was open for 3% of the time, Pallas kernels for 0%

commit v1 on v0

v1 whole, which is shorter than its diff:
```python
import jax
import jax.numpy as jnp
from jax import lax
from jax.sharding import Mesh
from jax.sharding import PartitionSpec as P

AXES = ("x", "c", "y", "z")
F32 = jnp.float32
BF16 = jnp.bfloat16


def linear(x, c, y, z):
    return ((x * 2 + c) * 4 + y) * 4 + z


def partner_pairs(axis, step):
    pairs = []
    for x in range(4):
        for c in range(2):
            for y in range(4):
                for z in range(4):
                    other = {"x": x, "y": y, "z": z}
                    other[axis] ^= (1, 3)[step ^ c]
                    pairs.append((linear(x, c, y, z), linear(other["x"], c, other["y"], other["z"])))
    return pairs


def exchange(v, axis, step):
    return lax.ppermute(v, AXES, partner_pairs(axis, step))


def core_swap(v):
    return lax.ppermute(v, "c", [(0, 1), (1, 0)])


def relative_blocks(first, second):
    c = lax.axis_index("c")
    m0 = jnp.where(c == 0, 1, 3)
    m1 = jnp.where(c == 0, 3, 1)
    blocks = []
    for p in range(16):
        at = {"y": lax.axis_index("y"), "z": lax.axis_index("z")}
        b = [(p >> i) & 1 for i in range(4)]
        at[first] = at[first] ^ (m0 * b[0]) ^ (m1 * b[1])
        at[second] = at[second] ^ (m0 * b[2]) ^ (m1 * b[3])
        blocks.append(at["y"] * 4 + at["z"])
    return blocks


def take_rows(w, blocks, n):
    return jnp.concatenate([lax.dynamic_slice_in_dim(w, b * n, n, 0) for b in blocks], axis=0)


def shards(tokens, w_query, w_keyvalue, w_output, key_cache, value_cache):
    c = lax.axis_index("c")
    column = lax.axis_index("y") * 4 + lax.axis_index("z")
    rows_dev, _, head_size = key_cache.shape
    feat = tokens.shape[1]
    kv_cols = w_keyvalue.shape[1] // 16
    q_cols = w_query.shape[1]

    by_core = tokens.T.reshape(feat, 4, 2, 128)
    own = lax.dynamic_index_in_dim(by_core, c, 2, keepdims=False).reshape(feat, 512)
    oth = lax.dynamic_index_in_dim(by_core, 1 - c, 2, keepdims=False).reshape(feat, 512)
    a, b = oth, own
    for axis_a, axis_b, step in (("z", "y", 0), ("z", "y", 1), ("y", "z", 0)):
        ra, rb = exchange(a, axis_a, step), exchange(b, axis_b, step)
        ra, rb = lax.optimization_barrier((ra, rb))
        a, b = jnp.concatenate([a, ra], 0), jnp.concatenate([b, rb], 0)
    la, lb = exchange(a, "y", 1), exchange(b, "z", 1)

    kv_own = lax.dynamic_slice_in_dim(w_keyvalue, column * kv_cols, kv_cols, 1)
    w_all = jnp.concatenate([w_query, kv_own], 1)
    wa = take_rows(w_all, relative_blocks("z", "y"), feat)
    wb = take_rows(w_all, relative_blocks("y", "z"), feat)
    half = 8 * feat

    def product(v, w):
        return lax.dot_general(v, w, (((0,), (0,)), ((), ())), preferred_element_type=F32)

    def widen(v):
        q, kv = v[:, :q_cols], v[:, q_cols:]
        hi = lax.reduce_precision(kv, 8, 7)
        return jnp.concatenate([q.astype(BF16), hi.astype(BF16), (kv - hi).astype(BF16)], 1)

    def narrow(v):
        v = v.astype(F32)
        return jnp.concatenate([v[..., :q_cols], v[..., q_cols : q_cols + kv_cols] + v[..., q_cols + kv_cols :]], -1)

    part_oth = product(a, wa[:half]) + product(la, wa[half:])
    got = core_swap(widen(part_oth))
    part_own = product(b, wb[:half]) + product(lb, wb[half:])
    part = widen(part_own + narrow(got))
    part = lax.all_to_all(part.reshape(64, rows_dev, -1), ("x", "y", "z"), 0, 0, tiled=True)
    whole = jnp.sum(narrow(part).reshape(4, 16, rows_dev, -1), axis=0).astype(BF16)
    queries = whole[:, :, :q_cols].transpose(1, 0, 2).reshape(rows_dev, -1, head_size)
    new_keyvalue = whole[:, :, q_cols:].transpose(1, 0, 2).reshape(rows_dev, -1)

    new_key = new_keyvalue[:, :head_size]
    new_value = new_keyvalue[:, head_size:]
    score_scale = 1.0 / head_size**0.5
    scores = jnp.einsum("bhe,bte->bht", queries, key_cache, preferred_element_type=F32) * score_scale
    score_new = jnp.einsum("bhe,be->bh", queries, new_key, preferred_element_type=F32) * score_scale
    highest = jnp.maximum(jnp.max(scores, axis=2), score_new)
    raised = jnp.exp(scores - highest[:, :, None])
    raised_new = jnp.exp(score_new - highest)
    denominator = jnp.sum(raised, axis=2) + raised_new
    probs = (raised / denominator[:, :, None]).astype(BF16)
    prob_new = (raised_new / denominator).astype(BF16)
    mixed = jnp.einsum("bht,bte->bhe", probs, value_cache, preferred_element_type=F32)
    mixed = mixed + prob_new.astype(F32)[:, :, None] * new_value.astype(F32)[:, None, :]
    attended = mixed.astype(BF16).reshape(rows_dev, 16, q_cols).transpose(1, 0, 2)

    spread = jnp.broadcast_to(attended[None], (4, 16, rows_dev, q_cols)).reshape(64, rows_dev, q_cols)
    mine = lax.all_to_all(spread, ("x", "y", "z"), 0, 0, tiled=True).reshape(512, q_cols)
    theirs = core_swap(mine)

    wo = take_rows(w_output.T, relative_blocks("z", "y"), feat)

    def outward(v):
        return lax.dot_general(wo, v, (((1,), (1,)), ((), ())), preferred_element_type=F32).astype(BF16)

    p = outward(mine).reshape(2, 2, 2, 2, feat, 512)
    q = outward(theirs).reshape(2, 2, 2, 2, feat, 512).transpose(2, 3, 0, 1, 4, 5)
    p, q = p.reshape(16 * feat, 512), q.reshape(16 * feat, 512)
    for axis_p, axis_q, step in (("y", "z", 1), ("y", "z", 0), ("z", "y", 1), ("z", "y", 0)):
        n = p.shape[0] // 2
        rp, rq = exchange(p[n:], axis_p, step), exchange(q[n:], axis_q, step)
        p = (p[:n].astype(F32) + rp.astype(F32)).astype(BF16)
        q = (q[:n].astype(F32) + rq.astype(F32)).astype(BF16)
        if step == 1 or axis_p == "y":
            p, q = lax.optimization_barrier((p, q))
    p, q = p.reshape(feat, 4, 128), q.reshape(feat, 4, 128)
    first = jnp.where(c == 0, p, q)
    second = jnp.where(c == 0, q, p)
    out = jnp.stack([first, second], axis=2).reshape(feat, 1024)
    return out.T, new_keyvalue


def solution(mesh):
    fine = Mesh(mesh.devices.reshape(4, 2, 4, 4), AXES)
    gx, gy = ("x", "c"), ("y", "z")
    every = (*gx, *gy)
    return jax.shard_map(
        shards,
        mesh=fine,
        in_specs=(P(None, every), P(gx, gy), P(gx, None), P(gy, gx), P(every, None, None), P(every, None, None)),
        out_specs=(P(None, every), P(every, None)),
        check_vma=False,
    )
```

time: 299 us -> 211 us (0.71)
  waiting for transfers between devices: 224 us -> 61.4 us
  other arithmetic: 3.41 us -> 36.6 us
  blocking collectives: 11.7 us -> 38.4 us
  local copies, waits for them, and re-layouts: 12.8 us -> 29.3 us
  starting transfers between devices: 7.24 us -> 21.7 us
  between operations: 13.8 us -> 1.2 us
  matrix products: 25.4 us -> 20.1 us
    reduce_scatter x3 -> x0, waiting for transfers between devices: 136 us -> none  [the longest x1 79 us: shards(): lax.psum_scatter(partials.astype(jnp.bfloat16), 'gy', scatter_dimension=1...]
    all_gather x2 -> x0, waiting for transfers between devices: 79 us -> none  [the longest x1 58.8 us: shards(): features = lax.all_gather(tokens, 'gy', axis=1, tiled=True)]
    ppermute x0 -> x18, waiting for transfers between devices: none -> 61.4 us  [the longest x16 61.4 us: exchange(): return lax.ppermute(v, AXES, partner_pairs(axis, step))]
    all_to_all x1 -> x2, blocking collectives: 11.7 us -> 38.4 us  [the longest x1 20.6 us: shards(): lax.all_to_all(part.reshape(64, rows_dev, -1), ('x', 'y', 'z'), 0, 0, til...]
    unnamed x0 -> x20, other arithmetic: none -> 26.4 us
    ppermute x0 -> x18, starting transfers between devices: none -> 21.7 us  [the longest x16 21.5 us: exchange(): return lax.ppermute(v, AXES, partner_pairs(axis, step))]
    dynamic_slice x0 -> x3, local copies, waits for them, and re-layouts: none -> 8.71 us  [the longest x1 5.81 us: take_rows(): lax.dynamic_slice_in_dim(w, b * n, n, 0)]
    concatenate x0 -> x4, local copies, waits for them, and re-layouts: none -> 7.94 us  [the longest x1 7.27 us: take_rows(): jnp.concatenate([lax.dynamic_slice_in_dim(w, b * n, n, 0) for b in blocks...]
  transfers between devices with their start and end apart: 6 -> 18, of which waited for: 6 -> 13; matrix products, arithmetic and copies ran while one was open for 3% -> 31% of each run, Pallas kernels for 0% -> 0%
where the time goes in v1:
time: 211 us; the launch traced here: 209 us
  waiting for transfers between devices  61.4 us (29%)
  blocking collectives  38.4 us (18%)
  other arithmetic  36.6 us (17%)
  local copies, waits for them, and re-layouts  29.3 us (14%)
  starting transfers between devices  21.7 us (10%)
  matrix products  20.1 us (10%)
    ppermute x16, waiting for transfers between devices, exchange(): return lax.ppermute(v, AXES, partner_pairs(axis, step))  61.4 us
    unnamed x20, other arithmetic  26.4 us
    ppermute x16, starting transfers between devices, exchange(): return lax.ppermute(v, AXES, partner_pairs(axis, step))  21.5 us
    all_to_all x1, blocking collectives, shards(): lax.all_to_all(part.reshape(64, rows_dev, -1), ('x', 'y', 'z'), 0, 0, til...  20.6 us
    all_to_all x1, blocking collectives, shards(): lax.all_to_all(spread, ('x', 'y', 'z'), 0, 0, tiled=True)  17.7 us
    dot_general x4, matrix products, product(): lax.dot_general(v, w, (((0,), (0,)), ((), ())), preferred_element_type=F32)  8.25 us
    concatenate x1, local copies, waits for them, and re-layouts, take_rows(): jnp.concatenate([lax.dynamic_slice_in_dim(w, b * n, n, 0) for b in blocks...  7.27 us
    dot_general x2, matrix products, outward(): lax.dot_general(wo, v, (((1,), (1,)), ((), ())), preferred_element_type=F32)  6.38 us
  transfers between devices with their start and end apart: 18, of which 13 were waited for; matrix products, arithmetic and copies ran while one was open for 31% of the time, Pallas kernels for 0%

profile of v1, /device:TPU:0, one launch (start us, length us, event | category | flops | bytes accessed | tf_op | source)
XLA Modules:
  0.0 208.8 jit_solution(988015435856055369)
XLA Ops:
  0.7 1.3 reshape.92
  2.0 1.8 dynamic-slice_reduce_fusion.1
  4.6 2.0 collective-permute-start
  7.2 1.6 collective-permute-start.1
  9.9 1.7 constant_dynamic-update-slice_fusion.31
  11.6 3.2 %copy.60 = bf16[1152,800]{1,0:T(8,128)(2,1)} copy(bf16[1152,800]{1,0:T(8,128)(2,1)} %constant_dynamic-update-slice_fusion.31) | data formatting | bytes 3686400
  14.8 1.5 constant_dynamic-update-slice_fusion.10
  16.3 1.5 constant_dynamic-update-slice_fusion.9
  17.8 1.5 constant_dynamic-update-slice_fusion.8
  19.3 1.5 constant_dynamic-update-slice_fusion.7
  20.8 1.5 constant_dynamic-update-slice_fusion.6
  22.3 1.7 constant_dynamic-update-slice_fusion.5
  24.0 1.5 constant_dynamic-update-slice_fusion.18
  25.5 1.5 constant_dynamic-update-slice_fusion.17
  27.0 1.5 constant_dynamic-update-slice_fusion.16
  28.4 1.5 constant_dynamic-update-slice_fusion.15
  29.9 1.5 constant_dynamic-update-slice_fusion.14
  31.4 1.6 constant_dynamic-update-slice_fusion.13
  34.1 2.6 %collective-permute-start.2 = (bf16[288,512]{1,0:T(8,128)(2,1)S(1)}, bf16[288,512]{1,0:T(8,128)(2,1)S(1)}, u32[]{:S(2)}, u32[]{:S(2)}) collective-permute-start(bf16[288,512]{1,0:T(8,128)(2,1)S(1)} %pad_maximum_fusion.5), channel_id=1, source_target_pairs={{0,3},{1,2},{2,1},{3,0},{4,7},{5,6},{6,5},{7,4},{8,11},{9,10},{10,... | collective-permute-start | bytes 884744 | tf_op jit(solution)/shard_map/ppermute | solution.py:29
  37.7 2.3 %collective-permute-start.3 = (bf16[288,512]{1,0:T(8,128)(2,1)S(1)}, bf16[288,512]{1,0:T(8,128)(2,1)S(1)}, u32[]{:S(2)}, u32[]{:S(2)}) collective-permute-start(bf16[288,512]{1,0:T(8,128)(2,1)S(1)} %pad_maximum_fusion.6), channel_id=1, source_target_pairs={{0,12},{1,13},{2,14},{3,15},{4,8},{5,9},{6,10},{7,11},{8,4},{9,5},... | collective-permute-start | bytes 884744 | tf_op jit(solution)/shard_map/ppermute | solution.py:29
  40.0 1.5 constant_dynamic-update-slice_fusion.28
  42.1 3.6 %collective-permute-done.3 = bf16[288,512]{1,0:T(8,128)(2,1)S(1)} collective-permute-done((bf16[288,512]{1,0:T(8,128)(2,1)S(1)}, bf16[288,512]{1,0:T(8,128)(2,1)S(1)}, u32[]{:S(2)}, u32[]{:S(2)}) %collective-permute-start.3) | collective-permute-done | bytes 294944 | tf_op jit(solution)/shard_map/ppermute | solution.py:29
  48.9 1.7 constant_dynamic-update-slice_fusion.4
  51.7 4.9 %collective-permute-done.4 = bf16[576,512]{1,0:T(8,128)(2,1)S(1)} collective-permute-done((bf16[576,512]{1,0:T(8,128)(2,1)S(1)}, bf16[576,512]{1,0:T(8,128)(2,1)S(1)}, u32[]{:S(2)}, u32[]{:S(2)}) %collective-permute-start.4) | collective-permute-done | bytes 589856 | tf_op jit(solution)/shard_map/ppermute | solution.py:29
  57.9 2.3 %collective-permute-start.7 = (bf16[1152,512]{1,0:T(8,128)(2,1)S(1)}, bf16[1152,512]{1,0:T(8,128)(2,1)S(1)}, u32[]{:S(2)}, u32[]{:S(2)}) collective-permute-start(bf16[1152,512]{1,0:T(8,128)(2,1)S(1)} %constant_dynamic-update-slice_fusion.20), channel_id=1, source_target_pairs={{0,12},{1,13},{2,14},{3,15},{4,8},{5,9},{6,10},{7,11},{8,4},{9,5},... | collective-permute-start | bytes 3538952 | tf_op jit(solution)/shard_map/ppermute | solution.py:29
  67.6 7.8 %collective-permute-done.7 = bf16[1152,512]{1,0:T(8,128)(2,1)S(1)} collective-permute-done((bf16[1152,512]{1,0:T(8,128)(2,1)S(1)}, bf16[1152,512]{1,0:T(8,128)(2,1)S(1)}, u32[]{:S(2)}, u32[]{:S(2)}) %collective-permute-start.7) | collective-permute-done | bytes 1179680 | tf_op jit(solution)/shard_map/ppermute | solution.py:29
  78.4 5.9 %collective-permute-done.6 = bf16[1152,512]{1,0:T(8,128)(2,1)S(1)} collective-permute-done((bf16[1152,512]{1,0:T(8,128)(2,1)S(1)}, bf16[1152,512]{1,0:T(8,128)(2,1)S(1)}, u32[]{:S(2)}, u32[]{:S(2)}) %collective-permute-start.6) | collective-permute-done | bytes 1179680 | tf_op jit(solution)/shard_map/ppermute | solution.py:29
  84.3 2.8 %fusion.30 = f32[512,800]{0,1:T(8,128)S(1)} fusion(bf16[1152,512]{1,0:T(8,128)(2,1)S(1)} %collective-permute-done.6, bf16[1152,800]{1,0:T(8,128)(2,1)} %get-tuple-element.31), kind=kOutput, calls=%fused_computation.165 | convolution fusion | flops 943718400 | bytes 4661248 | tf_op jit(solution)/shard_map/dot_general | solution.py:79
  87.6 2.9 %maximum_add_fusion = f32[512,800]{0,1:T(8,128)S(1)} fusion(f32[512,32]{0,1:T(8,128)S(1)} %slice_add_fusion.1, f32[512,768]{0,1:T(8,128)S(1)} %slice.137, f32[512,800]{0,1:T(8,128)S(1)} %fusion.30, bf16[1152,512]{1,0:T(8,128)(2,1)S(1)} %constant_dynamic-update-slice_fusion, bf16[1152,800]{1,0:T(8,128)(2,1)} %get-tuple-element.28), kind=kOutput, calls=%fused_computation.23 | convolution fusion | flops 944947200 | bytes 7938048 | tf_op jit(solution)/shard_map/dot_general | solution.py:79
  91.3 20.6 %all_to_all.10 = bf16[64,8,832]{2,1,0:T(8,128)(2,1)S(1)} all-to-all(bf16[64,8,832]{2,1,0:T(8,128)(2,1)S(1)} %bitcast.86), channel_id=1, replica_groups=mesh['x'=4,'c'=2,'y'=4,'z'=4] {'x','y','z'}, dimensions={0} | all-to-all | bytes 1703936 | tf_op jit(solution)/shard_map/all_to_all | solution.py:94
  113.0 3.8 %fusion.29 = (f32[8,48]{1,0:T(8,128)S(1)}, f32[8,48,1024]{2,1,0:T(8,128)S(1)}) fusion(bf16[8,48,256]{2,1,0:T(8,128)(2,1)S(1)} %reshape.97, bf16[8,1024,256]{2,1,0:T(8,128)(2,1)} %param.10), kind=kOutput, calls=%fused_computation.164 | convolution fusion | flops 202112640 | bytes 5965312 | tf_op jit(solution)/shard_map/bhe,bte->bht/dot_general | solution.py:102
  117.3 1.5 fusion.2
  118.8 1.7 reshape.99
  121.5 17.7 %all_to_all.11 = bf16[64,8,768]{2,1,0:T(8,128)(2,1)} all-to-all(bf16[64,8,768]{2,1,0:T(8,128)(2,1)S(1)} %bitcast.87), channel_id=1, replica_groups=mesh['x'=4,'c'=2,'y'=4,'z'=4] {'x','y','z'}, dimensions={0} | all-to-all | bytes 1572864 | tf_op jit(solution)/shard_map/all_to_all | solution.py:115
  139.3 5.8 %dynamic-slice_bitcast_fusion = (bf16[144,768]{0,1:T(8,128)(2,1)}, bf16[144,768]{0,1:T(8,128)(2,1)}, bf16[144,768]{0,1:T(8,128)(2,1)}, bf16[144,768]{0,1:T(8,128...) fusion(bf16[768,2304]{1,0:T(8,128)(2,1)S(1)} %copy-done.3, ...), kind=kLoop, calls=%fused_computation.59 | loop fusion | bytes 7077952 | tf_op jit(solution)/shard_map/dynamic_slice | solution.py:51
  145.1 7.3 %concatenate.54 = bf16[2304,768]{0,1:T(8,128)(2,1)S(1)} concatenate(bf16[144,768]{0,1:T(8,128)(2,1)} %get-tuple-element.55, bf16[144,768]{0,1:T(8,128)(2,1)} %get-tuple-element.54, bf16[144,768]{0,1:T(8,128)(2,1)} %get-tuple-element.53, bf16[144,768]{0,1:T(8,128)(2,1)} %get-tuple-element.52, bf16[144,768]{0,1:T(8,128)(2,1)} %get-tuple-element.51, ...), dimensions={0} | concatenate | bytes 7077888 | tf_op jit(solution)/shard_map/concatenate | solution.py:51
  152.4 3.2 %convolution_convert_fusion.1 = bf16[2304,512]{1,0:T(8,128)(2,1)S(1)} fusion(bf16[2304,768]{0,1:T(8,128)(2,1)S(1)} %concatenate.54, bf16[64,8,768]{2,1,0:T(8,128)(2,1)} %all_to_all.11), kind=kOutput, calls=%fused_computation.17 | convolution fusion | flops 1813118976 | bytes 6684672 | tf_op jit(solution)/shard_map/dot_general | solution.py:121
  156.1 3.2 %convolution_convert_fusion = bf16[2304,512]{1,0:T(8,128)(2,1)S(1)} fusion(bf16[2304,768]{0,1:T(8,128)(2,1)S(1)} %concatenate.54, bf16[512,768]{1,0:T(8,128)(2,1)} %collective-permute-done.10), kind=kOutput, calls=%fused_computation.16 | convolution fusion | flops 1813118976 | bytes 6684672 | tf_op jit(solution)/shard_map/dot_general | solution.py:121
  159.7 2.0 collective-permute-start.11
  161.6 11.5 %collective-permute-done.9 = bf16[1152,512]{1,0:T(8,128)(2,1)S(1)} collective-permute-done((bf16[1152,512]{1,0:T(8,128)(2,1)S(1)}, bf16[1152,512]{1,0:T(8,128)(2,1)S(1)}, u32[]{:S(2)}, u32[]{:S(2)}) %collective-permute-start.9) | collective-permute-done | bytes 1179680 | tf_op jit(solution)/shard_map/ppermute | solution.py:29
  173.5 3.6 %collective-permute-done.11 = bf16[1152,512]{1,0:T(8,128)(2,1)S(1)} collective-permute-done((bf16[1152,512]{1,0:T(8,128)(2,1)S(1)}, bf16[1152,512]{1,0:T(8,128)(2,1)S(1)}, u32[]{:S(2)}, u32[]{:S(2)}) %collective-permute-start.11) | collective-permute-done | bytes 1179680 | tf_op jit(solution)/shard_map/ppermute | solution.py:29
  178.0 9.5 %collective-permute-done.13 = bf16[576,512]{1,0:T(8,128)(2,1)S(1)} collective-permute-done((bf16[576,512]{1,0:T(8,128)(2,1)S(1)}, bf16[576,512]{1,0:T(8,128)(2,1)S(1)}, u32[]{:S(2)}, u32[]{:S(2)}) %collective-permute-start.13) | collective-permute-done | bytes 589856 | tf_op jit(solution)/shard_map/ppermute | solution.py:29
  187.9 3.0 %collective-permute-start.15 = (bf16[288,512]{1,0:T(8,128)(2,1)S(1)}, bf16[288,512]{1,0:T(8,128)(2,1)S(1)}, u32[]{:S(2)}, u32[]{:S(2)}) collective-permute-start(bf16[288,512]{1,0:T(8,128)(2,1)S(1)} %slice.130), channel_id=1, source_target_pairs={{0,12},{1,13},{2,14},{3,15},{4,8},{5,9},{6,10},{7,11},{8,4},{9,5},... | collective-permute-start | bytes 884744 | tf_op jit(solution)/shard_map/ppermute | solution.py:29
  191.9 4.0 %collective-permute-done.15 = bf16[288,512]{1,0:T(8,128)(2,1)S(1)} collective-permute-done((bf16[288,512]{1,0:T(8,128)(2,1)S(1)}, bf16[288,512]{1,0:T(8,128)(2,1)S(1)}, u32[]{:S(2)}, u32[]{:S(2)}) %collective-permute-start.15) | collective-permute-done | bytes 294944 | tf_op jit(solution)/shard_map/ppermute | solution.py:29
  196.0 4.2 %collective-permute-done.14 = bf16[288,512]{1,0:T(8,128)(2,1)S(1)} collective-permute-done((bf16[288,512]{1,0:T(8,128)(2,1)S(1)}, bf16[288,512]{1,0:T(8,128)(2,1)S(1)}, u32[]{:S(2)}, u32[]{:S(2)}) %collective-permute-start.14) | collective-permute-done | bytes 294944 | tf_op jit(solution)/shard_map/ppermute | solution.py:29
  200.3 1.4 collective-permute-start.16
  202.4 3.2 %collective-permute-done.16 = bf16[144,512]{1,0:T(8,128)(2,1)S(1)} collective-permute-done((bf16[144,512]{1,0:T(8,128)(2,1)S(1)}, bf16[144,512]{1,0:T(8,128)(2,1)S(1)}, u32[]{:S(2)}, u32[]{:S(2)}) %collective-permute-start.16) | collective-permute-done | bytes 147488 | tf_op jit(solution)/shard_map/ppermute | solution.py:29
  205.5 1.4 collective-permute-done.17
  (112 shorter events, 30.5 us)
Async XLA Ops:
  0.6 8.2 %copy-start = (bf16[2304,512]{1,0:T(8,128)(2,1)S(1)}, bf16[2304,512]{1,0:T(8,128)(2,1)}, u32[]{:S(2)}) copy-start(bf16[2304,512]{1,0:T(8,128)(2,1)} %param.8) | copy-start | bytes 7077892
  3.8 2.8 %copy-start.5 = (bf16[144,4,128]{2,1,0:T(4,128)(2,1)}, bf16[144,4,128]{2,1,0:T(4,128)(2,1)S(1)}, u32[]{:S(2)}) copy-start(bf16[144,4,128]{2,1,0:T(4,128)(2,1)S(1)} %get-tuple-element.26) | copy-start | bytes 442372
  3.8 3.4 %copy-start.7 = (bf16[144,4,128]{2,1,0:T(4,128)(2,1)}, bf16[144,4,128]{2,1,0:T(4,128)(2,1)S(1)}, u32[]{:S(2)}) copy-start(bf16[144,4,128]{2,1,0:T(4,128)(2,1)S(1)} %get-tuple-element.27) | copy-start | bytes 442372
  4.6 28.5 %collective-permute-start = (bf16[144,512]{1,0:T(8,128)(2,1)}, bf16[144,512]{1,0:T(8,128)(2,1)}, u32[]{:S(2)}, u32[]{:S(2)}) collective-permute-start(bf16[144,512]{1,0:T(8,128)(2,1)} %bitcast.82), channel_id=1, source_target_pairs={{0,1},{1,0},{2,3},{3,2},{4,5},{5,4},{6,7},{7,6},{8,9},{9,8},{10,11... | collective-permute-start | bytes 442376 | tf_op jit(solution)/shard_map/ppermute | solution.py:29
  7.2 25.8 %collective-permute-start.1 = (bf16[144,512]{1,0:T(8,128)(2,1)}, bf16[144,512]{1,0:T(8,128)(2,1)}, u32[]{:S(2)}, u32[]{:S(2)}) collective-permute-start(bf16[144,512]{1,0:T(8,128)(2,1)} %bitcast.83), channel_id=1, source_target_pairs={{0,4},{1,5},{2,6},{3,7},{4,0},{5,1},{6,2},{7,3},{8,12},{9,13},{10,... | collective-permute-start | bytes 442376 | tf_op jit(solution)/shard_map/ppermute | solution.py:29
  11.6 3.2 %copy-start.2 = (bf16[2304,768]{1,0:T(8,128)(2,1)S(1)}, bf16[2304,768]{1,0:T(8,128)(2,1)}, u32[]{:S(2)}) copy-start(bf16[2304,768]{1,0:T(8,128)(2,1)} %param.7) | copy-start | bytes 10616836
  34.1 8.0 %collective-permute-start.2 = (bf16[288,512]{1,0:T(8,128)(2,1)S(1)}, bf16[288,512]{1,0:T(8,128)(2,1)S(1)}, u32[]{:S(2)}, u32[]{:S(2)}) collective-permute-start(bf16[288,512]{1,0:T(8,128)(2,1)S(1)} %pad_maximum_fusion.5), channel_id=1, source_target_pairs={{0,3},{1,2},{2,1},{3,0},{4,7},{5,6},{6,5},{7,4},{8,11},{9,10},{10,... | collective-permute-start | bytes 884744 | tf_op jit(solution)/shard_map/ppermute | solution.py:29
  37.7 8.0 %collective-permute-start.3 = (bf16[288,512]{1,0:T(8,128)(2,1)S(1)}, bf16[288,512]{1,0:T(8,128)(2,1)S(1)}, u32[]{:S(2)}, u32[]{:S(2)}) collective-permute-start(bf16[288,512]{1,0:T(8,128)(2,1)S(1)} %pad_maximum_fusion.6), channel_id=1, source_target_pairs={{0,12},{1,13},{2,14},{3,15},{4,8},{5,9},{6,10},{7,11},{8,4},{9,5},... | collective-permute-start | bytes 884744 | tf_op jit(solution)/shard_map/ppermute | solution.py:29
  40.0 1.5 copy-start.8
  41.5 7.4 %copy-start.4 = (bf16[1152,800]{1,0:T(8,128)(2,1)S(1)}, bf16[1152,800]{1,0:T(8,128)(2,1)}, u32[]{:S(2)}) copy-start(bf16[1152,800]{1,0:T(8,128)(2,1)} %constant_dynamic-update-slice_fusion.28) | copy-start | bytes 5529604
  46.7 10.0 %collective-permute-start.4 = (bf16[576,512]{1,0:T(8,128)(2,1)S(1)}, bf16[576,512]{1,0:T(8,128)(2,1)S(1)}, u32[]{:S(2)}, u32[]{:S(2)}) collective-permute-start(bf16[576,512]{1,0:T(8,128)(2,1)S(1)} %pad_maximum_fusion.3), channel_id=1, source_target_pairs={{0,4},{1,5},{2,6},{3,7},{4,0},{5,1},{6,2},{7,3},{8,12},{9,13},{10,... | collective-permute-start | bytes 1769480 | tf_op jit(solution)/shard_map/ppermute | solution.py:29
  47.8 10.0 %collective-permute-start.5 = (bf16[576,512]{1,0:T(8,128)(2,1)S(1)}, bf16[576,512]{1,0:T(8,128)(2,1)S(1)}, u32[]{:S(2)}, u32[]{:S(2)}) collective-permute-start(bf16[576,512]{1,0:T(8,128)(2,1)S(1)} %pad_maximum_fusion.4), channel_id=1, source_target_pairs={{0,1},{1,0},{2,3},{3,2},{4,5},{5,4},{6,7},{7,6},{8,9},{9,8},{10,11... | collective-permute-start | bytes 1769480 | tf_op jit(solution)/shard_map/ppermute | solution.py:29
  48.9 1.7 copy-start.6
  57.9 17.5 %collective-permute-start.7 = (bf16[1152,512]{1,0:T(8,128)(2,1)S(1)}, bf16[1152,512]{1,0:T(8,128)(2,1)S(1)}, u32[]{:S(2)}, u32[]{:S(2)}) collective-permute-start(bf16[1152,512]{1,0:T(8,128)(2,1)S(1)} %constant_dynamic-update-slice_fusion.20), channel_id=1, source_target_pairs={{0,12},{1,13},{2,14},{3,15},{4,8},{5,9},{6,10},{7,11},{8,4},{9,5},... | collective-permute-start | bytes 3538952 | tf_op jit(solution)/shard_map/ppermute | solution.py:29
  66.8 17.5 %collective-permute-start.6 = (bf16[1152,512]{1,0:T(8,128)(2,1)S(1)}, bf16[1152,512]{1,0:T(8,128)(2,1)S(1)}, u32[]{:S(2)}, u32[]{:S(2)}) collective-permute-start(bf16[1152,512]{1,0:T(8,128)(2,1)S(1)} %constant_dynamic-update-slice_fusion), channel_id=1, source_target_pairs={{0,3},{1,2},{2,1},{3,0},{4,7},{5,6},{6,5},{7,4},{8,11},{9,10},{10,... | collective-permute-start | bytes 3538952 | tf_op jit(solution)/shard_map/ppermute | solution.py:29
  78.1 9.0 %collective-permute-start.8 = (bf16[512,832]{0,1:T(8,128)(2,1)S(1)}, bf16[512,832]{0,1:T(8,128)(2,1)S(1)}, u32[]{:S(2)}, u32[]{:S(2)}) collective-permute-start(bf16[512,832]{0,1:T(8,128)(2,1)S(1)} %pad_maximum_fusion.1), channel_id=1, source_target_pairs={{0,16},{16,0},{1,17},{17,1},{2,18},{18,2},{3,19},{19,3},{4,20},{20... | collective-permute-start | bytes 2555912 | tf_op jit(solution)/shard_map/ppermute | solution.py:33
  112.8 4.0 %copy-start.9 = (bf16[8,512]{1,0:T(8,128)(2,1)}, bf16[8,512]{1,0:T(8,128)(2,1)S(1)}, u32[]{:S(2)}) copy-start(bf16[8,512]{1,0:T(8,128)(2,1)S(1)} %reshape.98) | copy-start | bytes 24580
  113.0 4.2 %copy-start.10 = (bf16[8,1024,256]{2,1,0:T(8,128)(2,1)S(1)}, bf16[8,1024,256]{2,1,0:T(8,128)(2,1)}, u32[]{:S(2)}) copy-start(bf16[8,1024,256]{2,1,0:T(8,128)(2,1)} %param.11) | copy-start | bytes 12582916
  117.2 22.0 %copy-start.3 = (bf16[768,2304]{1,0:T(8,128)(2,1)S(1)}, bf16[768,2304]{1,0:T(8,128)(2,1)}, u32[]{:S(2)}) copy-start(bf16[768,2304]{1,0:T(8,128)(2,1)} %param.9) | copy-start | bytes 10616836
  139.3 16.8 %collective-permute-start.10 = (bf16[512,768]{1,0:T(8,128)(2,1)}, bf16[512,768]{1,0:T(8,128)(2,1)}, u32[]{:S(2)}, u32[]{:S(2)}) collective-permute-start(bf16[512,768]{1,0:T(8,128)(2,1)} %bitcast.26), channel_id=1, source_target_pairs={{0,16},{16,0},{1,17},{17,1},{2,18},{18,2},{3,19},{19,3},{4,20},{20... | collective-permute-start | bytes 2359304 | tf_op jit(solution)/shard_map/ppermute | solution.py:33
  155.7 17.5 %collective-permute-start.9 = (bf16[1152,512]{1,0:T(8,128)(2,1)S(1)}, bf16[1152,512]{1,0:T(8,128)(2,1)S(1)}, u32[]{:S(2)}, u32[]{:S(2)}) collective-permute-start(bf16[1152,512]{1,0:T(8,128)(2,1)S(1)} %slice.150), channel_id=1, source_target_pairs={{0,12},{1,13},{2,14},{3,15},{4,8},{5,9},{6,10},{7,11},{8,4},{9,5},... | collective-permute-start | bytes 3538952 | tf_op jit(solution)/shard_map/ppermute | solution.py:29
  159.7 17.5 %collective-permute-start.11 = (bf16[1152,512]{1,0:T(8,128)(2,1)S(1)}, bf16[1152,512]{1,0:T(8,128)(2,1)S(1)}, u32[]{:S(2)}, u32[]{:S(2)}) collective-permute-start(bf16[1152,512]{1,0:T(8,128)(2,1)S(1)} %bitcast.93), channel_id=1, source_target_pairs={{0,3},{1,2},{2,1},{3,0},{4,7},{5,6},{6,5},{7,4},{8,11},{9,10},{10,... | collective-permute-start | bytes 3538952 | tf_op jit(solution)/shard_map/ppermute | solution.py:29
  177.6 10.0 %collective-permute-start.13 = (bf16[576,512]{1,0:T(8,128)(2,1)S(1)}, bf16[576,512]{1,0:T(8,128)(2,1)S(1)}, u32[]{:S(2)}, u32[]{:S(2)}) collective-permute-start(bf16[576,512]{1,0:T(8,128)(2,1)S(1)} %slice.126), channel_id=1, source_target_pairs={{0,1},{1,0},{2,3},{3,2},{4,5},{5,4},{6,7},{7,6},{8,9},{9,8},{10,11... | collective-permute-start | bytes 1769480 | tf_op jit(solution)/shard_map/ppermute | solution.py:29
  177.8 10.0 %collective-permute-start.12 = (bf16[576,512]{1,0:T(8,128)(2,1)S(1)}, bf16[576,512]{1,0:T(8,128)(2,1)S(1)}, u32[]{:S(2)}, u32[]{:S(2)}) collective-permute-start(bf16[576,512]{1,0:T(8,128)(2,1)S(1)} %slice.124), channel_id=1, source_target_pairs={{0,4},{1,5},{2,6},{3,7},{4,0},{5,1},{6,2},{7,3},{8,12},{9,13},{10,... | collective-permute-start | bytes 1769480 | tf_op jit(solution)/shard_map/ppermute | solution.py:29
  187.9 8.0 %collective-permute-start.15 = (bf16[288,512]{1,0:T(8,128)(2,1)S(1)}, bf16[288,512]{1,0:T(8,128)(2,1)S(1)}, u32[]{:S(2)}, u32[]{:S(2)}) collective-permute-start(bf16[288,512]{1,0:T(8,128)(2,1)S(1)} %slice.130), channel_id=1, source_target_pairs={{0,12},{1,13},{2,14},{3,15},{4,8},{5,9},{6,10},{7,11},{8,4},{9,5},... | collective-permute-start | bytes 884744 | tf_op jit(solution)/shard_map/ppermute | solution.py:29
  190.9 9.3 %collective-permute-start.14 = (bf16[288,512]{1,0:T(8,128)(2,1)S(1)}, bf16[288,512]{1,0:T(8,128)(2,1)S(1)}, u32[]{:S(2)}, u32[]{:S(2)}) collective-permute-start(bf16[288,512]{1,0:T(8,128)(2,1)S(1)} %slice.128), channel_id=1, source_target_pairs={{0,3},{1,2},{2,1},{3,0},{4,7},{5,6},{6,5},{7,4},{8,11},{9,10},{10,... | collective-permute-start | bytes 884744 | tf_op jit(solution)/shard_map/ppermute | solution.py:29
  200.2 8.6 %copy-start.1 = (bf16[2304,512]{1,0:T(8,128)(2,1)S(1)}, bf16[2304,512]{1,0:T(8,128)(2,1)}, u32[]{:S(2)}) copy-start(bf16[2304,512]{1,0:T(8,128)(2,1)} %param.8) | copy-start | bytes 7077892
  200.3 5.2 %collective-permute-start.16 = (bf16[144,512]{1,0:T(8,128)(2,1)S(1)}, bf16[144,512]{1,0:T(8,128)(2,1)S(1)}, u32[]{:S(2)}, u32[]{:S(2)}) collective-permute-start(bf16[144,512]{1,0:T(8,128)(2,1)S(1)} %slice.132), channel_id=1, source_target_pairs={{0,1},{1,0},{2,3},{3,2},{4,5},{5,4},{6,7},{7,6},{8,9},{9,8},{10,11... | collective-permute-start | bytes 442376 | tf_op jit(solution)/shard_map/ppermute | solution.py:29
  201.8 5.2 %collective-permute-start.17 = (bf16[144,512]{1,0:T(8,128)(2,1)S(1)}, bf16[144,512]{1,0:T(8,128)(2,1)S(1)}, u32[]{:S(2)}, u32[]{:S(2)}) collective-permute-start(bf16[144,512]{1,0:T(8,128)(2,1)S(1)} %slice.134), channel_id=1, source_target_pairs={{0,4},{1,5},{2,6},{3,7},{4,0},{5,1},{6,2},{7,3},{8,12},{9,13},{10,... | collective-permute-start | bytes 442376 | tf_op jit(solution)/shard_map/ppermute | solution.py:29

commit v2 on v1

v2 whole, which is shorter than its diff:
```python
import jax
import jax.numpy as jnp
from jax import lax
from jax.experimental import pallas as pl
from jax.experimental.pallas import tpu as pltpu
from jax.sharding import Mesh
from jax.sharding import PartitionSpec as P

AXES = ("x", "c", "y", "z")
F32 = jnp.float32
BF16 = jnp.bfloat16


def linear(x, c, y, z):
    return ((x * 2 + c) * 4 + y) * 4 + z


def partner_pairs(axis, step):
    pairs = []
    for x in range(4):
        for c in range(2):
            for y in range(4):
                for z in range(4):
                    other = {"x": x, "y": y, "z": z}
                    other[axis] ^= (1, 3)[step ^ c]
                    pairs.append((linear(x, c, y, z), linear(other["x"], c, other["y"], other["z"])))
    return pairs


def exchange(v, axis, step):
    return lax.ppermute(v, AXES, partner_pairs(axis, step))


def core_swap(v):
    return lax.ppermute(v, "c", [(0, 1), (1, 0)])


def relative_blocks(first, second):
    c = lax.axis_index("c")
    m0 = jnp.where(c == 0, 1, 3)
    m1 = jnp.where(c == 0, 3, 1)
    blocks = []
    for p in range(16):
        at = {"y": lax.axis_index("y"), "z": lax.axis_index("z")}
        b = [(p >> i) & 1 for i in range(4)]
        at[first] = at[first] ^ (m0 * b[0]) ^ (m1 * b[1])
        at[second] = at[second] ^ (m0 * b[2]) ^ (m1 * b[3])
        blocks.append(at["y"] * 4 + at["z"])
    return blocks


def split_kernel(c_ref, t_ref, own_ref, oth_ref):
    c = c_ref[0]
    for x in range(4):
        to = pl.ds(x * 128, 128)
        own_ref[:, to] = t_ref[:, pl.ds(pl.multiple_of((2 * x + c) * 128, 128), 128)]
        oth_ref[:, to] = t_ref[:, pl.ds(pl.multiple_of((2 * x + 1 - c) * 128, 128), 128)]


def split_cores(c, t):
    rows = t.shape[0]
    return pl.pallas_call(
        split_kernel,
        in_specs=[pl.BlockSpec(memory_space=pltpu.SMEM), pl.BlockSpec(memory_space=pltpu.VMEM)],
        out_specs=[pl.BlockSpec(memory_space=pltpu.VMEM)] * 2,
        out_shape=[jax.ShapeDtypeStruct((rows, 512), t.dtype)] * 2,
    )(c.reshape(1), t)


def merge_kernel(c_ref, p_ref, rp_ref, q_ref, rq_ref, out_ref):
    c = c_ref[0]
    for x in range(4):
        at = pl.ds(x * 128, 128)
        p = p_ref[:, at].astype(F32) + rp_ref[:, at].astype(F32)
        q = q_ref[:, at].astype(F32) + rq_ref[:, at].astype(F32)
        out_ref[:, pl.ds(pl.multiple_of((2 * x + c) * 128, 128), 128)] = p.astype(BF16)
        out_ref[:, pl.ds(pl.multiple_of((2 * x + 1 - c) * 128, 128), 128)] = q.astype(BF16)


def merge_cores(c, *parts):
    return pl.pallas_call(
        merge_kernel,
        in_specs=[pl.BlockSpec(memory_space=pltpu.SMEM)] + [pl.BlockSpec(memory_space=pltpu.VMEM)] * 4,
        out_specs=pl.BlockSpec(memory_space=pltpu.VMEM),
        out_shape=jax.ShapeDtypeStruct((parts[0].shape[0], 1024), BF16),
    )(c.reshape(1), *parts)


def reorder(orders, sources, n):
    widths = [s.shape[1] for s in sources]
    n_src, n_out = len(sources), len(orders)
    shape = (16 * n, sum(widths))

    def kernel(order_ref, *refs):
        srcs, outs, sems = refs[:n_src], refs[n_src : n_src + n_out], refs[-1]
        copies = []
        for p in range(16):
            for o in range(n_out):
                start = pl.multiple_of(order_ref[o, p] * n, 16)
                at = 0
                for s in range(n_src):
                    copies.append(
                        pltpu.make_async_copy(
                            srcs[s].at[pl.ds(start, n), :],
                            outs[o].at[pl.ds(p * n, n), pl.ds(at, widths[s])],
                            sems.at[len(copies)],
                        )
                    )
                    at += widths[s]
        for copy in copies:
            copy.start()
        for copy in copies:
            copy.wait()

    total = 2 * n_out * shape[0] * shape[1] * 2
    return pl.pallas_call(
        kernel,
        in_specs=[pl.BlockSpec(memory_space=pltpu.SMEM)] + [pl.BlockSpec(memory_space=pl.ANY)] * n_src,
        out_specs=[pl.BlockSpec(memory_space=pl.ANY)] * n_out,
        out_shape=[jax.ShapeDtypeStruct(shape, sources[0].dtype)] * n_out,
        scratch_shapes=[pltpu.SemaphoreType.DMA((16 * n_out * n_src,))],
        cost_estimate=pl.CostEstimate(flops=0, bytes_accessed=total, transcendentals=0),
    )(jnp.stack([jnp.stack(o) for o in orders]), *sources)


def shards(tokens, w_query, w_keyvalue, w_output, key_cache, value_cache):
    c = lax.axis_index("c")
    column = lax.axis_index("y") * 4 + lax.axis_index("z")
    rows_dev, _, head_size = key_cache.shape
    feat = tokens.shape[1]
    kv_cols = w_keyvalue.shape[1] // 16
    q_cols = w_query.shape[1]

    own, oth = split_cores(c, tokens.T)
    a, b = oth, own
    for axis_a, axis_b, step in (("z", "y", 0), ("z", "y", 1)):
        ra, rb = exchange(a, axis_a, step), exchange(b, axis_b, step)
        ra, rb = lax.optimization_barrier((ra, rb))
        a, b = jnp.concatenate([a, ra], 0), jnp.concatenate([b, rb], 0)

    kv_own = lax.dynamic_slice_in_dim(w_keyvalue, column * kv_cols, kv_cols, 1)
    kv_own = jnp.pad(kv_own, ((0, 0), (0, 128 - kv_cols)))
    orders = [relative_blocks("z", "y"), relative_blocks("y", "z")]
    wa, wb = reorder(orders, [w_query, kv_own], feat)
    wp, wq = reorder(orders, [w_output.T], feat)
    a, b, wa, wb = lax.optimization_barrier((a, b, wa, wb))

    pa, pb = [a, exchange(a, "y", 0), exchange(a, "y", 1)], [b, exchange(b, "z", 0), exchange(b, "z", 1)]
    pa[1], pb[1], wp, wq = lax.optimization_barrier((pa[1], pb[1], wp, wq))
    pa.append(exchange(pa[1], "y", 1))
    pb.append(exchange(pb[1], "z", 1))
    quarter = 4 * feat

    def product(v, w, i):
        w = w[i * quarter : (i + 1) * quarter]
        return lax.dot_general(v, w, (((0,), (0,)), ((), ())), preferred_element_type=F32)

    part_oth = sum(product(pa[i], wa, i) for i in range(3))
    part_oth = (part_oth + product(pa[3], wa, 3)).astype(BF16)
    part_own = sum(product(pb[i], wb, i) for i in range(3))
    part_own = part_own + core_swap(part_oth).astype(F32)
    part = (part_own + product(pb[3], wb, 3)).astype(BF16)
    part = lax.all_to_all(part.reshape(64, rows_dev, -1), ("x", "y", "z"), 0, 0, tiled=True)
    whole = jnp.sum(part.astype(F32).reshape(4, 16, rows_dev, -1), axis=0).astype(BF16)
    queries = whole[:, :, :q_cols].transpose(1, 0, 2).reshape(rows_dev, -1, head_size)
    new_keyvalue = whole[:, :, q_cols : q_cols + kv_cols].transpose(1, 0, 2).reshape(rows_dev, -1)

    new_key = new_keyvalue[:, :head_size]
    new_value = new_keyvalue[:, head_size:]
    score_scale = 1.0 / head_size**0.5
    scores = jnp.einsum("bhe,bte->bht", queries, key_cache, preferred_element_type=F32) * score_scale
    score_new = jnp.einsum("bhe,be->bh", queries, new_key, preferred_element_type=F32) * score_scale
    highest = jnp.maximum(jnp.max(scores, axis=2), score_new)
    raised = jnp.exp(scores - highest[:, :, None])
    raised_new = jnp.exp(score_new - highest)
    denominator = jnp.sum(raised, axis=2) + raised_new
    probs = (raised / denominator[:, :, None]).astype(BF16)
    prob_new = (raised_new / denominator).astype(BF16)
    mixed = jnp.einsum("bht,bte->bhe", probs, value_cache, preferred_element_type=F32)
    mixed = mixed + prob_new.astype(F32)[:, :, None] * new_value.astype(F32)[:, None, :]
    attended = mixed.astype(BF16).reshape(rows_dev, 16, q_cols).transpose(1, 0, 2)

    spread = jnp.broadcast_to(attended[None], (4, 16, rows_dev, q_cols)).reshape(64, rows_dev, q_cols)
    mine = lax.all_to_all(spread, ("x", "y", "z"), 0, 0, tiled=True).reshape(512, q_cols)
    theirs = core_swap(mine)

    def outward(w, v, i):
        w = w[i * quarter : (i + 1) * quarter]
        return lax.dot_general(w, v, (((1,), (1,)), ((), ())), preferred_element_type=F32).astype(BF16)

    def add(*terms):
        return sum(t.astype(F32) for t in terms).astype(BF16)

    def scatter_start(w, v, axis):
        far = [exchange(outward(w, v, 3), axis, 1), exchange(outward(w, v, 2), axis, 1)]
        away = exchange(add(outward(w, v, 1), far[0]), axis, 0)
        return add(outward(w, v, 0), far[1], away)

    p, q = scatter_start(wp, mine, "y"), scatter_start(wq, theirs, "z")
    n = 2 * feat
    rp, rq = exchange(p[n:], "z", 1), exchange(q[n:], "y", 1)
    p, q = add(p[:n], rp), add(q[:n], rq)
    rp, rq = exchange(p[feat:], "z", 0), exchange(q[feat:], "y", 0)
    out = merge_cores(c, p[:feat], rp, q[:feat], rq)
    return out.T, new_keyvalue


def solution(mesh):
    fine = Mesh(mesh.devices.reshape(4, 2, 4, 4), AXES)
    gx, gy = ("x", "c"), ("y", "z")
    every = (*gx, *gy)
    return jax.shard_map(
        shards,
        mesh=fine,
        in_specs=(P(None, every), P(gx, gy), P(gx, None), P(gy, gx), P(every, None, None), P(every, None, None)),
        out_specs=(P(None, every), P(every, None)),
        check_vma=False,
    )
```

time: 211 us -> 626 us (2.97)
  Pallas kernels: 0 us -> 473 us
  other arithmetic: 36.6 us -> 5.04 us
  local copies, waits for them, and re-layouts: 29.3 us -> 9.75 us
  waiting for transfers between devices: 61.4 us -> 48.2 us
    pallas_call x0 -> x4, Pallas kernels: none -> 473 us  [the longest x2 469 us: reorder(): pl.pallas_call(kernel, in_specs=[pl.BlockSpec(memory_space=pltpu.SMEM)] +...]
    unnamed x20 -> x0, other arithmetic: 26.4 us -> none
    ppermute x16 -> x20, waiting for transfers between devices: 61.4 us -> 48.2 us  [exchange(): return lax.ppermute(v, AXES, partner_pairs(axis, step))]
    concatenate x4 -> x0, local copies, waits for them, and re-layouts: 7.94 us -> none  [the longest x1 7.27 us: take_rows(): jnp.concatenate([lax.dynamic_slice_in_dim(w, b * n, n, 0) for b in blocks...]
    dynamic_slice x2 -> x0, local copies, waits for them, and re-layouts: 7.65 us -> none  [the longest x1 5.81 us: take_rows(): lax.dynamic_slice_in_dim(w, b * n, n, 0)]
    ppermute x16 -> x20, starting transfers between devices: 21.5 us -> 24.2 us  [exchange(): return lax.ppermute(v, AXES, partner_pairs(axis, step))]
  transfers between devices with their start and end apart: 18 -> 22, of which waited for: 13 -> 12; matrix products, arithmetic and copies ran while one was open for 31% -> 4% of each run, Pallas kernels for 0% -> 75%
where the time goes in v2:
time: 626 us; the launch traced here: 625 us
  Pallas kernels  473 us (76%)
  waiting for transfers between devices  48.2 us (8%)
  blocking collectives  41.9 us (7%)
  starting transfers between devices  24.3 us (4%)
  matrix products  22.2 us (4%)
  local copies, waits for them, and re-layouts  9.75 us (2%)
    pallas_call x2, Pallas kernels, reorder(): pl.pallas_call(kernel, in_specs=[pl.BlockSpec(memory_space=pltpu.SMEM)] +...  469 us
    ppermute x20, waiting for transfers between devices, exchange(): return lax.ppermute(v, AXES, partner_pairs(axis, step))  48.2 us
    ppermute x20, starting transfers between devices, exchange(): return lax.ppermute(v, AXES, partner_pairs(axis, step))  24.2 us
    all_to_all x1, blocking collectives, shards(): lax.all_to_all(part.reshape(64, rows_dev, -1), ('x', 'y', 'z'), 0, 0, til...  22.3 us
    all_to_all x1, blocking collectives, shards(): lax.all_to_all(spread, ('x', 'y', 'z'), 0, 0, tiled=True)  19.6 us
  transfers between devices with their start and end apart: 22, of which 12 were waited for; matrix products, arithmetic and copies ran while one was open for 4% of the time, Pallas kernels for 75%

profile of v2, /device:TPU:0, one launch (start us, length us, event | category | flops | bytes accessed | tf_op | source)
XLA Modules:
  0.0 625.5 jit_solution(16251585848995608706)
XLA Ops:
  0.7 1.9 shard_map.77
  2.6 2.0 collective-permute-start
  4.6 1.6 collective-permute-start.1
  6.3 1.6 collective-permute-done
  7.9 2.0 collective-permute-done.1
  9.9 0.9 pad_maximum_fusion.2
  10.8 2.6 collective-permute-start.2
  13.4 0.9 pad_maximum_fusion.3
  14.4 3.1 collective-permute-start.3
  17.7 1.0 pad.4.refs_1_
  19.3 252.7 %shard_map.78 = (bf16[2304,896]{1,0:T(8,128)(2,1)}, bf16[2304,896]{1,0:T(8,128)(2,1)}) custom-call(s32[2,16]{1,0:T(2,128)} %pad_add_fusion.order_ref, bf16[2304,768]{1,0:T(8,128)(2,1)} %refs_0_.1, bf16[2304,128]{1,0:T(8,128)(2,1)} %pad.4.refs_1_), custom_call_target="tpu_custom_call" | custom-call | bytes 16515072 | tf_op jit(solution)/shard_map/pallas_call | solution.py:116
  272.0 1.9 pad_maximum_fusion
  274.0 1.0 collective-permute-start.5
  275.1 5.7 copy.13
  280.8 216.5 %shard_map.79 = (bf16[2304,768]{1,0:T(8,128)(2,1)}, bf16[2304,768]{1,0:T(8,128)(2,1)}) custom-call(s32[2,16]{1,0:T(2,128)} %pad_add_fusion.order_ref, bf16[2304,768]{1,0:T(8,128)(2,1)} %bitcast.60), custom_call_target="tpu_custom_call" | custom-call | bytes 14155776 | tf_op jit(solution)/shard_map/pallas_call | solution.py:116
  497.3 1.1 collective-permute-start.7
  499.1 2.5 fusion.31
  501.6 2.3 collective-permute-start.8
  503.9 2.2 fusion.29
  506.1 2.6 collective-permute-done.7
  508.7 1.0 fusion.27
  509.7 5.3 collective-permute-done.8
  515.0 1.0 add_convert_fusion.1
  516.1 1.0 fusion.37
  517.1 0.7 collective-permute-start.10
  517.8 1.0 fusion.35
  518.8 1.0 fusion.33
  519.8 8.5 %collective-permute-done.10 = bf16[576,512]{1,0:T(8,128)(2,1)S(1)} collective-permute-done((bf16[576,512]{1,0:T(8,128)(2,1)S(1)}, bf16[576,512]{1,0:T(8,128)(2,1)S(1)}, u32[]{:S(2)}, u32[]{:S(2)}) %collective-permute-start.10) | collective-permute-done | bytes 589856 | tf_op jit(solution)/shard_map/ppermute | solution.py:31
  528.3 1.2 fusion.20
  529.5 22.3 %all_to_all.10 = bf16[64,8,896]{2,1,0:T(8,128)(2,1)S(1)} all-to-all(bf16[64,8,896]{2,1,0:T(8,128)(2,1)S(1)} %fusion.20), channel_id=1, replica_groups=mesh['x'=4,'c'=2,'y'=4,'z'=4] {'x','y','z'}, dimensions={0} | all-to-all | bytes 1835008 | tf_op jit(solution)/shard_map/all_to_all | solution.py:163
  552.3 3.8 fusion.59
  556.7 0.8 fusion.15
  557.8 19.6 %all_to_all.11 = bf16[64,8,768]{2,1,0:T(8,128)(2,1)S(1)} all-to-all(bf16[64,8,768]{2,1,0:T(8,128)(2,1)S(1)} %bitcast.62), channel_id=1, replica_groups=mesh['x'=4,'c'=2,'y'=4,'z'=4] {'x','y','z'}, dimensions={0} | all-to-all | bytes 1572864 | tf_op jit(solution)/shard_map/all_to_all | solution.py:184
  577.4 2.0 convolution_convert_fusion.4
  580.5 1.8 collective-permute-start.18
  583.0 2.1 collective-permute-start.11
  585.0 5.5 collective-permute-done.12
  591.9 1.0 collective-permute-start.17
  594.1 6.0 collective-permute-done.11
  600.1 1.4 collective-permute-done.13
  601.5 0.7 fusion.14
  602.2 1.0 collective-permute-start.14
  603.2 5.0 collective-permute-done.17
  608.2 0.7 fusion.7
  609.0 1.9 collective-permute-start.20
  612.4 4.6 collective-permute-done.20
  617.8 5.1 collective-permute-done.21.rq_ref
  623.6 1.9 shard_map.80
  (74 shorter events, 10.3 us)
Async XLA Ops:
  0.6 16.8 %copy-start = (bf16[2304,512]{1,0:T(8,128)(2,1)S(1)}, bf16[2304,512]{1,0:T(8,128)(2,1)}, u32[]{:S(2)}) copy-start(bf16[2304,512]{1,0:T(8,128)(2,1)} %param.8) | copy-start | bytes 7077892
  2.6 5.4 collective-permute-start
  4.6 5.4 collective-permute-start.1
  10.8 261.1 %collective-permute-start.2 = (bf16[288,512]{1,0:T(8,128)(2,1)S(1)}, bf16[288,512]{1,0:T(8,128)(2,1)S(1)}, u32[]{:S(2)}, u32[]{:S(2)}) collective-permute-start(bf16[288,512]{1,0:T(8,128)(2,1)S(1)} %pad_maximum_fusion.2), channel_id=1, source_target_pairs={{0,3},{1,2},{2,1},{3,0},{4,7},{5,6},{6,5},{7,4},{8,11},{9,10},{10,... | collective-permute-start | bytes 884744 | tf_op jit(solution)/shard_map/ppermute | solution.py:31
  14.4 257.6 %collective-permute-start.3 = (bf16[288,512]{1,0:T(8,128)(2,1)S(1)}, bf16[288,512]{1,0:T(8,128)(2,1)}, u32[]{:S(2)}, u32[]{:S(2)}) collective-permute-start(bf16[288,512]{1,0:T(8,128)(2,1)S(1)} %pad_maximum_fusion.3), channel_id=1, source_target_pairs={{0,12},{1,13},{2,14},{3,15},{4,8},{5,9},{6,10},{7,11},{8,4},{9,5},... | collective-permute-start | bytes 884744 | tf_op jit(solution)/shard_map/ppermute | solution.py:31
  19.3 252.7 %copy-start.2 = (bf16[144,512]{1,0:T(8,128)(2,1)S(1)}, bf16[144,512]{1,0:T(8,128)(2,1)}, u32[]{:S(2)}) copy-start(bf16[144,512]{1,0:T(8,128)(2,1)} %get-tuple-element.21) | copy-start | bytes 442372
  19.3 252.7 %copy-start.3 = (bf16[144,512]{1,0:T(8,128)(2,1)S(1)}, bf16[144,512]{1,0:T(8,128)(2,1)}, u32[]{:S(2)}) copy-start(bf16[144,512]{1,0:T(8,128)(2,1)} %get-tuple-element.20) | copy-start | bytes 442372
  273.9 227.7 %collective-permute-start.4 = (bf16[576,512]{1,0:T(8,128)(2,1)}, bf16[576,512]{1,0:T(8,128)(2,1)S(1)}, u32[]{:S(2)}, u32[]{:S(2)}) collective-permute-start(bf16[576,512]{1,0:T(8,128)(2,1)} %get-tuple-element.28), channel_id=1, source_target_pairs={{0,4},{1,5},{2,6},{3,7},{4,0},{5,1},{6,2},{7,3},{8,12},{9,13},{10,... | collective-permute-start | bytes 1769480 | tf_op jit(solution)/shard_map/ppermute | solution.py:31
  274.0 227.6 %collective-permute-start.5 = (bf16[576,512]{1,0:T(8,128)(2,1)S(1)}, bf16[576,512]{1,0:T(8,128)(2,1)S(1)}, u32[]{:S(2)}, u32[]{:S(2)}) collective-permute-start(bf16[576,512]{1,0:T(8,128)(2,1)S(1)} %get-tuple-element.29), channel_id=1, source_target_pairs={{0,1},{1,0},{2,3},{3,2},{4,5},{5,4},{6,7},{7,6},{8,9},{9,8},{10,11... | collective-permute-start | bytes 1769480 | tf_op jit(solution)/shard_map/ppermute | solution.py:31
  497.3 11.4 %collective-permute-start.7 = (bf16[576,512]{1,0:T(8,128)(2,1)}, bf16[576,512]{1,0:T(8,128)(2,1)S(1)}, u32[]{:S(2)}, u32[]{:S(2)}) collective-permute-start(bf16[576,512]{1,0:T(8,128)(2,1)} %get-tuple-element.28), channel_id=1, source_target_pairs={{0,12},{1,13},{2,14},{3,15},{4,8},{5,9},{6,10},{7,11},{8,4},{9,5},... | collective-permute-start | bytes 1769480 | tf_op jit(solution)/shard_map/ppermute | solution.py:31
  498.4 20.4 %collective-permute-start.6 = (bf16[576,512]{1,0:T(8,128)(2,1)S(1)}, bf16[576,512]{1,0:T(8,128)(2,1)S(1)}, u32[]{:S(2)}, u32[]{:S(2)}) collective-permute-start(bf16[576,512]{1,0:T(8,128)(2,1)S(1)} %get-tuple-element.29), channel_id=1, source_target_pairs={{0,3},{1,2},{2,1},{3,0},{4,7},{5,6},{6,5},{7,4},{8,11},{9,10},{10,... | collective-permute-start | bytes 1769480 | tf_op jit(solution)/shard_map/ppermute | solution.py:31
  499.1 9.6 %copy-start.5 = (bf16[2304,896]{1,0:T(8,128)(2,1)S(1)}, bf16[2304,896]{1,0:T(8,128)(2,1)}, u32[]{:S(2)}) copy-start(bf16[2304,896]{1,0:T(8,128)(2,1)} %get-tuple-element.35) | copy-start | bytes 12386308
  501.6 13.4 %collective-permute-start.8 = (bf16[576,512]{1,0:T(8,128)(2,1)S(1)}, bf16[576,512]{1,0:T(8,128)(2,1)S(1)}, u32[]{:S(2)}, u32[]{:S(2)}) collective-permute-start(bf16[576,512]{1,0:T(8,128)(2,1)S(1)} %collective-permute-done.4), channel_id=1, source_target_pairs={{0,12},{1,13},{2,14},{3,15},{4,8},{5,9},{6,10},{7,11},{8,4},{9,5},... | collective-permute-start | bytes 1769480 | tf_op jit(solution)/shard_map/ppermute | solution.py:31
  509.7 6.5 %copy-start.4 = (bf16[2304,896]{1,0:T(8,128)(2,1)S(1)}, bf16[2304,896]{1,0:T(8,128)(2,1)}, u32[]{:S(2)}) copy-start(bf16[2304,896]{1,0:T(8,128)(2,1)} %get-tuple-element.33) | copy-start | bytes 12386308
  516.0 12.3 %collective-permute-start.9 = (bf16[512,896]{1,0:T(8,128)(2,1)S(1)}, bf16[512,896]{1,0:T(8,128)(2,1)S(1)}, u32[]{:S(2)}, u32[]{:S(2)}) collective-permute-start(bf16[512,896]{1,0:T(8,128)(2,1)S(1)} %add_convert_fusion.1), channel_id=1, source_target_pairs={{0,16},{16,0},{1,17},{17,1},{2,18},{18,2},{3,19},{19,3},{4,20},{20... | collective-permute-start | bytes 2752520 | tf_op jit(solution)/shard_map/ppermute | solution.py:35
  517.1 11.2 %collective-permute-start.10 = (bf16[576,512]{1,0:T(8,128)(2,1)S(1)}, bf16[576,512]{1,0:T(8,128)(2,1)S(1)}, u32[]{:S(2)}, u32[]{:S(2)}) collective-permute-start(bf16[576,512]{1,0:T(8,128)(2,1)S(1)} %collective-permute-done.5), channel_id=1, source_target_pairs={{0,3},{1,2},{2,1},{3,0},{4,7},{5,6},{6,5},{7,4},{8,11},{9,10},{10,... | collective-permute-start | bytes 1769480 | tf_op jit(solution)/shard_map/ppermute | solution.py:31
  552.3 3.8 copy-start.8
  552.3 4.4 copy-start.9
  557.8 22.1 %copy-start.10 = (bf16[2304,768]{1,0:T(8,128)(2,1)S(1)}, bf16[2304,768]{1,0:T(8,128)(2,1)}, u32[]{:S(2)}) copy-start(bf16[2304,768]{1,0:T(8,128)(2,1)} %get-tuple-element.37) | copy-start | bytes 10616836
  577.4 2.5 collective-permute-start.16
  577.4 4.9 copy-start.11
  579.3 11.2 %collective-permute-start.12 = (bf16[576,512]{1,0:T(8,128)(2,1)S(1)}, bf16[576,512]{1,0:T(8,128)(2,1)S(1)}, u32[]{:S(2)}, u32[]{:S(2)}) collective-permute-start(bf16[576,512]{1,0:T(8,128)(2,1)S(1)} %convolution_convert_fusion.4), channel_id=1, source_target_pairs={{0,12},{1,13},{2,14},{3,15},{4,8},{5,9},{6,10},{7,11},{8,4},{9,5},... | collective-permute-start | bytes 1769480 | tf_op jit(solution)/shard_map/ppermute | solution.py:31
  580.5 12.4 %collective-permute-start.18 = (bf16[576,512]{1,0:T(8,128)(2,1)S(1)}, bf16[576,512]{1,0:T(8,128)(2,1)S(1)}, u32[]{:S(2)}, u32[]{:S(2)}) collective-permute-start(bf16[576,512]{1,0:T(8,128)(2,1)S(1)} %convolution_convert_fusion), channel_id=1, source_target_pairs={{0,3},{1,2},{2,1},{3,0},{4,7},{5,6},{6,5},{7,4},{8,11},{9,10},{10,... | collective-permute-start | bytes 1769480 | tf_op jit(solution)/shard_map/ppermute | solution.py:31
  583.0 17.1 %collective-permute-start.11 = (bf16[576,512]{1,0:T(8,128)(2,1)S(1)}, bf16[576,512]{1,0:T(8,128)(2,1)S(1)}, u32[]{:S(2)}, u32[]{:S(2)}) collective-permute-start(bf16[576,512]{1,0:T(8,128)(2,1)S(1)} %convolution_convert_fusion.6), channel_id=1, source_target_pairs={{0,12},{1,13},{2,14},{3,15},{4,8},{5,9},{6,10},{7,11},{8,4},{9,5},... | collective-permute-start | bytes 1769480 | tf_op jit(solution)/shard_map/ppermute | solution.py:31
  591.2 10.3 %collective-permute-start.13 = (bf16[576,512]{1,0:T(8,128)(2,1)S(1)}, bf16[576,512]{1,0:T(8,128)(2,1)S(1)}, u32[]{:S(2)}, u32[]{:S(2)}) collective-permute-start(bf16[576,512]{1,0:T(8,128)(2,1)S(1)} %fusion.10), channel_id=1, source_target_pairs={{0,4},{1,5},{2,6},{3,7},{4,0},{5,1},{6,2},{7,3},{8,12},{9,13},{10,... | collective-permute-start | bytes 1769480 | tf_op jit(solution)/shard_map/ppermute | solution.py:31
  591.9 16.3 %collective-permute-start.17 = (bf16[576,512]{1,0:T(8,128)(2,1)S(1)}, bf16[576,512]{1,0:T(8,128)(2,1)S(1)}, u32[]{:S(2)}, u32[]{:S(2)}) collective-permute-start(bf16[576,512]{1,0:T(8,128)(2,1)S(1)} %convolution_convert_fusion.2), channel_id=1, source_target_pairs={{0,3},{1,2},{2,1},{3,0},{4,7},{5,6},{6,5},{7,4},{8,11},{9,10},{10,... | collective-permute-start | bytes 1769480 | tf_op jit(solution)/shard_map/ppermute | solution.py:31
  593.6 14.7 %collective-permute-start.19 = (bf16[576,512]{1,0:T(8,128)(2,1)S(1)}, bf16[576,512]{1,0:T(8,128)(2,1)S(1)}, u32[]{:S(2)}, u32[]{:S(2)}) collective-permute-start(bf16[576,512]{1,0:T(8,128)(2,1)S(1)} %fusion.3), channel_id=1, source_target_pairs={{0,1},{1,0},{2,3},{3,2},{4,5},{5,4},{6,7},{7,6},{8,9},{9,8},{10,11... | collective-permute-start | bytes 1769480 | tf_op jit(solution)/shard_map/ppermute | solution.py:31
  602.2 9.2 %collective-permute-start.14 = (bf16[288,512]{1,0:T(8,128)(2,1)S(1)}, bf16[288,512]{1,0:T(8,128)(2,1)S(1)}, u32[]{:S(2)}, u32[]{:S(2)}) collective-permute-start(bf16[288,512]{1,0:T(8,128)(2,1)S(1)} %slice.117), channel_id=1, source_target_pairs={{0,3},{1,2},{2,1},{3,0},{4,7},{5,6},{6,5},{7,4},{8,11},{9,10},{10,... | collective-permute-start | bytes 884744 | tf_op jit(solution)/shard_map/ppermute | solution.py:31
  608.9 16.6 %copy-start.1 = (bf16[2304,512]{1,0:T(8,128)(2,1)S(1)}, bf16[2304,512]{1,0:T(8,128)(2,1)}, u32[]{:S(2)}) copy-start(bf16[2304,512]{1,0:T(8,128)(2,1)} %param.8) | copy-start | bytes 7077892
  609.0 8.0 %collective-permute-start.20 = (bf16[288,512]{1,0:T(8,128)(2,1)S(1)}, bf16[288,512]{1,0:T(8,128)(2,1)S(1)}, u32[]{:S(2)}, u32[]{:S(2)}) collective-permute-start(bf16[288,512]{1,0:T(8,128)(2,1)S(1)} %slice.121), channel_id=1, source_target_pairs={{0,12},{1,13},{2,14},{3,15},{4,8},{5,9},{6,10},{7,11},{8,4},{9,5},... | collective-permute-start | bytes 884744 | tf_op jit(solution)/shard_map/ppermute | solution.py:31
  612.1 5.6 collective-permute-start.15
  617.8 5.1 collective-permute-start.21
  617.8 5.1 copy-start.6
  622.9 0.7 copy-start.7

commit v3 on v1

v3 whole, which is shorter than its diff:
```python
import jax
import jax.numpy as jnp
from jax import lax
from jax.experimental import pallas as pl
from jax.experimental.pallas import tpu as pltpu
from jax.sharding import Mesh
from jax.sharding import PartitionSpec as P

AXES = ("x", "c", "y", "z")
F32 = jnp.float32
BF16 = jnp.bfloat16


def linear(x, c, y, z):
    return ((x * 2 + c) * 4 + y) * 4 + z


def partner_pairs(phase, mask):
    pairs = []
    for x in range(4):
        for c in range(2):
            for y in range(4):
                for z in range(4):
                    other = (y ^ mask, z) if phase != c else (y, z ^ mask)
                    pairs.append((linear(x, c, y, z), linear(x, c, *other)))
    return pairs


def exchange(v, phase, mask):
    return lax.ppermute(v, AXES, partner_pairs(phase, mask))


def core_swap(v):
    return lax.ppermute(v, "c", [(0, 1), (1, 0)])


MASKS = (1, 3, 2)
SMEM = pl.BlockSpec(memory_space=pltpu.SMEM)
VMEM = pl.BlockSpec(memory_space=pltpu.VMEM)


def block(i, n):
    return pl.ds(pl.multiple_of(i * n, 16), n)


def lanes(i):
    return pl.ds(pl.multiple_of(i * 128, 128), 128)


def split_kernel(c_ref, t_ref, out_ref):
    c = c_ref[0]
    for x in range(4):
        out_ref[:, x * 128 : (x + 1) * 128] = t_ref[:, lanes(2 * x + 1 - c)]
        out_ref[:, (x + 4) * 128 : (x + 5) * 128] = t_ref[:, lanes(2 * x + c)]


def split_cores(c, t):
    return pl.pallas_call(
        split_kernel, in_specs=[SMEM, VMEM], out_specs=VMEM, out_shape=jax.ShapeDtypeStruct(t.shape, t.dtype)
    )(c.reshape(1), t)


def merge_kernel(c_ref, *refs):
    c, terms, out_ref = c_ref[0], refs[:-1], refs[-1]
    for x in range(8):
        total = sum(t[:, x * 128 : (x + 1) * 128].astype(F32) for t in terms)
        out_ref[:, lanes(2 * (x % 4) + (c if x >= 4 else 1 - c))] = total.astype(BF16)


def merge_cores(c, *terms):
    return pl.pallas_call(
        merge_kernel,
        in_specs=[SMEM] + [VMEM] * len(terms),
        out_specs=VMEM,
        out_shape=jax.ShapeDtypeStruct(terms[0].shape, BF16),
    )(c.reshape(1), *terms)


def assemble_kernel(at_ref, *refs):
    n = refs[0].shape[0]
    for p in range(4):
        refs[4][block(at_ref[p], n), :] = refs[p][...]


def assemble(places, *pieces):
    n, m = pieces[0].shape
    return pl.pallas_call(
        assemble_kernel,
        in_specs=[SMEM] + [VMEM] * 4,
        out_specs=VMEM,
        out_shape=jax.ShapeDtypeStruct((4 * n, m), BF16),
    )(jnp.stack(places), *pieces)


def part_kernel(at_ref, *refs):
    terms, outs = refs[:8], refs[8:]
    n, m = terms[0].shape[0] // 4, terms[0].shape[1]
    for p in range(4):
        at = block(at_ref[p], n)
        for half in range(2):
            total = sum(t[at, :].astype(F32) for t in terms[4 * half : 4 * half + 4])
            outs[p][:, half * m : (half + 1) * m] = total.astype(BF16)


def add_and_part(places, *terms):
    n, m = terms[0].shape
    return pl.pallas_call(
        part_kernel,
        in_specs=[SMEM] + [VMEM] * 8,
        out_specs=[VMEM] * 4,
        out_shape=[jax.ShapeDtypeStruct((n // 4, 2 * m), BF16)] * 4,
        compiler_params=pltpu.CompilerParams(vmem_limit_bytes=32 * 1024 * 1024),
    )(jnp.stack(places), *terms)


def shards(tokens, w_query, w_keyvalue, w_output, key_cache, value_cache):
    c = lax.axis_index("c")
    column = lax.axis_index("y") * 4 + lax.axis_index("z")
    rows_dev, _, head_size = key_cache.shape
    feat = tokens.shape[1]
    kv_cols = w_keyvalue.shape[1] // 16
    q_cols = w_query.shape[1]

    y, z = lax.axis_index("y"), lax.axis_index("z")
    first, second = jnp.where(c == 0, z, y), jnp.where(c == 0, y, z)
    firsts, seconds = [first ^ m for m in (0, *MASKS)], [second ^ m for m in (0, *MASKS)]

    t = split_cores(c, tokens.T)
    t = assemble(firsts, t, *[exchange(t, 0, m) for m in MASKS])
    t1, t3 = exchange(t, 1, 1), exchange(t, 1, 3)
    half = t.shape[0] // 2
    low, high = exchange(t3[:half], 1, 1), exchange(t1[half:], 1, 3)

    def by_blocks(w):
        w = w.reshape(4, 4, feat, -1)
        return jnp.where(c == 0, w, w.swapaxes(0, 1)).reshape(16 * feat, -1)

    kv_own = lax.dynamic_slice_in_dim(w_keyvalue, column * kv_cols, kv_cols, 1)
    w_all = by_blocks(jnp.concatenate([w_query, jnp.pad(kv_own, ((0, 0), (0, 128 - kv_cols)))], 1))
    w_out = by_blocks(lax.optimization_barrier(w_output.T))

    def product(v, i, skip=0):
        w = lax.dynamic_slice_in_dim(w_all, i * 4 * feat + skip, v.shape[0], 0)
        return lax.dot_general(v, w, (((0,), (0,)), ((), ())), preferred_element_type=F32)

    part = product(t, seconds[0]) + product(t1, seconds[1]) + product(t3, seconds[2])
    part = part + product(low, seconds[3]) + product(high, seconds[3], half)
    part = core_swap(part[:512].astype(BF16)).astype(F32) + part[512:]
    part = part.astype(BF16)
    part = lax.all_to_all(part.reshape(64, rows_dev, -1), ("x", "y", "z"), 0, 0, tiled=True)
    whole = jnp.sum(part.astype(F32).reshape(4, 16, rows_dev, -1), axis=0).astype(BF16)
    queries = whole[:, :, :q_cols].transpose(1, 0, 2).reshape(rows_dev, -1, head_size)
    new_keyvalue = whole[:, :, q_cols : q_cols + kv_cols].transpose(1, 0, 2).reshape(rows_dev, -1)

    new_key = new_keyvalue[:, :head_size]
    new_value = new_keyvalue[:, head_size:]
    score_scale = 1.0 / head_size**0.5
    scores = jnp.einsum("bhe,bte->bht", queries, key_cache, preferred_element_type=F32) * score_scale
    score_new = jnp.einsum("bhe,be->bh", queries, new_key, preferred_element_type=F32) * score_scale
    highest = jnp.maximum(jnp.max(scores, axis=2), score_new)
    raised = jnp.exp(scores - highest[:, :, None])
    raised_new = jnp.exp(score_new - highest)
    denominator = jnp.sum(raised, axis=2) + raised_new
    probs = (raised / denominator[:, :, None]).astype(BF16)
    prob_new = (raised_new / denominator).astype(BF16)
    mixed = jnp.einsum("bht,bte->bhe", probs, value_cache, preferred_element_type=F32)
    mixed = mixed + prob_new.astype(F32)[:, :, None] * new_value.astype(F32)[:, None, :]
    attended = mixed.astype(BF16).reshape(rows_dev, 16, q_cols).transpose(1, 0, 2)

    spread = jnp.broadcast_to(attended[None], (4, 16, rows_dev, q_cols)).reshape(64, rows_dev, q_cols)
    mine = lax.all_to_all(spread, ("x", "y", "z"), 0, 0, tiled=True).reshape(512, q_cols)
    theirs = core_swap(mine)

    def outward(i, v):
        w = lax.dynamic_slice_in_dim(w_out, i * 4 * feat, 4 * feat, 0)
        return lax.dot_general(w, v, (((1,), (1,)), ((), ())), preferred_element_type=F32).astype(BF16)

    terms = []
    for v in (theirs, mine):
        terms.append(outward(seconds[0], v))
        terms += [exchange(outward(seconds[i + 1], v), 1, MASKS[i]) for i in range(3)]
    keep, *away = add_and_part(firsts, *terms)
    out = merge_cores(c, keep, *[exchange(v, 0, m) for v, m in zip(away, MASKS)])
    return out.T, new_keyvalue


def solution(mesh):
    fine = Mesh(mesh.devices.reshape(4, 2, 4, 4), AXES)
    gx, gy = ("x", "c"), ("y", "z")
    every = (*gx, *gy)
    return jax.shard_map(
        shards,
        mesh=fine,
        in_specs=(P(None, every), P(gx, gy), P(gx, None), P(gy, gx), P(every, None, None), P(every, None, None)),
        out_specs=(P(None, every), P(every, None)),
        check_vma=False,
    )
```

time: 211 us -> 156 us (0.74)
  other arithmetic: 36.6 us -> 4.26 us
  local copies, waits for them, and re-layouts: 29.3 us -> 8.73 us
  blocking collectives: 38.4 us -> 26.3 us
  Pallas kernels: 0 us -> 7.54 us
  starting transfers between devices: 21.7 us -> 27.7 us
  waiting for transfers between devices: 61.4 us -> 56.8 us
  matrix products: 20.1 us -> 22.8 us
    unnamed x20 -> x0, other arithmetic: 26.4 us -> none
    all_to_all x1 -> x0, blocking collectives: 17.7 us -> none  [shards(): lax.all_to_all(spread, ('x', 'y', 'z'), 0, 0, tiled=True)]
    ppermute x16, waiting for transfers between devices: 61.4 us -> 44.7 us  [exchange(): return lax.ppermute(v, AXES, partner_pairs(phase, mask))]
    all_to_all x0 -> x1, waiting for transfers between devices: none -> 9.66 us  [shards(): lax.all_to_all(spread, ('x', 'y', 'z'), 0, 0, tiled=True)]
    concatenate x4 -> x0, local copies, waits for them, and re-layouts: 7.94 us -> none  [the longest x1 7.27 us: take_rows(): jnp.concatenate([lax.dynamic_slice_in_dim(w, b * n, n, 0) for b in blocks...]
    dynamic_slice x2 -> x0, local copies, waits for them, and re-layouts: 7.65 us -> none  [the longest x1 5.81 us: take_rows(): lax.dynamic_slice_in_dim(w, b * n, n, 0)]
    pallas_call x0 -> x4, Pallas kernels: none -> 7.54 us  [the longest x1 2.37 us: assemble(): pl.pallas_call(assemble_kernel, in_specs=[SMEM] + [VMEM] * 4, out_specs=V...]
    all_to_all x1, blocking collectives: 20.6 us -> 26.3 us  [shards(): lax.all_to_all(part.reshape(64, rows_dev, -1), ('x', 'y', 'z'), 0, 0, til...]
  transfers between devices with their start and end apart: 18 -> 19, of which waited for: 13 -> 13; matrix products, arithmetic and copies ran while one was open for 31% -> 16% of each run, Pallas kernels for 0% -> 0%
where the time goes in v3:
time: 156 us; the launch traced here: 155 us
  waiting for transfers between devices  56.8 us (36%)
  starting transfers between devices  27.7 us (18%)
  blocking collectives  26.3 us (17%)
  matrix products  22.8 us (15%)
  local copies, waits for them, and re-layouts  8.73 us (6%)
  Pallas kernels  7.54 us (5%)
  other arithmetic  4.26 us (3%)
    ppermute x16, waiting for transfers between devices, exchange(): return lax.ppermute(v, AXES, partner_pairs(phase, mask))  44.7 us
    all_to_all x1, blocking collectives, shards(): lax.all_to_all(part.reshape(64, rows_dev, -1), ('x', 'y', 'z'), 0, 0, til...  26.3 us
    ppermute x16, starting transfers between devices, exchange(): return lax.ppermute(v, AXES, partner_pairs(phase, mask))  22.2 us
    dot_general x8, matrix products, outward(): lax.dot_general(w, v, (((1,), (1,)), ((), ())), preferred_element_type=F32)  9.76 us
    all_to_all x1, waiting for transfers between devices, shards(): lax.all_to_all(spread, ('x', 'y', 'z'), 0, 0, tiled=True)  9.66 us
    dot_general x5, matrix products, product(): lax.dot_general(v, w, (((0,), (0,)), ((), ())), preferred_element_type=F32)  8.28 us
    unnamed x25, local copies, waits for them, and re-layouts  6.92 us
    all_to_all x1, starting transfers between devices, shards(): lax.all_to_all(spread, ('x', 'y', 'z'), 0, 0, tiled=True)  5.47 us
  transfers between devices with their start and end apart: 19, of which 13 were waited for; matrix products, arithmetic and copies ran while one was open for 16% of the time, Pallas kernels for 0%

profile of v3, /device:TPU:0, one launch (start us, length us, event | category | flops | bytes accessed | tf_op | source)
XLA Modules:
  0.0 155.2 jit_solution(6496982106347993529)
XLA Ops:
  0.7 1.9 %shard_map.77.refs_0_ = bf16[144,1024]{1,0:T(8,128)(2,1)} custom-call(s32[1]{0:T(128)} %bitcast.c_ref, bf16[144,1024]{1,0:T(8,128)(2,1)} %bitcast.68), custom_call_target="tpu_custom_call" | custom-call | tf_op jit(solution)/shard_map/pallas_call | solution.py:58
  2.6 4.0 %collective-permute-start.2 = (bf16[144,1024]{1,0:T(8,128)(2,1)}, bf16[144,1024]{1,0:T(8,128)(2,1)S(1)}, u32[]{:S(2)}, u32[]{:S(2)}) collective-permute-start(bf16[144,1024]{1,0:T(8,128)(2,1)} %shard_map.77.refs_0_), channel_id=1, source_target_pairs={{0,2},{1,3},{2,0},{3,1},{4,6},{5,7},{6,4},{7,5},{8,10},{9,11},{10,... | collective-permute-start | bytes 884744 | tf_op jit(solution)/shard_map/ppermute | solution.py:30
  6.5 0.7 collective-permute-start.1
  8.4 3.0 %collective-permute-done.2.refs_3_ = bf16[144,1024]{1,0:T(8,128)(2,1)S(1)} collective-permute-done((bf16[144,1024]{1,0:T(8,128)(2,1)}, bf16[144,1024]{1,0:T(8,128)(2,1)S(1)}, u32[]{:S(2)}, u32[]{:S(2)}) %collective-permute-start.2) | collective-permute-done | bytes 294944 | tf_op jit(solution)/shard_map/ppermute | solution.py:30
  11.4 3.3 %collective-permute-done.1.refs_2_ = bf16[144,1024]{1,0:T(8,128)(2,1)S(1)} collective-permute-done((bf16[144,1024]{1,0:T(8,128)(2,1)}, bf16[144,1024]{1,0:T(8,128)(2,1)S(1)}, u32[]{:S(2)}, u32[]{:S(2)}) %collective-permute-start.1) | collective-permute-done | bytes 294944 | tf_op jit(solution)/shard_map/ppermute | solution.py:30
  14.7 1.1 collective-permute-done.refs_1_
  15.8 2.4 %shard_map.78 = bf16[576,1024]{1,0:T(8,128)(2,1)} custom-call(s32[4]{0:T(128)} %pad_add_fusion.at_ref, bf16[144,1024]{1,0:T(8,128)(2,1)} %shard_map.77.refs_0_, bf16[144,1024]{1,0:T(8,128)(2,1)} %collective-permute-done.refs_1_, bf16[144,1024]{1,0:T(8,128)(2,1)} %copy-done.6, bf16[144,1024]{1,0:T(8,128)(2,1)} %copy-done.5), custom_call_target="tpu_custom_call" | custom-call | tf_op jit(solution)/shard_map/pallas_call | solution.py:87
  18.1 3.0 %collective-permute-start.4 = (bf16[576,1024]{1,0:T(8,128)(2,1)}, bf16[576,1024]{1,0:T(8,128)(2,1)S(1)}, u32[]{:S(2)}, u32[]{:S(2)}) collective-permute-start(bf16[576,1024]{1,0:T(8,128)(2,1)} %shard_map.78), channel_id=1, source_target_pairs={{0,12},{1,13},{2,14},{3,15},{4,8},{5,9},{6,10},{7,11},{8,4},{9,5},... | collective-permute-start | bytes 3538952 | tf_op jit(solution)/shard_map/ppermute | solution.py:30
  21.3 2.2 %fusion.1 = bf16[2304,896]{1,0:T(8,128)(2,1)S(1)} fusion(bf16[2304,32]{1,0:T(8,128)(2,1)S(1)} %constant_dynamic-slice_fusion, bf16[2304,768]{1,0:T(8,128)(2,1)} %param.7), kind=kLoop, calls=%fused_computation.2 | loop fusion | flops 12386304 | bytes 7815168 | tf_op jit(solution)/shard_map/concatenate | solution.py:139
  23.9 0.8 copy-done.4
  24.7 1.8 %fusion.9 = f32[1024,896]{1,0:T(8,128)S(1)} fusion(bf16[576,1024]{1,0:T(8,128)(2,1)S(1)} %copy-done.4, bf16[2304,896]{1,0:T(8,128)(2,1)S(1)} %bitcast.53, s32[]{:T(128)S(6)} %select_n.53), kind=kOutput, calls=%fused_computation.27 | convolution fusion | flops 1056964608 | bytes 5881860 | tf_op jit(solution)/shard_map/dot_general | solution.py:144
  26.5 9.2 %collective-permute-done.4 = bf16[576,1024]{1,0:T(8,128)(2,1)S(1)} collective-permute-done((bf16[576,1024]{1,0:T(8,128)(2,1)}, bf16[576,1024]{1,0:T(8,128)(2,1)S(1)}, u32[]{:S(2)}, u32[]{:S(2)}) %collective-permute-start.4) | collective-permute-done | bytes 1179680 | tf_op jit(solution)/shard_map/ppermute | solution.py:30
  36.2 1.3 collective-permute-done.3
  37.6 1.4 collective-permute-start.6
  39.0 1.8 %fusion.5 = f32[1024,896]{1,0:T(8,128)S(1)} fusion(bf16[576,1024]{1,0:T(8,128)(2,1)S(1)} %collective-permute-done.4, bf16[2304,896]{1,0:T(8,128)(2,1)S(1)} %bitcast.54, s32[]{:T(128)S(6)} %select_n.58), kind=kOutput, calls=%fused_computation.23 | convolution fusion | flops 1056964608 | bytes 5881860 | tf_op jit(solution)/shard_map/dot_general | solution.py:144
  40.8 1.8 %fusion.7 = f32[1024,896]{1,0:T(8,128)S(1)} fusion(bf16[576,1024]{1,0:T(8,128)(2,1)S(1)} %collective-permute-done.3, bf16[2304,896]{1,0:T(8,128)(2,1)S(1)} %bitcast.55, s32[]{:T(128)S(6)} %select_n.57), kind=kOutput, calls=%fused_computation.25 | convolution fusion | flops 1056964608 | bytes 5881860 | tf_op jit(solution)/shard_map/dot_general | solution.py:144
  42.6 3.1 %collective-permute-done.5 = bf16[288,1024]{1,0:T(8,128)(2,1)S(1)} collective-permute-done((bf16[288,1024]{1,0:T(8,128)(2,1)S(1)}, bf16[288,1024]{1,0:T(8,128)(2,1)S(1)}, u32[]{:S(2)}, u32[]{:S(2)}) %collective-permute-start.5) | collective-permute-done | bytes 589856 | tf_op jit(solution)/shard_map/ppermute | solution.py:30
  45.8 1.2 fusion.26
  47.0 1.8 %collective-permute-done.6 = bf16[288,1024]{1,0:T(8,128)(2,1)S(1)} collective-permute-done((bf16[288,1024]{1,0:T(8,128)(2,1)S(1)}, bf16[288,1024]{1,0:T(8,128)(2,1)S(1)}, u32[]{:S(2)}, u32[]{:S(2)}) %collective-permute-start.6) | collective-permute-done | bytes 589856 | tf_op jit(solution)/shard_map/ppermute | solution.py:30
  48.8 1.7 %add_add_fusion = f32[1024,896]{1,0:T(8,128)S(1)} fusion(f32[1024,896]{1,0:T(8,128)S(1)} %fusion.26, f32[1024,896]{1,0:T(8,128)S(1)} %fusion.5, f32[1024,896]{1,0:T(8,128)S(1)} %fusion.9, f32[1024,896]{1,0:T(8,128)S(1)} %fusion.7, bf16[288,1024]{1,0:T(8,128)(2,1)S(1)} %collective-permute-done.6, bf16[2304,896]{1,0:T(8,128)(2,1)S(1)} %bitcast.57, ...), kind=kOutput, calls=%fused_computation.4 | convolution fusion | flops 532152320 | bytes 19456004 | tf_op jit(solution)/shard_map/dot_general | solution.py:144
  50.6 2.5 %collective-permute-done.7 = bf16[512,896]{1,0:T(8,128)(2,1)S(1)} collective-permute-done((bf16[512,896]{1,0:T(8,128)(2,1)S(1)}, bf16[512,896]{1,0:T(8,128)(2,1)S(1)}, u32[]{:S(2)}, u32[]{:S(2)}) %collective-permute-start.7) | collective-permute-done | bytes 917536 | tf_op jit(solution)/shard_map/ppermute | solution.py:34
  53.3 26.3 %all_to_all.10 = bf16[64,8,896]{2,1,0:T(8,128)(2,1)S(1)} all-to-all(bf16[64,8,896]{2,1,0:T(8,128)(2,1)S(1)} %fusion.11), channel_id=1, replica_groups=mesh['x'=4,'c'=2,'y'=4,'z'=4] {'x','y','z'}, dimensions={0} | all-to-all | bytes 1835008 | tf_op jit(solution)/shard_map/all_to_all | solution.py:150
  80.2 3.8 %fusion.49 = (f32[8,48]{1,0:T(8,128)S(1)}, f32[8,48,1024]{2,1,0:T(8,128)S(1)}) fusion(bf16[8,48,256]{2,1,0:T(8,128)(2,1)S(1)} %reshape.57, bf16[8,1024,256]{2,1,0:T(8,128)(2,1)} %param.10), kind=kOutput, calls=%fused_computation.74 | convolution fusion | flops 202112640 | bytes 5965312 | tf_op jit(solution)/shard_map/bhe,bte->bht/dot_general | solution.py:158
  84.4 0.9 fusion.4
  85.5 1.0 broadcast_in_dim.2
  86.4 5.5 %all-to-all-start.1 = ((bf16[64,8,768]{2,1,0:T(8,128)(2,1)}), bf16[64,8,768]{2,1,0:T(8,128)(2,1)}, u32[]{:S(2)}, u32[]{:S(2)}) async-start(bf16[64,8,768]{2,1,0:T(8,128)(2,1)} %bitcast.21), calls=%async_computation.1 | async-start | bytes 1572864 | tf_op jit(solution)/shard_map/all_to_all | solution.py:171
  91.9 4.5 %copy.20 = bf16[768,2304]{0,1:T(8,128)(2,1)S(1)} copy(bf16[768,2304]{1,0:T(8,128)(2,1)} %param.9) | data formatting | bytes 7077888 | tf_op args[3]
  96.5 9.7 %all-to-all-done.1 = bf16[64,8,768]{2,1,0:T(8,128)(2,1)} async-done(((bf16[64,8,768]{2,1,0:T(8,128)(2,1)}), bf16[64,8,768]{2,1,0:T(8,128)(2,1)}, u32[]{:S(2)}, u32[]{:S(2)}) %all-to-all-start.1) | async-done | bytes 786464 | tf_op jit(solution)/shard_map/all_to_all | solution.py:171
  106.4 1.8 %convolution_convert_fusion = bf16[576,512]{1,0:T(8,128)(2,1)S(1)} fusion(bf16[2304,768]{1,0:T(8,128)(2,1)S(1)} %bitcast.59, s32[]{:T(128)S(6)} %select_n.59, bf16[64,8,768]{2,1,0:T(8,128)(2,1)} %all-to-all-done.1), kind=kOutput, calls=%fused_computation.13 | convolution fusion | flops 453279744 | bytes 2260996 | tf_op jit(solution)/shard_map/dot_general | solution.py:176
  108.9 1.8 %convolution_convert_fusion.1 = bf16[576,512]{1,0:T(8,128)(2,1)S(1)} fusion(bf16[2304,768]{1,0:T(8,128)(2,1)S(1)} %bitcast.60, s32[]{:T(128)S(6)} %select_n.58, bf16[64,8,768]{2,1,0:T(8,128)(2,1)} %all-to-all-done.1), kind=kOutput, calls=%fused_computation.14 | convolution fusion | flops 453279744 | bytes 2260996 | tf_op jit(solution)/shard_map/dot_general | solution.py:176
  110.7 2.6 %collective-permute-start.13 = (bf16[576,512]{1,0:T(8,128)(2,1)S(1)}, bf16[576,512]{1,0:T(8,128)(2,1)S(1)}, u32[]{:S(2)}, u32[]{:S(2)}) collective-permute-start(bf16[576,512]{1,0:T(8,128)(2,1)S(1)} %convolution_convert_fusion.1), channel_id=1, source_target_pairs={{0,12},{1,13},{2,14},{3,15},{4,8},{5,9},{6,10},{7,11},{8,4},{9,5},... | collective-permute-start | bytes 1769480 | tf_op jit(solution)/shard_map/ppermute | solution.py:30
  113.3 1.8 %convolution_convert_fusion.2 = bf16[576,512]{1,0:T(8,128)(2,1)S(1)} fusion(bf16[2304,768]{1,0:T(8,128)(2,1)S(1)} %bitcast.61, s32[]{:T(128)S(6)} %select_n.57, bf16[64,8,768]{2,1,0:T(8,128)(2,1)} %all-to-all-done.1), kind=kOutput, calls=%fused_computation.15 | convolution fusion | flops 453279744 | bytes 2260996 | tf_op jit(solution)/shard_map/dot_general | solution.py:176
  115.6 0.7 convolution_convert_fusion.5
  116.2 0.7 collective-permute-start.10
  117.6 3.2 %collective-permute-start.11 = (bf16[576,512]{1,0:T(8,128)(2,1)S(1)}, bf16[576,512]{1,0:T(8,128)(2,1)S(1)}, u32[]{:S(2)}, u32[]{:S(2)}) collective-permute-start(bf16[576,512]{1,0:T(8,128)(2,1)S(1)} %convolution_convert_fusion.4), channel_id=1, source_target_pairs={{0,8},{1,9},{2,10},{3,11},{4,12},{5,13},{6,14},{7,15},{8,0},{9,1},... | collective-permute-start | bytes 1769480 | tf_op jit(solution)/shard_map/ppermute | solution.py:30
  120.8 0.7 convolution_convert_fusion.6
  121.9 1.8 %convolution_convert_fusion.3.refs_4_ = bf16[576,512]{1,0:T(8,128)(2,1)S(1)} fusion(bf16[2304,768]{1,0:T(8,128)(2,1)S(1)} %bitcast.65, s32[]{:T(128)S(6)} %select_n.53, bf16[64,8,768]{2,1,0:T(8,128)(2,1)} %all-to-all-done.1), kind=kOutput, calls=%fused_computation.16 | convolution fusion | flops 453279744 | bytes 2260996 | tf_op jit(solution)/shard_map/dot_general | solution.py:176
  123.7 0.7 convolution_convert_fusion.7.refs_0_
  124.4 1.7 %collective-permute-done.13.refs_6_ = bf16[576,512]{1,0:T(8,128)(2,1)S(1)} collective-permute-done((bf16[576,512]{1,0:T(8,128)(2,1)S(1)}, bf16[576,512]{1,0:T(8,128)(2,1)S(1)}, u32[]{:S(2)}, u32[]{:S(2)}) %collective-permute-start.13) | collective-permute-done | bytes 589856 | tf_op jit(solution)/shard_map/ppermute | solution.py:30
  126.0 12.6 %collective-permute-done.10.refs_2_ = bf16[576,512]{1,0:T(8,128)(2,1)S(1)} collective-permute-done((bf16[576,512]{1,0:T(8,128)(2,1)S(1)}, bf16[576,512]{1,0:T(8,128)(2,1)S(1)}, u32[]{:S(2)}, u32[]{:S(2)}) %collective-permute-start.10) | collective-permute-done | bytes 589856 | tf_op jit(solution)/shard_map/ppermute | solution.py:30
  138.7 1.1 shard_map.79
  139.8 0.7 copy-done.2
  141.1 1.3 collective-permute-start.16
  142.4 2.2 %collective-permute-start.17 = (bf16[144,1024]{1,0:T(8,128)(2,1)S(1)}, bf16[144,1024]{1,0:T(8,128)(2,1)S(1)}, u32[]{:S(2)}, u32[]{:S(2)}) collective-permute-start(bf16[144,1024]{1,0:T(8,128)(2,1)S(1)} %get-tuple-element.9), channel_id=1, source_target_pairs={{0,2},{1,3},{2,0},{3,1},{4,6},{5,7},{6,4},{7,5},{8,10},{9,11},{10,... | collective-permute-start | bytes 884744 | tf_op jit(solution)/shard_map/ppermute | solution.py:30
  144.6 2.6 %collective-permute-done.15.refs_1_ = bf16[144,1024]{1,0:T(8,128)(2,1)S(1)} collective-permute-done((bf16[144,1024]{1,0:T(8,128)(2,1)S(1)}, bf16[144,1024]{1,0:T(8,128)(2,1)S(1)}, u32[]{:S(2)}, u32[]{:S(2)}) %collective-permute-start.15) | collective-permute-done | bytes 294944 | tf_op jit(solution)/shard_map/ppermute | solution.py:30
  147.2 4.9 %collective-permute-done.16.refs_2_ = bf16[144,1024]{1,0:T(8,128)(2,1)S(1)} collective-permute-done((bf16[144,1024]{1,0:T(8,128)(2,1)S(1)}, bf16[144,1024]{1,0:T(8,128)(2,1)S(1)}, u32[]{:S(2)}, u32[]{:S(2)}) %collective-permute-start.16) | collective-permute-done | bytes 294944 | tf_op jit(solution)/shard_map/ppermute | solution.py:30
  152.2 0.7 copy-done.8
  153.0 2.1 %shard_map.80 = bf16[144,1024]{1,0:T(8,128)(2,1)} custom-call(s32[1]{0:T(128)} %bitcast.c_ref, bf16[144,1024]{1,0:T(8,128)(2,1)} %copy-done.2, bf16[144,1024]{1,0:T(8,128)(2,1)} %copy-done.7, bf16[144,1024]{1,0:T(8,128)(2,1)} %copy-done.8, bf16[144,1024]{1,0:T(8,128)(2,1)} %copy-done.9), custom_call_target="tpu_custom_call" | custom-call | tf_op jit(solution)/shard_map/pallas_call | solution.py:71
  (59 shorter events, 6.9 us)
Async XLA Ops:
  0.6 7.5 %copy-start = (bf16[2304,512]{1,0:T(8,128)(2,1)S(1)}, bf16[2304,512]{1,0:T(8,128)(2,1)}, u32[]{:S(2)}) copy-start(bf16[2304,512]{1,0:T(8,128)(2,1)} %param.8) | copy-start | bytes 7077892
  2.6 8.9 %collective-permute-start.2 = (bf16[144,1024]{1,0:T(8,128)(2,1)}, bf16[144,1024]{1,0:T(8,128)(2,1)S(1)}, u32[]{:S(2)}, u32[]{:S(2)}) collective-permute-start(bf16[144,1024]{1,0:T(8,128)(2,1)} %shard_map.77.refs_0_), channel_id=1, source_target_pairs={{0,2},{1,3},{2,0},{3,1},{4,6},{5,7},{6,4},{7,5},{8,10},{9,11},{10,... | collective-permute-start | bytes 884744 | tf_op jit(solution)/shard_map/ppermute | solution.py:30
  6.5 8.2 %collective-permute-start.1 = (bf16[144,1024]{1,0:T(8,128)(2,1)}, bf16[144,1024]{1,0:T(8,128)(2,1)S(1)}, u32[]{:S(2)}, u32[]{:S(2)}) collective-permute-start(bf16[144,1024]{1,0:T(8,128)(2,1)} %shard_map.77.refs_0_), channel_id=1, source_target_pairs={{0,3},{1,2},{2,1},{3,0},{4,7},{5,6},{6,5},{7,4},{8,11},{9,10},{10,... | collective-permute-start | bytes 884744 | tf_op jit(solution)/shard_map/ppermute | solution.py:30
  7.2 8.5 %collective-permute-start = (bf16[144,1024]{1,0:T(8,128)(2,1)}, bf16[144,1024]{1,0:T(8,128)(2,1)}, u32[]{:S(2)}, u32[]{:S(2)}) collective-permute-start(bf16[144,1024]{1,0:T(8,128)(2,1)} %shard_map.77.refs_0_), channel_id=1, source_target_pairs={{0,1},{1,0},{2,3},{3,2},{4,5},{5,4},{6,7},{7,6},{8,9},{9,8},{10,11... | collective-permute-start | bytes 884744 | tf_op jit(solution)/shard_map/ppermute | solution.py:30
  11.4 4.3 %copy-start.5 = (bf16[144,1024]{1,0:T(8,128)(2,1)}, bf16[144,1024]{1,0:T(8,128)(2,1)S(1)}, u32[]{:S(2)}) copy-start(bf16[144,1024]{1,0:T(8,128)(2,1)S(1)} %collective-permute-done.2.refs_3_) | copy-start | bytes 884740
  14.7 1.1 copy-start.6
  18.1 17.6 %collective-permute-start.4 = (bf16[576,1024]{1,0:T(8,128)(2,1)}, bf16[576,1024]{1,0:T(8,128)(2,1)S(1)}, u32[]{:S(2)}, u32[]{:S(2)}) collective-permute-start(bf16[576,1024]{1,0:T(8,128)(2,1)} %shard_map.78), channel_id=1, source_target_pairs={{0,12},{1,13},{2,14},{3,15},{4,8},{5,9},{6,10},{7,11},{8,4},{9,5},... | collective-permute-start | bytes 3538952 | tf_op jit(solution)/shard_map/ppermute | solution.py:30
  21.1 16.4 %collective-permute-start.3 = (bf16[576,1024]{1,0:T(8,128)(2,1)}, bf16[576,1024]{1,0:T(8,128)(2,1)S(1)}, u32[]{:S(2)}, u32[]{:S(2)}) collective-permute-start(bf16[576,1024]{1,0:T(8,128)(2,1)} %shard_map.78), channel_id=1, source_target_pairs={{0,4},{1,5},{2,6},{3,7},{4,0},{5,1},{6,2},{7,3},{8,12},{9,13},{10,... | collective-permute-start | bytes 3538952 | tf_op jit(solution)/shard_map/ppermute | solution.py:30
  23.5 1.3 copy-start.4
  35.8 10.0 %collective-permute-start.5 = (bf16[288,1024]{1,0:T(8,128)(2,1)S(1)}, bf16[288,1024]{1,0:T(8,128)(2,1)S(1)}, u32[]{:S(2)}, u32[]{:S(2)}) collective-permute-start(bf16[288,1024]{1,0:T(8,128)(2,1)S(1)} %slice.33), channel_id=1, source_target_pairs={{0,4},{1,5},{2,6},{3,7},{4,0},{5,1},{6,2},{7,3},{8,12},{9,13},{10,... | collective-permute-start | bytes 1769480 | tf_op jit(solution)/shard_map/ppermute | solution.py:30
  37.6 11.2 %collective-permute-start.6 = (bf16[288,1024]{1,0:T(8,128)(2,1)S(1)}, bf16[288,1024]{1,0:T(8,128)(2,1)S(1)}, u32[]{:S(2)}, u32[]{:S(2)}) collective-permute-start(bf16[288,1024]{1,0:T(8,128)(2,1)S(1)} %slice.34), channel_id=1, source_target_pairs={{0,12},{1,13},{2,14},{3,15},{4,8},{5,9},{6,10},{7,11},{8,4},{9,5},... | collective-permute-start | bytes 1769480 | tf_op jit(solution)/shard_map/ppermute | solution.py:30
  50.5 2.6 %collective-permute-start.7 = (bf16[512,896]{1,0:T(8,128)(2,1)S(1)}, bf16[512,896]{1,0:T(8,128)(2,1)S(1)}, u32[]{:S(2)}, u32[]{:S(2)}) collective-permute-start(bf16[512,896]{1,0:T(8,128)(2,1)S(1)} %slice.51), channel_id=1, source_target_pairs={{0,16},{16,0},{1,17},{17,1},{2,18},{18,2},{3,19},{19,3},{4,20},{20... | collective-permute-start | bytes 2752520 | tf_op jit(solution)/shard_map/ppermute | solution.py:34
  80.0 4.4 %copy-start.10 = (bf16[8,512]{1,0:T(8,128)(2,1)}, bf16[8,512]{1,0:T(8,128)(2,1)S(1)}, u32[]{:S(2)}) copy-start(bf16[8,512]{1,0:T(8,128)(2,1)S(1)} %reshape.58) | copy-start | bytes 24580
  80.2 4.3 %copy-start.11 = (bf16[8,1024,256]{2,1,0:T(8,128)(2,1)S(1)}, bf16[8,1024,256]{2,1,0:T(8,128)(2,1)}, u32[]{:S(2)}) copy-start(bf16[8,1024,256]{2,1,0:T(8,128)(2,1)} %param.11) | copy-start | bytes 12582916
  86.4 19.7 %all-to-all-start.1 = ((bf16[64,8,768]{2,1,0:T(8,128)(2,1)}), bf16[64,8,768]{2,1,0:T(8,128)(2,1)}, u32[]{:S(2)}, u32[]{:S(2)}) async-start(bf16[64,8,768]{2,1,0:T(8,128)(2,1)} %bitcast.21), calls=%async_computation.1 | async-start | bytes 1572864 | tf_op jit(solution)/shard_map/all_to_all | solution.py:171
  106.1 9.4 %collective-permute-start.8 = (bf16[512,768]{1,0:T(8,128)(2,1)}, bf16[512,768]{1,0:T(8,128)(2,1)S(1)}, u32[]{:S(2)}, u32[]{:S(2)}) collective-permute-start(bf16[512,768]{1,0:T(8,128)(2,1)} %bitcast.22), channel_id=1, source_target_pairs={{0,16},{16,0},{1,17},{17,1},{2,18},{18,2},{3,19},{19,3},{4,20},{20... | collective-permute-start | bytes 2359304 | tf_op jit(solution)/shard_map/ppermute | solution.py:34
  108.2 13.2 %collective-permute-start.14 = (bf16[576,512]{1,0:T(8,128)(2,1)S(1)}, bf16[576,512]{1,0:T(8,128)(2,1)S(1)}, u32[]{:S(2)}, u32[]{:S(2)}) collective-permute-start(bf16[576,512]{1,0:T(8,128)(2,1)S(1)} %convolution_convert_fusion), channel_id=1, source_target_pairs={{0,8},{1,9},{2,10},{3,11},{4,12},{5,13},{6,14},{7,15},{8,0},{9,1},... | collective-permute-start | bytes 1769480 | tf_op jit(solution)/shard_map/ppermute | solution.py:30
  110.7 15.4 %collective-permute-start.13 = (bf16[576,512]{1,0:T(8,128)(2,1)S(1)}, bf16[576,512]{1,0:T(8,128)(2,1)S(1)}, u32[]{:S(2)}, u32[]{:S(2)}) collective-permute-start(bf16[576,512]{1,0:T(8,128)(2,1)S(1)} %convolution_convert_fusion.1), channel_id=1, source_target_pairs={{0,12},{1,13},{2,14},{3,15},{4,8},{5,9},{6,10},{7,11},{8,4},{9,5},... | collective-permute-start | bytes 1769480 | tf_op jit(solution)/shard_map/ppermute | solution.py:30
  115.1 10.9 %collective-permute-start.12 = (bf16[576,512]{1,0:T(8,128)(2,1)S(1)}, bf16[576,512]{1,0:T(8,128)(2,1)S(1)}, u32[]{:S(2)}, u32[]{:S(2)}) collective-permute-start(bf16[576,512]{1,0:T(8,128)(2,1)S(1)} %convolution_convert_fusion.2), channel_id=1, source_target_pairs={{0,4},{1,5},{2,6},{3,7},{4,0},{5,1},{6,2},{7,3},{8,12},{9,13},{10,... | collective-permute-start | bytes 1769480 | tf_op jit(solution)/shard_map/ppermute | solution.py:30
  116.2 22.5 %collective-permute-start.10 = (bf16[576,512]{1,0:T(8,128)(2,1)S(1)}, bf16[576,512]{1,0:T(8,128)(2,1)S(1)}, u32[]{:S(2)}, u32[]{:S(2)}) collective-permute-start(bf16[576,512]{1,0:T(8,128)(2,1)S(1)} %convolution_convert_fusion.5), channel_id=1, source_target_pairs={{0,12},{1,13},{2,14},{3,15},{4,8},{5,9},{6,10},{7,11},{8,4},{9,5},... | collective-permute-start | bytes 1769480 | tf_op jit(solution)/shard_map/ppermute | solution.py:30
  117.6 21.1 %copy-start.3 = (s32[4]{0:T(128)S(1)}, s32[4]{0:T(128)}, u32[]{:S(2)}) copy-start(s32[4]{0:T(128)} %pad_add_fusion.at_ref) | copy-start | bytes 52
  117.6 21.1 %collective-permute-start.11 = (bf16[576,512]{1,0:T(8,128)(2,1)S(1)}, bf16[576,512]{1,0:T(8,128)(2,1)S(1)}, u32[]{:S(2)}, u32[]{:S(2)}) collective-permute-start(bf16[576,512]{1,0:T(8,128)(2,1)S(1)} %convolution_convert_fusion.4), channel_id=1, source_target_pairs={{0,8},{1,9},{2,10},{3,11},{4,12},{5,13},{6,14},{7,15},{8,0},{9,1},... | collective-permute-start | bytes 1769480 | tf_op jit(solution)/shard_map/ppermute | solution.py:30
  121.5 17.2 %collective-permute-start.9 = (bf16[576,512]{1,0:T(8,128)(2,1)S(1)}, bf16[576,512]{1,0:T(8,128)(2,1)S(1)}, u32[]{:S(2)}, u32[]{:S(2)}) collective-permute-start(bf16[576,512]{1,0:T(8,128)(2,1)S(1)} %convolution_convert_fusion.6), channel_id=1, source_target_pairs={{0,4},{1,5},{2,6},{3,7},{4,0},{5,1},{6,2},{7,3},{8,12},{9,13},{10,... | collective-permute-start | bytes 1769480 | tf_op jit(solution)/shard_map/ppermute | solution.py:30
  123.7 31.5 %copy-start.1 = (bf16[2304,512]{1,0:T(8,128)(2,1)S(1)}, bf16[2304,512]{1,0:T(8,128)(2,1)}, u32[]{:S(2)}) copy-start(bf16[2304,512]{1,0:T(8,128)(2,1)} %param.8) | copy-start | bytes 7077892
  139.8 0.7 copy-start.2
  140.5 6.7 %collective-permute-start.15 = (bf16[144,1024]{1,0:T(8,128)(2,1)S(1)}, bf16[144,1024]{1,0:T(8,128)(2,1)S(1)}, u32[]{:S(2)}, u32[]{:S(2)}) collective-permute-start(bf16[144,1024]{1,0:T(8,128)(2,1)S(1)} %get-tuple-element.7), channel_id=1, source_target_pairs={{0,1},{1,0},{2,3},{3,2},{4,5},{5,4},{6,7},{7,6},{8,9},{9,8},{10,11... | collective-permute-start | bytes 884744 | tf_op jit(solution)/shard_map/ppermute | solution.py:30
  141.1 11.1 %collective-permute-start.16 = (bf16[144,1024]{1,0:T(8,128)(2,1)S(1)}, bf16[144,1024]{1,0:T(8,128)(2,1)S(1)}, u32[]{:S(2)}, u32[]{:S(2)}) collective-permute-start(bf16[144,1024]{1,0:T(8,128)(2,1)S(1)} %get-tuple-element.8), channel_id=1, source_target_pairs={{0,3},{1,2},{2,1},{3,0},{4,7},{5,6},{6,5},{7,4},{8,11},{9,10},{10,... | collective-permute-start | bytes 884744 | tf_op jit(solution)/shard_map/ppermute | solution.py:30
  142.4 9.7 %collective-permute-start.17 = (bf16[144,1024]{1,0:T(8,128)(2,1)S(1)}, bf16[144,1024]{1,0:T(8,128)(2,1)S(1)}, u32[]{:S(2)}, u32[]{:S(2)}) collective-permute-start(bf16[144,1024]{1,0:T(8,128)(2,1)S(1)} %get-tuple-element.9), channel_id=1, source_target_pairs={{0,2},{1,3},{2,0},{3,1},{4,6},{5,7},{6,4},{7,5},{8,10},{9,11},{10,... | collective-permute-start | bytes 884744 | tf_op jit(solution)/shard_map/ppermute | solution.py:30
  147.2 4.9 %copy-start.7 = (bf16[144,1024]{1,0:T(8,128)(2,1)}, bf16[144,1024]{1,0:T(8,128)(2,1)S(1)}, u32[]{:S(2)}) copy-start(bf16[144,1024]{1,0:T(8,128)(2,1)S(1)} %collective-permute-done.15.refs_1_) | copy-start | bytes 884740
  152.2 0.7 copy-start.8
  152.2 0.8 copy-start.9

commit v4 on v3

--- a/solution.py
+++ b/solution.py
@@ -1,3 +1,5 @@
+import functools
+
 import jax
 import jax.numpy as jnp
 from jax import lax
@@ -39,6 +41,10 @@
 VMEM = pl.BlockSpec(memory_space=pltpu.VMEM)
 
 
+def few(mib):
+    return pltpu.CompilerParams(vmem_limit_bytes=mib * 1024 * 1024)
+
+
 def block(i, n):
     return pl.ds(pl.multiple_of(i * n, 16), n)
 
@@ -56,7 +62,8 @@
 
 def split_cores(c, t):
     return pl.pallas_call(
-        split_kernel, in_specs=[SMEM, VMEM], out_specs=VMEM, out_shape=jax.ShapeDtypeStruct(t.shape, t.dtype)
+        split_kernel,
+        compiler_params=few(2), in_specs=[SMEM, VMEM], out_specs=VMEM, out_shape=jax.ShapeDtypeStruct(t.shape, t.dtype)
     )(c.reshape(1), t)
 
 
@@ -70,46 +77,103 @@
 def merge_cores(c, *terms):
     return pl.pallas_call(
         merge_kernel,
+        compiler_params=few(6),
         in_specs=[SMEM] + [VMEM] * len(terms),
         out_specs=VMEM,
         out_shape=jax.ShapeDtypeStruct(terms[0].shape, BF16),
     )(c.reshape(1), *terms)
 
 
+def join_kernel(a_ref, b_ref, out_ref):
+    out_ref[: a_ref.shape[0], :] = a_ref[...]
+    out_ref[a_ref.shape[0] :, :] = b_ref[...]
+
+
+def join(a, b):
+    return pl.pallas_call(
+        join_kernel,
+        compiler_params=few(6),
+        in_specs=[VMEM] * 2,
+        out_specs=VMEM,
+        out_shape=jax.ShapeDtypeStruct((2 * a.shape[0], a.shape[1]), a.dtype),
+    )(a, b)
+
+
+def add_products_kernel(side, at_ref, part_ref, *refs):
+    *pieces, w_ref, out_ref = refs
+    m, n = out_ref.shape
+    k = pieces[0].shape[0]
+    for i in range(0, m, 256):
+        at = slice(side * m + i, side * m + i + 256)
+        turned = [piece[:, at].T for piece in pieces]
+        for j in range(0, n, 256):
+            to = slice(j, min(j + 256, n))
+            total = part_ref[i : i + 256, to] if part_ref.shape[0] == m else part_ref[at, to]
+            for p, piece in enumerate(turned):
+                w = w_ref[pl.ds(pl.multiple_of(at_ref[p], 16), k), to]
+                total += jnp.dot(piece, w, preferred_element_type=F32)
+            out_ref[i : i + 256, to] = total.astype(out_ref.dtype)
+
+
+def add_products(starts, part, pieces, w, rows, side=0, dtype=F32):
+    return pl.pallas_call(
+        functools.partial(add_products_kernel, side),
+        compiler_params=few(16),
+        in_specs=[SMEM] + [VMEM] * (2 + len(pieces)),
+        out_specs=VMEM,
+        out_shape=jax.ShapeDtypeStruct((rows, part.shape[1]), dtype),
+        cost_estimate=pl.CostEstimate(flops=0, bytes_accessed=0, transcendentals=0),
+    )(jnp.stack(starts), part, *pieces, w)
+
+
+def in_halves(i, n, use):
+    for half in range(2):
+
+        @pl.when(i // 2 == half)
+        def _():
+            use(half, block(i - 2 * half, n))
+
+
 def assemble_kernel(at_ref, *refs):
     n = refs[0].shape[0]
     for p in range(4):
-        refs[4][block(at_ref[p], n), :] = refs[p][...]
+
+        def put(half, at):
+            refs[4 + half][at, :] = refs[p][...]
+
+        in_halves(at_ref[p], n, put)
 
 
 def assemble(places, *pieces):
     n, m = pieces[0].shape
     return pl.pallas_call(
         assemble_kernel,
+        compiler_params=few(6),
         in_specs=[SMEM] + [VMEM] * 4,
-        out_specs=VMEM,
-        out_shape=jax.ShapeDtypeStruct((4 * n, m), BF16),
+        out_specs=[VMEM] * 2,
+        out_shape=[jax.ShapeDtypeStruct((2 * n, m), BF16)] * 2,
     )(jnp.stack(places), *pieces)
 
 
 def part_kernel(at_ref, *refs):
-    terms, outs = refs[:8], refs[8:]
-    n, m = terms[0].shape[0] // 4, terms[0].shape[1]
+    terms, outs = (refs[:3], refs[3:6]), refs[6:]
+    n = outs[0].shape[0]
     for p in range(4):
-        at = block(at_ref[p], n)
-        for half in range(2):
-            total = sum(t[at, :].astype(F32) for t in terms[4 * half : 4 * half + 4])
-            outs[p][:, half * m : (half + 1) * m] = total.astype(BF16)
+
+        def put(half, at):
+            outs[p][...] = sum(t[at, :].astype(F32) for t in terms[half]).astype(BF16)
+
+        in_halves(at_ref[p], n, put)
 
 
 def add_and_part(places, *terms):
     n, m = terms[0].shape
     return pl.pallas_call(
         part_kernel,
-        in_specs=[SMEM] + [VMEM] * 8,
+        compiler_params=few(12),
+        in_specs=[SMEM] + [VMEM] * 6,
         out_specs=[VMEM] * 4,
-        out_shape=[jax.ShapeDtypeStruct((n // 4, 2 * m), BF16)] * 4,
-        compiler_params=pltpu.CompilerParams(vmem_limit_bytes=32 * 1024 * 1024),
+        out_shape=[jax.ShapeDtypeStruct((n // 2, m), BF16)] * 4,
     )(jnp.stack(places), *terms)
 
 
@@ -126,11 +190,8 @@
     firsts, seconds = [first ^ m for m in (0, *MASKS)], [second ^ m for m in (0, *MASKS)]
 
     t = split_cores(c, tokens.T)
-    t = assemble(firsts, t, *[exchange(t, 0, m) for m in MASKS])
-    t1, t3 = exchange(t, 1, 1), exchange(t, 1, 3)
-    half = t.shape[0] // 2
-    low, high = exchange(t3[:half], 1, 1), exchange(t1[half:], 1, 3)
-
+    low, high = assemble(firsts, t, *[exchange(t, 0, m) for m in MASKS])
+    half = low.shape[0]
     def by_blocks(w):
         w = w.reshape(4, 4, feat, -1)
         return jnp.where(c == 0, w, w.swapaxes(0, 1)).reshape(16 * feat, -1)
@@ -143,10 +204,18 @@
         w = lax.dynamic_slice_in_dim(w_all, i * 4 * feat + skip, v.shape[0], 0)
         return lax.dot_general(v, w, (((0,), (0,)), ((), ())), preferred_element_type=F32)
 
-    part = product(t, seconds[0]) + product(t1, seconds[1]) + product(t3, seconds[2])
-    part = part + product(low, seconds[3]) + product(high, seconds[3], half)
-    part = core_swap(part[:512].astype(BF16)).astype(F32) + part[512:]
-    part = part.astype(BF16)
+    high1, low3 = exchange(high, 1, 1), exchange(low, 1, 3)
+    part = product(low, seconds[0]) + product(high, seconds[0], half)
+    low, high, part = lax.optimization_barrier((low, high, part))
+    low1, high3 = exchange(low, 1, 1), exchange(high, 1, 3)
+    low2, high2 = exchange(low3, 1, 1), exchange(high1, 1, 3)
+    part = part + product(high1, seconds[1], half) + product(low3, seconds[2])
+    starts = [seconds[1] * 2 * half, seconds[2] * 2 * half + half, seconds[3] * 2 * half, seconds[3] * 2 * half + half]
+    part = add_products(starts[:2], part, (low1, high3), w_all, 1024)
+    last = low2, high2
+    given = core_swap(add_products(starts[2:], part, last, w_all, 512, 0, BF16))
+    part = add_products(starts[2:], part, last, w_all, 512, 1)
+    part = (part + given.astype(F32)).astype(BF16)
     part = lax.all_to_all(part.reshape(64, rows_dev, -1), ("x", "y", "z"), 0, 0, tiled=True)
     whole = jnp.sum(part.astype(F32).reshape(4, 16, rows_dev, -1), axis=0).astype(BF16)
     queries = whole[:, :, :q_cols].transpose(1, 0, 2).reshape(rows_dev, -1, head_size)
@@ -169,17 +238,21 @@
 
     spread = jnp.broadcast_to(attended[None], (4, 16, rows_dev, q_cols)).reshape(64, rows_dev, q_cols)
     mine = lax.all_to_all(spread, ("x", "y", "z"), 0, 0, tiled=True).reshape(512, q_cols)
-    theirs = core_swap(mine)
-
-    def outward(i, v):
-        w = lax.dynamic_slice_in_dim(w_out, i * 4 * feat, 4 * feat, 0)
-        return lax.dot_general(w, v, (((1,), (1,)), ((), ())), preferred_element_type=F32).astype(BF16)
-
-    terms = []
-    for v in (theirs, mine):
-        terms.append(outward(seconds[0], v))
-        terms += [exchange(outward(seconds[i + 1], v), 1, MASKS[i]) for i in range(3)]
-    keep, *away = add_and_part(firsts, *terms)
+    mine, w_out = lax.optimization_barrier((mine, w_out))
+    rows = join(core_swap(mine), mine)
+
+    def outward(i, skip):
+        w = lax.dynamic_slice_in_dim(w_out, i * 4 * feat + skip, half, 0)
+        return lax.dot_general(w, rows, (((1,), (1,)), ((), ())), preferred_element_type=F32)
+
+    def send(v, mask):
+        return exchange(v.astype(BF16), 1, mask)
+
+    low2, high2 = send(outward(seconds[3], 0), 1), send(outward(seconds[3], half), 3)
+    low1, high3 = send(outward(seconds[1], 0), 1), send(outward(seconds[2], half), 3)
+    high1, low3 = send(outward(seconds[1], half) + high2.astype(F32), 1), send(outward(seconds[2], 0) + low2.astype(F32), 3)
+    low, high = outward(seconds[0], 0).astype(BF16), outward(seconds[0], half).astype(BF16)
+    keep, *away = add_and_part(firsts, low, low1, low3, high, high1, high3)
     out = merge_cores(c, keep, *[exchange(v, 0, m) for v, m in zip(away, MASKS)])
     return out.T, new_keyvalue
 

time: 156 us -> 141 us (0.904)
  waiting for transfers between devices: 56.8 us -> 36.5 us
  other arithmetic: 4.26 us -> 13.5 us
  matrix products: 22.8 us -> 16.1 us
  starting transfers between devices: 27.7 us -> 29.5 us
  Pallas kernels: 7.54 us -> 9.2 us
    ppermute x16 -> x18, waiting for transfers between devices: 44.7 us -> 29.8 us  [exchange(): return lax.ppermute(v, AXES, partner_pairs(phase, mask))]
    select_n x2, other arithmetic: 0.74 us -> 9.05 us  [by_blocks(): return jnp.where(c == 0, w, w.swapaxes(0, 1)).reshape(16 * feat, -1)]
    all_to_all x1, waiting for transfers between devices: 9.66 us -> 3.83 us  [shards(): lax.all_to_all(spread, ('x', 'y', 'z'), 0, 0, tiled=True)]
    dot_general x8, matrix products: 9.76 us -> 6.24 us  [outward(): lax.dot_general(w, rows, (((1,), (1,)), ((), ())), preferred_element_type...]
    dot_general x5 -> x4, matrix products: 8.28 us -> 5.06 us  [product(): lax.dot_general(v, w, (((0,), (0,)), ((), ())), preferred_element_type=F32)]
    ppermute x16 -> x18, starting transfers between devices: 22.2 us -> 24.4 us  [exchange(): return lax.ppermute(v, AXES, partner_pairs(phase, mask))]
    pallas_call x4 -> x8, Pallas kernels: 7.54 us -> 9.2 us  [the longest x3 6.37 us: add_products(): pl.pallas_call(functools.partial(add_products_kernel, side), compiler_par...]
    unnamed x25 -> x13, local copies, waits for them, and re-layouts: 6.92 us -> 6.9 us
  transfers between devices with their start and end apart: 19 -> 21, of which waited for: 13 -> 13; matrix products, arithmetic and copies ran while one was open for 16% -> 20% of each run, Pallas kernels for 0% -> 3%
where the time goes in v4:
time: 141 us
  waiting for transfers between devices  36.5 us (26%)
  starting transfers between devices  29.5 us (21%)
  blocking collectives  26.3 us (19%)
  matrix products  16.1 us (11%)
  other arithmetic  13.5 us (10%)
  Pallas kernels  9.2 us (7%)
  local copies, waits for them, and re-layouts  8.48 us (6%)
    ppermute x18, waiting for transfers between devices, exchange(): return lax.ppermute(v, AXES, partner_pairs(phase, mask))  29.8 us
    all_to_all x1, blocking collectives, shards(): lax.all_to_all(part.reshape(64, rows_dev, -1), ('x', 'y', 'z'), 0, 0, til...  26.3 us
    ppermute x18, starting transfers between devices, exchange(): return lax.ppermute(v, AXES, partner_pairs(phase, mask))  24.4 us
    select_n x2, other arithmetic, by_blocks(): return jnp.where(c == 0, w, w.swapaxes(0, 1)).reshape(16 * feat, -1)  9.05 us
    unnamed x13, local copies, waits for them, and re-layouts  6.9 us
    pallas_call x3, Pallas kernels, add_products(): pl.pallas_call(functools.partial(add_products_kernel, side), compiler_par...  6.37 us
    dot_general x8, matrix products, outward(): lax.dot_general(w, rows, (((1,), (1,)), ((), ())), preferred_element_type...  6.24 us
    dot_general x4, matrix products, product(): lax.dot_general(v, w, (((0,), (0,)), ((), ())), preferred_element_type=F32)  5.06 us
  transfers between devices with their start and end apart: 21, of which 13 were waited for; matrix products, arithmetic and copies ran while one was open for 20% of the time, Pallas kernels for 3%

profile of v4, /device:TPU:0, one launch (start us, length us, event | category | flops | bytes accessed | tf_op | source)
XLA Modules:
  0.0 140.6 jit_solution(2060460462820910884)
XLA Ops:
  0.7 1.1 copy-done.2
  1.8 2.1 %collective-permute-start = (bf16[144,1024]{1,0:T(8,128)(2,1)S(1)}, bf16[144,1024]{1,0:T(8,128)(2,1)S(1)}, u32[]{:S(2)}, u32[]{:S(2)}) collective-permute-start(bf16[144,1024]{1,0:T(8,128)(2,1)S(1)} %shard_map.77.refs_0_), channel_id=1, source_target_pairs={{0,1},{1,0},{2,3},{3,2},{4,5},{5,4},{6,7},{7,6},{8,9},{9,8},{10,11... | collective-permute-start | bytes 884744 | tf_op jit(solution)/shard_map/ppermute | solution.py:32
  3.9 2.5 %collective-permute-start.1 = (bf16[144,1024]{1,0:T(8,128)(2,1)S(1)}, bf16[144,1024]{1,0:T(8,128)(2,1)S(1)}, u32[]{:S(2)}, u32[]{:S(2)}) collective-permute-start(bf16[144,1024]{1,0:T(8,128)(2,1)S(1)} %shard_map.77.refs_0_), channel_id=1, source_target_pairs={{0,3},{1,2},{2,1},{3,0},{4,7},{5,6},{6,5},{7,4},{8,11},{9,10},{10,... | collective-permute-start | bytes 884744 | tf_op jit(solution)/shard_map/ppermute | solution.py:32
  6.4 1.1 collective-permute-start.2
  7.7 3.6 %fusion.1 = bf16[2304,896]{1,0:T(8,128)(2,1)} fusion(bf16[2304,32]{1,0:T(8,128)(2,1)S(1)} %constant_dynamic-slice_fusion, bf16[2304,768]{1,0:T(8,128)(2,1)} %param.7), kind=kLoop, calls=%fused_computation.2 | loop fusion | flops 12386304 | bytes 7815168 | tf_op jit(solution)/shard_map/concatenate | solution.py:200
  11.5 3.9 %bitcast_select_fusion = bf16[4,4,144,896]{3,2,1,0:T(8,128)(2,1)S(1)} fusion(bf16[4,4,144,896]{3,2,1,0:T(8,128)(2,1)} %bitcast.60, pred[]{:T(512)S(6)} %eq.2), kind=kLoop, calls=%fused_computation.3 | loop fusion | flops 2064384 | bytes 8257537 | tf_op jit(solution)/shard_map/jit(_where)/select_n | solution.py:197
  15.4 0.7 shard_map.78
  16.1 1.7 %collective-permute-start.3 = (bf16[288,1024]{1,0:T(8,128)(2,1)S(1)}, bf16[288,1024]{1,0:T(8,128)(2,1)S(1)}, u32[]{:S(2)}, u32[]{:S(2)}) collective-permute-start(bf16[288,1024]{1,0:T(8,128)(2,1)S(1)} %get-tuple-element.17), channel_id=1, source_target_pairs={{0,4},{1,5},{2,6},{3,7},{4,0},{5,1},{6,2},{7,3},{8,12},{9,13},{10,... | collective-permute-start | bytes 1769480 | tf_op jit(solution)/shard_map/ppermute | solution.py:32
  17.7 2.2 %collective-permute-start.4 = (bf16[288,1024]{1,0:T(8,128)(2,1)S(1)}, bf16[288,1024]{1,0:T(8,128)(2,1)S(1)}, u32[]{:S(2)}, u32[]{:S(2)}) collective-permute-start(bf16[288,1024]{1,0:T(8,128)(2,1)S(1)} %get-tuple-element.16), channel_id=1, source_target_pairs={{0,12},{1,13},{2,14},{3,15},{4,8},{5,9},{6,10},{7,11},{8,4},{9,5},... | collective-permute-start | bytes 1769480 | tf_op jit(solution)/shard_map/ppermute | solution.py:32
  19.9 1.2 fusion.15
  21.1 1.3 convolution_add_fusion
  22.5 0.8 collective-permute-start.5
  23.8 5.0 %collective-permute-done.4 = bf16[288,1024]{1,0:T(8,128)(2,1)S(1)} collective-permute-done((bf16[288,1024]{1,0:T(8,128)(2,1)S(1)}, bf16[288,1024]{1,0:T(8,128)(2,1)S(1)}, u32[]{:S(2)}, u32[]{:S(2)}) %collective-permute-start.4) | collective-permute-done | bytes 589856 | tf_op jit(solution)/shard_map/ppermute | solution.py:32
  28.8 2.2 %collective-permute-start.8 = (bf16[288,1024]{1,0:T(8,128)(2,1)S(1)}, bf16[288,1024]{1,0:T(8,128)(2,1)S(1)}, u32[]{:S(2)}, u32[]{:S(2)}) collective-permute-start(bf16[288,1024]{1,0:T(8,128)(2,1)S(1)} %collective-permute-done.3), channel_id=1, source_target_pairs={{0,12},{1,13},{2,14},{3,15},{4,8},{5,9},{6,10},{7,11},{8,4},{9,5},... | collective-permute-start | bytes 1769480 | tf_op jit(solution)/shard_map/ppermute | solution.py:32
  31.1 1.2 fusion.13
  32.3 1.3 add_add_fusion.part_ref
  33.6 1.5 %collective-permute-done.6.refs_1_ = bf16[288,1024]{1,0:T(8,128)(2,1)S(1)} collective-permute-done((bf16[288,1024]{1,0:T(8,128)(2,1)S(1)}, bf16[288,1024]{1,0:T(8,128)(2,1)S(1)}, u32[]{:S(2)}, u32[]{:S(2)}) %collective-permute-start.6) | collective-permute-done | bytes 589856 | tf_op jit(solution)/shard_map/ppermute | solution.py:32
  35.1 2.8 %shard_map.79.part_ref = f32[1024,896]{1,0:T(8,128)S(1)} custom-call(s32[2]{0:T(128)S(1)} %get-tuple-element.31.at_ref, f32[1024,896]{1,0:T(8,128)S(1)} %add_add_fusion.part_ref, bf16[288,1024]{1,0:T(8,128)(2,1)S(1)} %collective-permute-done.5.refs_0_, bf16[288,1024]{1,0:T(8,128)(2,1)S(1)} %collective-permute-done.6.refs_1_, bf16[2304,896]{1,0:T(8,128)(2,1)S(1)} %bitcast.54), custom_call_target="tpu_custom_call" | custom-call | tf_op jit(solution)/shard_map/pallas_call | solution.py:119
  37.9 0.8 collective-permute-done.7.refs_0_
  38.8 2.7 %collective-permute-done.8.refs_1_ = bf16[288,1024]{1,0:T(8,128)(2,1)S(1)} collective-permute-done((bf16[288,1024]{1,0:T(8,128)(2,1)S(1)}, bf16[288,1024]{1,0:T(8,128)(2,1)S(1)}, u32[]{:S(2)}, u32[]{:S(2)}) %collective-permute-start.8) | collective-permute-done | bytes 589856 | tf_op jit(solution)/shard_map/ppermute | solution.py:32
  41.5 1.8 %shard_map.81 = bf16[512,896]{1,0:T(8,128)(2,1)S(1)} custom-call(s32[2]{0:T(128)S(1)} %get-tuple-element.30.at_ref, f32[1024,896]{1,0:T(8,128)S(1)} %shard_map.79.part_ref, bf16[288,1024]{1,0:T(8,128)(2,1)S(1)} %collective-permute-done.7.refs_0_, bf16[288,1024]{1,0:T(8,128)(2,1)S(1)} %collective-permute-done.8.refs_1_, bf16[2304,896]{1,0:T(8,128)(2,1)S(1)} %bitcast.55), custom_call_target="tpu_custom_call" | custom-call | tf_op jit(solution)/shard_map/pallas_call | solution.py:119
  43.5 1.8 %shard_map.80 = f32[512,896]{1,0:T(8,128)S(1)} custom-call(s32[2]{0:T(128)S(1)} %get-tuple-element.30.at_ref, f32[1024,896]{1,0:T(8,128)S(1)} %shard_map.79.part_ref, bf16[288,1024]{1,0:T(8,128)(2,1)S(1)} %collective-permute-done.7.refs_0_, bf16[288,1024]{1,0:T(8,128)(2,1)S(1)} %collective-permute-done.8.refs_1_, bf16[2304,896]{1,0:T(8,128)(2,1)S(1)} %bitcast.56), custom_call_target="tpu_custom_call" | custom-call | tf_op jit(solution)/shard_map/pallas_call | solution.py:119
  45.3 0.7 collective-permute-done.9
  46.2 26.3 %all_to_all.10 = bf16[64,8,896]{2,1,0:T(8,128)(2,1)S(1)} all-to-all(bf16[64,8,896]{2,1,0:T(8,128)(2,1)S(1)} %fusion.6), channel_id=1, replica_groups=mesh['x'=4,'c'=2,'y'=4,'z'=4] {'x','y','z'}, dimensions={0} | all-to-all | bytes 1835008 | tf_op jit(solution)/shard_map/all_to_all | solution.py:219
  73.1 3.8 %fusion.42 = (f32[8,48]{1,0:T(8,128)S(1)}, f32[8,48,1024]{2,1,0:T(8,128)S(1)}) fusion(bf16[8,48,256]{2,1,0:T(8,128)(2,1)S(1)} %reshape.55, bf16[8,1024,256]{2,1,0:T(8,128)(2,1)} %param.10), kind=kOutput, calls=%fused_computation.69 | convolution fusion | flops 202112640 | bytes 5965312 | tf_op jit(solution)/shard_map/bhe,bte->bht/dot_general | solution.py:227
  77.3 0.9 fusion.5
  78.3 0.9 broadcast_in_dim.2
  79.3 4.8 %all-to-all-start.1 = ((bf16[64,8,768]{2,1,0:T(8,128)(2,1)}), bf16[64,8,768]{2,1,0:T(8,128)(2,1)S(1)}, u32[]{:S(2)}, u32[]{:S(2)}) async-start(bf16[64,8,768]{2,1,0:T(8,128)(2,1)} %bitcast.21), calls=%async_computation.1 | async-start | bytes 1572864 | tf_op jit(solution)/shard_map/all_to_all | solution.py:240
  84.0 5.8 %copy.24 = bf16[768,2304]{0,1:T(8,128)(2,1)} copy(bf16[768,2304]{1,0:T(8,128)(2,1)} %param.9) | data formatting | bytes 7077888 | tf_op args[3]
  89.8 5.2 %bitcast_select_fusion.1 = bf16[4,4,144,768]{3,2,1,0:T(8,128)(2,1)} fusion(bf16[4,4,144,768]{3,2,1,0:T(8,128)(2,1)} %bitcast.61, pred[]{:T(512)S(6)} %eq.2), kind=kLoop, calls=%fused_computation.5 | loop fusion | flops 1769472 | bytes 7077889 | tf_op jit(solution)/shard_map/jit(_where)/select_n | solution.py:197
  95.0 3.8 %all-to-all-done.1 = bf16[64,8,768]{2,1,0:T(8,128)(2,1)S(1)} async-done(((bf16[64,8,768]{2,1,0:T(8,128)(2,1)}), bf16[64,8,768]{2,1,0:T(8,128)(2,1)S(1)}, u32[]{:S(2)}, u32[]{:S(2)}) %all-to-all-start.1) | async-done | bytes 786464 | tf_op jit(solution)/shard_map/all_to_all | solution.py:240
  98.8 2.3 %collective-permute-done.10.a_ref = bf16[512,768]{1,0:T(8,128)(2,1)S(1)} collective-permute-done((bf16[512,768]{1,0:T(8,128)(2,1)S(1)}, bf16[512,768]{1,0:T(8,128)(2,1)S(1)}, u32[]{:S(2)}, u32[]{:S(2)}) %collective-permute-start.10) | collective-permute-done | bytes 786464 | tf_op jit(solution)/shard_map/ppermute | solution.py:36
  101.2 1.7 %convolution_convert_fusion.1 = bf16[288,1024]{1,0:T(8,128)(2,1)S(1)} fusion(bf16[1024,768]{1,0:T(8,128)(2,1)S(1)} %shard_map.82, bf16[2304,768]{1,0:T(8,128)(2,1)} %bitcast.63, s32[]{:T(128)S(6)} %select_n.67), kind=kOutput, calls=%fused_computation.15 | convolution fusion | flops 453279744 | bytes 2605060 | tf_op jit(solution)/shard_map/dot_general | solution.py:246
  104.9 2.8 %collective-permute-start.16 = (bf16[288,1024]{1,0:T(8,128)(2,1)S(1)}, bf16[288,1024]{1,0:T(8,128)(2,1)S(1)}, u32[]{:S(2)}, u32[]{:S(2)}) collective-permute-start(bf16[288,1024]{1,0:T(8,128)(2,1)S(1)} %convolution_convert_fusion), channel_id=1, source_target_pairs={{0,12},{1,13},{2,14},{3,15},{4,8},{5,9},{6,10},{7,11},{8,4},{9,5},... | collective-permute-start | bytes 1769480 | tf_op jit(solution)/shard_map/ppermute | solution.py:32
  108.4 1.5 %collective-permute-start.11 = (bf16[288,1024]{1,0:T(8,128)(2,1)S(1)}, bf16[288,1024]{1,0:T(8,128)(2,1)S(1)}, u32[]{:S(2)}, u32[]{:S(2)}) collective-permute-start(bf16[288,1024]{1,0:T(8,128)(2,1)S(1)} %convolution_convert_fusion.4), channel_id=1, source_target_pairs={{0,4},{1,5},{2,6},{3,7},{4,0},{5,1},{6,2},{7,3},{8,12},{9,13},{10,... | collective-permute-start | bytes 1769480 | tf_op jit(solution)/shard_map/ppermute | solution.py:32
  109.9 4.2 %collective-permute-done.14 = bf16[288,1024]{1,0:T(8,128)(2,1)S(1)} collective-permute-done((bf16[288,1024]{1,0:T(8,128)(2,1)S(1)}, bf16[288,1024]{1,0:T(8,128)(2,1)S(1)}, u32[]{:S(2)}, u32[]{:S(2)}) %collective-permute-start.14) | collective-permute-done | bytes 589856 | tf_op jit(solution)/shard_map/ppermute | solution.py:32
  114.8 0.7 fusion.3
  115.5 2.1 %collective-permute-start.13 = (bf16[288,1024]{1,0:T(8,128)(2,1)S(1)}, bf16[288,1024]{1,0:T(8,128)(2,1)S(1)}, u32[]{:S(2)}, u32[]{:S(2)}) collective-permute-start(bf16[288,1024]{1,0:T(8,128)(2,1)S(1)} %fusion.3), channel_id=1, source_target_pairs={{0,12},{1,13},{2,14},{3,15},{4,8},{5,9},{6,10},{7,11},{8,4},{9,5},... | collective-permute-start | bytes 1769480 | tf_op jit(solution)/shard_map/ppermute | solution.py:32
  118.2 0.7 convolution_convert_fusion.5.refs_0_
  118.9 1.5 %collective-permute-done.16.refs_5_ = bf16[288,1024]{1,0:T(8,128)(2,1)S(1)} collective-permute-done((bf16[288,1024]{1,0:T(8,128)(2,1)S(1)}, bf16[288,1024]{1,0:T(8,128)(2,1)S(1)}, u32[]{:S(2)}, u32[]{:S(2)}) %collective-permute-start.16) | collective-permute-done | bytes 589856 | tf_op jit(solution)/shard_map/ppermute | solution.py:32
  120.4 6.3 %collective-permute-done.15.refs_4_ = bf16[288,1024]{1,0:T(8,128)(2,1)S(1)} collective-permute-done((bf16[288,1024]{1,0:T(8,128)(2,1)S(1)}, bf16[288,1024]{1,0:T(8,128)(2,1)S(1)}, u32[]{:S(2)}, u32[]{:S(2)}) %collective-permute-start.15) | collective-permute-done | bytes 589856 | tf_op jit(solution)/shard_map/ppermute | solution.py:32
  126.7 1.0 shard_map.83
  127.8 0.8 collective-permute-start.17
  128.5 1.4 %collective-permute-start.18 = (bf16[144,1024]{1,0:T(8,128)(2,1)S(1)}, bf16[144,1024]{1,0:T(8,128)(2,1)S(1)}, u32[]{:S(2)}, u32[]{:S(2)}) collective-permute-start(bf16[144,1024]{1,0:T(8,128)(2,1)S(1)} %get-tuple-element.22), channel_id=1, source_target_pairs={{0,3},{1,2},{2,1},{3,0},{4,7},{5,6},{6,5},{7,4},{8,11},{9,10},{10,... | collective-permute-start | bytes 884744 | tf_op jit(solution)/shard_map/ppermute | solution.py:32
  129.9 2.0 %collective-permute-start.19 = (bf16[144,1024]{1,0:T(8,128)(2,1)S(1)}, bf16[144,1024]{1,0:T(8,128)(2,1)S(1)}, u32[]{:S(2)}, u32[]{:S(2)}) collective-permute-start(bf16[144,1024]{1,0:T(8,128)(2,1)S(1)} %get-tuple-element.23), channel_id=1, source_target_pairs={{0,2},{1,3},{2,0},{3,1},{4,6},{5,7},{6,4},{7,5},{8,10},{9,11},{10,... | collective-permute-start | bytes 884744 | tf_op jit(solution)/shard_map/ppermute | solution.py:32
  131.9 2.6 %collective-permute-done.17.refs_1_ = bf16[144,1024]{1,0:T(8,128)(2,1)S(1)} collective-permute-done((bf16[144,1024]{1,0:T(8,128)(2,1)S(1)}, bf16[144,1024]{1,0:T(8,128)(2,1)S(1)}, u32[]{:S(2)}, u32[]{:S(2)}) %collective-permute-start.17) | collective-permute-done | bytes 294944 | tf_op jit(solution)/shard_map/ppermute | solution.py:32
  134.6 5.1 %collective-permute-done.18.refs_2_ = bf16[144,1024]{1,0:T(8,128)(2,1)S(1)} collective-permute-done((bf16[144,1024]{1,0:T(8,128)(2,1)S(1)}, bf16[144,1024]{1,0:T(8,128)(2,1)S(1)}, u32[]{:S(2)}, u32[]{:S(2)}) %collective-permute-start.18) | collective-permute-done | bytes 294944 | tf_op jit(solution)/shard_map/ppermute | solution.py:32
  139.6 0.9 shard_map.84
  (52 shorter events, 6.8 us)
Async XLA Ops:
  0.6 6.9 %copy-start = (bf16[2304,512]{1,0:T(8,128)(2,1)S(1)}, bf16[2304,512]{1,0:T(8,128)(2,1)}, u32[]{:S(2)}) copy-start(bf16[2304,512]{1,0:T(8,128)(2,1)} %param.8) | copy-start | bytes 7077892
  0.7 1.1 copy-start.2
  1.8 13.5 %collective-permute-start = (bf16[144,1024]{1,0:T(8,128)(2,1)S(1)}, bf16[144,1024]{1,0:T(8,128)(2,1)S(1)}, u32[]{:S(2)}, u32[]{:S(2)}) collective-permute-start(bf16[144,1024]{1,0:T(8,128)(2,1)S(1)} %shard_map.77.refs_0_), channel_id=1, source_target_pairs={{0,1},{1,0},{2,3},{3,2},{4,5},{5,4},{6,7},{7,6},{8,9},{9,8},{10,11... | collective-permute-start | bytes 884744 | tf_op jit(solution)/shard_map/ppermute | solution.py:32
  3.9 11.4 %collective-permute-start.1 = (bf16[144,1024]{1,0:T(8,128)(2,1)S(1)}, bf16[144,1024]{1,0:T(8,128)(2,1)S(1)}, u32[]{:S(2)}, u32[]{:S(2)}) collective-permute-start(bf16[144,1024]{1,0:T(8,128)(2,1)S(1)} %shard_map.77.refs_0_), channel_id=1, source_target_pairs={{0,3},{1,2},{2,1},{3,0},{4,7},{5,6},{6,5},{7,4},{8,11},{9,10},{10,... | collective-permute-start | bytes 884744 | tf_op jit(solution)/shard_map/ppermute | solution.py:32
  6.4 8.9 %collective-permute-start.2 = (bf16[144,1024]{1,0:T(8,128)(2,1)S(1)}, bf16[144,1024]{1,0:T(8,128)(2,1)S(1)}, u32[]{:S(2)}, u32[]{:S(2)}) collective-permute-start(bf16[144,1024]{1,0:T(8,128)(2,1)S(1)} %shard_map.77.refs_0_), channel_id=1, source_target_pairs={{0,2},{1,3},{2,0},{3,1},{4,6},{5,7},{6,4},{7,5},{8,10},{9,11},{10,... | collective-permute-start | bytes 884744 | tf_op jit(solution)/shard_map/ppermute | solution.py:32
  16.1 12.8 %collective-permute-start.3 = (bf16[288,1024]{1,0:T(8,128)(2,1)S(1)}, bf16[288,1024]{1,0:T(8,128)(2,1)S(1)}, u32[]{:S(2)}, u32[]{:S(2)}) collective-permute-start(bf16[288,1024]{1,0:T(8,128)(2,1)S(1)} %get-tuple-element.17), channel_id=1, source_target_pairs={{0,4},{1,5},{2,6},{3,7},{4,0},{5,1},{6,2},{7,3},{8,12},{9,13},{10,... | collective-permute-start | bytes 1769480 | tf_op jit(solution)/shard_map/ppermute | solution.py:32
  17.7 11.1 %collective-permute-start.4 = (bf16[288,1024]{1,0:T(8,128)(2,1)S(1)}, bf16[288,1024]{1,0:T(8,128)(2,1)S(1)}, u32[]{:S(2)}, u32[]{:S(2)}) collective-permute-start(bf16[288,1024]{1,0:T(8,128)(2,1)S(1)} %get-tuple-element.16), channel_id=1, source_target_pairs={{0,12},{1,13},{2,14},{3,15},{4,8},{5,9},{6,10},{7,11},{8,4},{9,5},... | collective-permute-start | bytes 1769480 | tf_op jit(solution)/shard_map/ppermute | solution.py:32
  22.5 11.1 %collective-permute-start.5 = (bf16[288,1024]{1,0:T(8,128)(2,1)S(1)}, bf16[288,1024]{1,0:T(8,128)(2,1)S(1)}, u32[]{:S(2)}, u32[]{:S(2)}) collective-permute-start(bf16[288,1024]{1,0:T(8,128)(2,1)S(1)} %get-tuple-element.16), channel_id=1, source_target_pairs={{0,4},{1,5},{2,6},{3,7},{4,0},{5,1},{6,2},{7,3},{8,12},{9,13},{10,... | collective-permute-start | bytes 1769480 | tf_op jit(solution)/shard_map/ppermute | solution.py:32
  23.2 11.9 %collective-permute-start.6 = (bf16[288,1024]{1,0:T(8,128)(2,1)S(1)}, bf16[288,1024]{1,0:T(8,128)(2,1)S(1)}, u32[]{:S(2)}, u32[]{:S(2)}) collective-permute-start(bf16[288,1024]{1,0:T(8,128)(2,1)S(1)} %get-tuple-element.17), channel_id=1, source_target_pairs={{0,12},{1,13},{2,14},{3,15},{4,8},{5,9},{6,10},{7,11},{8,4},{9,5},... | collective-permute-start | bytes 1769480 | tf_op jit(solution)/shard_map/ppermute | solution.py:32
  28.8 9.9 %collective-permute-start.7 = (bf16[288,1024]{1,0:T(8,128)(2,1)S(1)}, bf16[288,1024]{1,0:T(8,128)(2,1)S(1)}, u32[]{:S(2)}, u32[]{:S(2)}) collective-permute-start(bf16[288,1024]{1,0:T(8,128)(2,1)S(1)} %collective-permute-done.4), channel_id=1, source_target_pairs={{0,4},{1,5},{2,6},{3,7},{4,0},{5,1},{6,2},{7,3},{8,12},{9,13},{10,... | collective-permute-start | bytes 1769480 | tf_op jit(solution)/shard_map/ppermute | solution.py:32
  28.8 12.6 %collective-permute-start.8 = (bf16[288,1024]{1,0:T(8,128)(2,1)S(1)}, bf16[288,1024]{1,0:T(8,128)(2,1)S(1)}, u32[]{:S(2)}, u32[]{:S(2)}) collective-permute-start(bf16[288,1024]{1,0:T(8,128)(2,1)S(1)} %collective-permute-done.3), channel_id=1, source_target_pairs={{0,12},{1,13},{2,14},{3,15},{4,8},{5,9},{6,10},{7,11},{8,4},{9,5},... | collective-permute-start | bytes 1769480 | tf_op jit(solution)/shard_map/ppermute | solution.py:32
  43.2 2.7 %collective-permute-start.9 = (bf16[512,896]{1,0:T(8,128)(2,1)S(1)}, bf16[512,896]{1,0:T(8,128)(2,1)S(1)}, u32[]{:S(2)}, u32[]{:S(2)}) collective-permute-start(bf16[512,896]{1,0:T(8,128)(2,1)S(1)} %shard_map.81), channel_id=1, source_target_pairs={{0,16},{16,0},{1,17},{17,1},{2,18},{18,2},{3,19},{19,3},{4,20},{20... | collective-permute-start | bytes 2752520 | tf_op jit(solution)/shard_map/ppermute | solution.py:36
  72.9 4.4 %copy-start.4 = (bf16[8,512]{1,0:T(8,128)(2,1)}, bf16[8,512]{1,0:T(8,128)(2,1)S(1)}, u32[]{:S(2)}) copy-start(bf16[8,512]{1,0:T(8,128)(2,1)S(1)} %reshape.56) | copy-start | bytes 24580
  73.0 4.2 %copy-start.5 = (bf16[8,1024,256]{2,1,0:T(8,128)(2,1)S(1)}, bf16[8,1024,256]{2,1,0:T(8,128)(2,1)}, u32[]{:S(2)}) copy-start(bf16[8,1024,256]{2,1,0:T(8,128)(2,1)} %param.11) | copy-start | bytes 12582916
  79.3 19.6 %all-to-all-start.1 = ((bf16[64,8,768]{2,1,0:T(8,128)(2,1)}), bf16[64,8,768]{2,1,0:T(8,128)(2,1)S(1)}, u32[]{:S(2)}, u32[]{:S(2)}) async-start(bf16[64,8,768]{2,1,0:T(8,128)(2,1)} %bitcast.21), calls=%async_computation.1 | async-start | bytes 1572864 | tf_op jit(solution)/shard_map/all_to_all | solution.py:240
  98.8 2.3 %collective-permute-start.10 = (bf16[512,768]{1,0:T(8,128)(2,1)S(1)}, bf16[512,768]{1,0:T(8,128)(2,1)S(1)}, u32[]{:S(2)}, u32[]{:S(2)}) collective-permute-start(bf16[512,768]{1,0:T(8,128)(2,1)S(1)} %bitcast.57), channel_id=1, source_target_pairs={{0,16},{16,0},{1,17},{17,1},{2,18},{18,2},{3,19},{19,3},{4,20},{20... | collective-permute-start | bytes 2359304 | tf_op jit(solution)/shard_map/ppermute | solution.py:36
  98.8 4.6 %copy-start.3 = (bf16[4,4,144,768]{3,2,1,0:T(8,128)(2,1)S(1)}, bf16[4,4,144,768]{3,2,1,0:T(8,128)(2,1)}, u32[]{:S(2)}) copy-start(bf16[4,4,144,768]{3,2,1,0:T(8,128)(2,1)} %bitcast_select_fusion.1) | copy-start | bytes 10616836
  102.9 11.2 %collective-permute-start.14 = (bf16[288,1024]{1,0:T(8,128)(2,1)S(1)}, bf16[288,1024]{1,0:T(8,128)(2,1)S(1)}, u32[]{:S(2)}, u32[]{:S(2)}) collective-permute-start(bf16[288,1024]{1,0:T(8,128)(2,1)S(1)} %convolution_convert_fusion.1), channel_id=1, source_target_pairs={{0,12},{1,13},{2,14},{3,15},{4,8},{5,9},{6,10},{7,11},{8,4},{9,5},... | collective-permute-start | bytes 1769480 | tf_op jit(solution)/shard_map/ppermute | solution.py:32
  104.1 10.8 %collective-permute-start.12 = (bf16[288,1024]{1,0:T(8,128)(2,1)S(1)}, bf16[288,1024]{1,0:T(8,128)(2,1)S(1)}, u32[]{:S(2)}, u32[]{:S(2)}) collective-permute-start(bf16[288,1024]{1,0:T(8,128)(2,1)S(1)} %convolution_convert_fusion.3), channel_id=1, source_target_pairs={{0,4},{1,5},{2,6},{3,7},{4,0},{5,1},{6,2},{7,3},{8,12},{9,13},{10,... | collective-permute-start | bytes 1769480 | tf_op jit(solution)/shard_map/ppermute | solution.py:32
  104.9 15.5 %collective-permute-start.16 = (bf16[288,1024]{1,0:T(8,128)(2,1)S(1)}, bf16[288,1024]{1,0:T(8,128)(2,1)S(1)}, u32[]{:S(2)}, u32[]{:S(2)}) collective-permute-start(bf16[288,1024]{1,0:T(8,128)(2,1)S(1)} %convolution_convert_fusion), channel_id=1, source_target_pairs={{0,12},{1,13},{2,14},{3,15},{4,8},{5,9},{6,10},{7,11},{8,4},{9,5},... | collective-permute-start | bytes 1769480 | tf_op jit(solution)/shard_map/ppermute | solution.py:32
  108.4 12.0 %collective-permute-start.11 = (bf16[288,1024]{1,0:T(8,128)(2,1)S(1)}, bf16[288,1024]{1,0:T(8,128)(2,1)S(1)}, u32[]{:S(2)}, u32[]{:S(2)}) collective-permute-start(bf16[288,1024]{1,0:T(8,128)(2,1)S(1)} %convolution_convert_fusion.4), channel_id=1, source_target_pairs={{0,4},{1,5},{2,6},{3,7},{4,0},{5,1},{6,2},{7,3},{8,12},{9,13},{10,... | collective-permute-start | bytes 1769480 | tf_op jit(solution)/shard_map/ppermute | solution.py:32
  114.7 11.9 %collective-permute-start.15 = (bf16[288,1024]{1,0:T(8,128)(2,1)S(1)}, bf16[288,1024]{1,0:T(8,128)(2,1)S(1)}, u32[]{:S(2)}, u32[]{:S(2)}) collective-permute-start(bf16[288,1024]{1,0:T(8,128)(2,1)S(1)} %fusion.4), channel_id=1, source_target_pairs={{0,4},{1,5},{2,6},{3,7},{4,0},{5,1},{6,2},{7,3},{8,12},{9,13},{10,... | collective-permute-start | bytes 1769480 | tf_op jit(solution)/shard_map/ppermute | solution.py:32
  115.5 11.2 %collective-permute-start.13 = (bf16[288,1024]{1,0:T(8,128)(2,1)S(1)}, bf16[288,1024]{1,0:T(8,128)(2,1)S(1)}, u32[]{:S(2)}, u32[]{:S(2)}) collective-permute-start(bf16[288,1024]{1,0:T(8,128)(2,1)S(1)} %fusion.3), channel_id=1, source_target_pairs={{0,12},{1,13},{2,14},{3,15},{4,8},{5,9},{6,10},{7,11},{8,4},{9,5},... | collective-permute-start | bytes 1769480 | tf_op jit(solution)/shard_map/ppermute | solution.py:32
  117.6 23.0 %copy-start.1 = (bf16[2304,512]{1,0:T(8,128)(2,1)S(1)}, bf16[2304,512]{1,0:T(8,128)(2,1)}, u32[]{:S(2)}) copy-start(bf16[2304,512]{1,0:T(8,128)(2,1)} %param.8) | copy-start | bytes 7077892
  127.8 6.8 %collective-permute-start.17 = (bf16[144,1024]{1,0:T(8,128)(2,1)S(1)}, bf16[144,1024]{1,0:T(8,128)(2,1)S(1)}, u32[]{:S(2)}, u32[]{:S(2)}) collective-permute-start(bf16[144,1024]{1,0:T(8,128)(2,1)S(1)} %get-tuple-element.21), channel_id=1, source_target_pairs={{0,1},{1,0},{2,3},{3,2},{4,5},{5,4},{6,7},{7,6},{8,9},{9,8},{10,11... | collective-permute-start | bytes 884744 | tf_op jit(solution)/shard_map/ppermute | solution.py:32
  128.5 11.1 %collective-permute-start.18 = (bf16[144,1024]{1,0:T(8,128)(2,1)S(1)}, bf16[144,1024]{1,0:T(8,128)(2,1)S(1)}, u32[]{:S(2)}, u32[]{:S(2)}) collective-permute-start(bf16[144,1024]{1,0:T(8,128)(2,1)S(1)} %get-tuple-element.22), channel_id=1, source_target_pairs={{0,3},{1,2},{2,1},{3,0},{4,7},{5,6},{6,5},{7,4},{8,11},{9,10},{10,... | collective-permute-start | bytes 884744 | tf_op jit(solution)/shard_map/ppermute | solution.py:32
  129.9 9.7 %collective-permute-start.19 = (bf16[144,1024]{1,0:T(8,128)(2,1)S(1)}, bf16[144,1024]{1,0:T(8,128)(2,1)S(1)}, u32[]{:S(2)}, u32[]{:S(2)}) collective-permute-start(bf16[144,1024]{1,0:T(8,128)(2,1)S(1)} %get-tuple-element.23), channel_id=1, source_target_pairs={{0,2},{1,3},{2,0},{3,1},{4,6},{5,7},{6,4},{7,5},{8,10},{9,11},{10,... | collective-permute-start | bytes 884744 | tf_op jit(solution)/shard_map/ppermute | solution.py:32

commit v5 on v4

--- a/solution.py
+++ b/solution.py
@@ -36,7 +36,7 @@
     return lax.ppermute(v, "c", [(0, 1), (1, 0)])
 
 
-MASKS = (1, 3, 2)
+MASKS = (2, 1, 3)
 SMEM = pl.BlockSpec(memory_space=pltpu.SMEM)
 VMEM = pl.BlockSpec(memory_space=pltpu.VMEM)
 
@@ -51,20 +51,6 @@
 
 def lanes(i):
     return pl.ds(pl.multiple_of(i * 128, 128), 128)
-
-
-def split_kernel(c_ref, t_ref, out_ref):
-    c = c_ref[0]
-    for x in range(4):
-        out_ref[:, x * 128 : (x + 1) * 128] = t_ref[:, lanes(2 * x + 1 - c)]
-        out_ref[:, (x + 4) * 128 : (x + 5) * 128] = t_ref[:, lanes(2 * x + c)]
-
-
-def split_cores(c, t):
-    return pl.pallas_call(
-        split_kernel,
-        compiler_params=few(2), in_specs=[SMEM, VMEM], out_specs=VMEM, out_shape=jax.ShapeDtypeStruct(t.shape, t.dtype)
-    )(c.reshape(1), t)
 
 
 def merge_kernel(c_ref, *refs):
@@ -84,6 +70,34 @@
     )(c.reshape(1), *terms)
 
 
+def add_products_kernel(at_ref, part_ref, *refs):
+    *pieces, w_ref, out_ref = refs
+    m, n = out_ref.shape
+    k = pieces[0].shape[0]
+    step = part_ref.shape[0] // m
+    for i in range(0, m // 128, 2):
+        blocks = [lanes(step * (i + d) + at_ref[0]) for d in range(2)]
+        turned = [jnp.concatenate([piece[:, b].T for b in blocks], 0) for piece in pieces]
+        for j in range(0, n, 256):
+            to = slice(j, min(j + 256, n))
+            total = jnp.concatenate([part_ref[b, to] for b in blocks], 0)
+            for p, piece in enumerate(turned):
+                w = w_ref[pl.ds(pl.multiple_of(at_ref[1 + p], 16), k), to]
+                total += jnp.dot(piece, w, preferred_element_type=F32)
+            out_ref[i * 128 : (i + 2) * 128, to] = total.astype(out_ref.dtype)
+
+
+def add_products(side, starts, part, pieces, w, rows, dtype=F32):
+    return pl.pallas_call(
+        add_products_kernel,
+        compiler_params=few(16),
+        in_specs=[SMEM] + [VMEM] * (2 + len(pieces)),
+        out_specs=VMEM,
+        out_shape=jax.ShapeDtypeStruct((rows, part.shape[1]), dtype),
+        cost_estimate=pl.CostEstimate(flops=0, bytes_accessed=0, transcendentals=0),
+    )(jnp.stack([side, *starts]), part, *pieces, w)
+
+
 def join_kernel(a_ref, b_ref, out_ref):
     out_ref[: a_ref.shape[0], :] = a_ref[...]
     out_ref[a_ref.shape[0] :, :] = b_ref[...]
@@ -97,33 +111,6 @@
         out_specs=VMEM,
         out_shape=jax.ShapeDtypeStruct((2 * a.shape[0], a.shape[1]), a.dtype),
     )(a, b)
-
-
-def add_products_kernel(side, at_ref, part_ref, *refs):
-    *pieces, w_ref, out_ref = refs
-    m, n = out_ref.shape
-    k = pieces[0].shape[0]
-    for i in range(0, m, 256):
-        at = slice(side * m + i, side * m + i + 256)
-        turned = [piece[:, at].T for piece in pieces]
-        for j in range(0, n, 256):
-            to = slice(j, min(j + 256, n))
-            total = part_ref[i : i + 256, to] if part_ref.shape[0] == m else part_ref[at, to]
-            for p, piece in enumerate(turned):
-                w = w_ref[pl.ds(pl.multiple_of(at_ref[p], 16), k), to]
-                total += jnp.dot(piece, w, preferred_element_type=F32)
-            out_ref[i : i + 256, to] = total.astype(out_ref.dtype)
-
-
-def add_products(starts, part, pieces, w, rows, side=0, dtype=F32):
-    return pl.pallas_call(
-        functools.partial(add_products_kernel, side),
-        compiler_params=few(16),
-        in_specs=[SMEM] + [VMEM] * (2 + len(pieces)),
-        out_specs=VMEM,
-        out_shape=jax.ShapeDtypeStruct((rows, part.shape[1]), dtype),
-        cost_estimate=pl.CostEstimate(flops=0, bytes_accessed=0, transcendentals=0),
-    )(jnp.stack(starts), part, *pieces, w)
 
 
 def in_halves(i, n, use):
@@ -187,9 +174,9 @@
 
     y, z = lax.axis_index("y"), lax.axis_index("z")
     first, second = jnp.where(c == 0, z, y), jnp.where(c == 0, y, z)
-    firsts, seconds = [first ^ m for m in (0, *MASKS)], [second ^ m for m in (0, *MASKS)]
-
-    t = split_cores(c, tokens.T)
+    firsts, seconds = [first ^ m for m in (0, *MASKS)], [second ^ m for m in (0, 1, 3, 2)]
+
+    t = tokens.T
     low, high = assemble(firsts, t, *[exchange(t, 0, m) for m in MASKS])
     half = low.shape[0]
     def by_blocks(w):
@@ -211,10 +198,11 @@
     low2, high2 = exchange(low3, 1, 1), exchange(high1, 1, 3)
     part = part + product(high1, seconds[1], half) + product(low3, seconds[2])
     starts = [seconds[1] * 2 * half, seconds[2] * 2 * half + half, seconds[3] * 2 * half, seconds[3] * 2 * half + half]
-    part = add_products(starts[:2], part, (low1, high3), w_all, 1024)
+    none = jnp.zeros_like(c)
+    part = add_products(none, starts[:2], part, (low1, high3), w_all, 1024)
     last = low2, high2
-    given = core_swap(add_products(starts[2:], part, last, w_all, 512, 0, BF16))
-    part = add_products(starts[2:], part, last, w_all, 512, 1)
+    given = core_swap(add_products(1 - c, starts[2:], part, last, w_all, 512, BF16))
+    part = add_products(c, starts[2:], part, last, w_all, 512)
     part = (part + given.astype(F32)).astype(BF16)
     part = lax.all_to_all(part.reshape(64, rows_dev, -1), ("x", "y", "z"), 0, 0, tiled=True)
     whole = jnp.sum(part.astype(F32).reshape(4, 16, rows_dev, -1), axis=0).astype(BF16)
@@ -239,9 +227,10 @@
     spread = jnp.broadcast_to(attended[None], (4, 16, rows_dev, q_cols)).reshape(64, rows_dev, q_cols)
     mine = lax.all_to_all(spread, ("x", "y", "z"), 0, 0, tiled=True).reshape(512, q_cols)
     mine, w_out = lax.optimization_barrier((mine, w_out))
-    rows = join(core_swap(mine), mine)
-
-    def outward(i, skip):
+    theirs = core_swap(mine)
+    rows = join(theirs, mine)
+
+    def outward(i, skip, rows=rows):
         w = lax.dynamic_slice_in_dim(w_out, i * 4 * feat + skip, half, 0)
         return lax.dot_general(w, rows, (((1,), (1,)), ((), ())), preferred_element_type=F32)
 

time: 141 us -> 139 us (0.986)
    pallas_call x4 -> x3, Pallas kernels: 6.44 us -> 6.39 us  [add_products(): pl.pallas_call(add_products_kernel, compiler_params=few(16), in_specs=[SM...]
  transfers between devices with their start and end apart: 21 -> 21, of which waited for: 13 -> 15; matrix products, arithmetic and copies ran while one was open for 20% -> 21% of each run, Pallas kernels for 3% -> 3%
where the time goes in v5:
time: 139 us
  waiting for transfers between devices  36.3 us (26%)
  starting transfers between devices  28.9 us (21%)
  blocking collectives  26.7 us (19%)
  matrix products  16.1 us (12%)
  other arithmetic  13.6 us (10%)
  Pallas kernels  9.15 us (7%)
  local copies, waits for them, and re-layouts  7.38 us (5%)
    ppermute x18, waiting for transfers between devices, exchange(): return lax.ppermute(v, AXES, partner_pairs(phase, mask))  29.6 us
    all_to_all x1, blocking collectives, shards(): lax.all_to_all(part.reshape(64, rows_dev, -1), ('x', 'y', 'z'), 0, 0, til...  26.7 us
    ppermute x18, starting transfers between devices, exchange(): return lax.ppermute(v, AXES, partner_pairs(phase, mask))  23.8 us
    select_n x2, other arithmetic, by_blocks(): return jnp.where(c == 0, w, w.swapaxes(0, 1)).reshape(16 * feat, -1)  9.08 us
    pallas_call x3, Pallas kernels, add_products(): pl.pallas_call(add_products_kernel, compiler_params=few(16), in_specs=[SM...  6.39 us
    dot_general x8, matrix products, outward(): lax.dot_general(w, rows, (((1,), (1,)), ((), ())), preferred_element_type...  6.24 us
    unnamed x13, local copies, waits for them, and re-layouts  5.8 us
    dot_general x4, matrix products, product(): lax.dot_general(v, w, (((0,), (0,)), ((), ())), preferred_element_type=F32)  5.06 us
  transfers between devices with their start and end apart: 21, of which 15 were waited for; matrix products, arithmetic and copies ran while one was open for 21% of the time, Pallas kernels for 3%

profile of v5, /device:TPU:0, one launch (start us, length us, event | category | flops | bytes accessed | tf_op | source)
XLA Modules:
  0.0 139.0 jit_solution(2385502626823684576)
XLA Ops:
  0.6 4.0 %collective-permute-start = (bf16[144,1024]{1,0:T(8,128)(2,1)}, bf16[144,1024]{1,0:T(8,128)(2,1)S(1)}, u32[]{:S(2)}, u32[]{:S(2)}) collective-permute-start(bf16[144,1024]{1,0:T(8,128)(2,1)} %bitcast.60), channel_id=1, source_target_pairs={{0,2},{1,3},{2,0},{3,1},{4,6},{5,7},{6,4},{7,5},{8,10},{9,11},{10,... | collective-permute-start | bytes 884744 | tf_op jit(solution)/shard_map/ppermute | solution.py:32
  4.7 1.0 collective-permute-start.1
  5.9 3.6 %fusion.1 = bf16[2304,896]{1,0:T(8,128)(2,1)} fusion(bf16[2304,32]{1,0:T(8,128)(2,1)S(1)} %constant_dynamic-slice_fusion, bf16[2304,768]{1,0:T(8,128)(2,1)} %param.7), kind=kLoop, calls=%fused_computation.2 | loop fusion | flops 12386304 | bytes 7815168 | tf_op jit(solution)/shard_map/concatenate | solution.py:187
  9.7 3.9 %bitcast_select_fusion = bf16[4,4,144,896]{3,2,1,0:T(8,128)(2,1)S(1)} fusion(bf16[4,4,144,896]{3,2,1,0:T(8,128)(2,1)} %bitcast.64, pred[]{:T(512)S(6)} %eq.2), kind=kLoop, calls=%fused_computation.3 | loop fusion | flops 2064384 | bytes 8257537 | tf_op jit(solution)/shard_map/jit(_where)/select_n | solution.py:184
  13.9 0.7 shard_map.77
  14.5 1.7 %collective-permute-start.3 = (bf16[288,1024]{1,0:T(8,128)(2,1)S(1)}, bf16[288,1024]{1,0:T(8,128)(2,1)S(1)}, u32[]{:S(2)}, u32[]{:S(2)}) collective-permute-start(bf16[288,1024]{1,0:T(8,128)(2,1)S(1)} %get-tuple-element.17), channel_id=1, source_target_pairs={{0,4},{1,5},{2,6},{3,7},{4,0},{5,1},{6,2},{7,3},{8,12},{9,13},{10,... | collective-permute-start | bytes 1769480 | tf_op jit(solution)/shard_map/ppermute | solution.py:32
  16.2 2.2 %collective-permute-start.4 = (bf16[288,1024]{1,0:T(8,128)(2,1)S(1)}, bf16[288,1024]{1,0:T(8,128)(2,1)S(1)}, u32[]{:S(2)}, u32[]{:S(2)}) collective-permute-start(bf16[288,1024]{1,0:T(8,128)(2,1)S(1)} %get-tuple-element.16), channel_id=1, source_target_pairs={{0,12},{1,13},{2,14},{3,15},{4,8},{5,9},{6,10},{7,11},{8,4},{9,5},... | collective-permute-start | bytes 1769480 | tf_op jit(solution)/shard_map/ppermute | solution.py:32
  18.4 1.2 fusion.15
  19.6 1.3 convolution_add_fusion
  20.9 0.8 collective-permute-start.5
  22.3 5.0 %collective-permute-done.4 = bf16[288,1024]{1,0:T(8,128)(2,1)S(1)} collective-permute-done((bf16[288,1024]{1,0:T(8,128)(2,1)S(1)}, bf16[288,1024]{1,0:T(8,128)(2,1)S(1)}, u32[]{:S(2)}, u32[]{:S(2)}) %collective-permute-start.4) | collective-permute-done | bytes 589856 | tf_op jit(solution)/shard_map/ppermute | solution.py:32
  27.3 2.3 %collective-permute-start.8 = (bf16[288,1024]{1,0:T(8,128)(2,1)S(1)}, bf16[288,1024]{1,0:T(8,128)(2,1)S(1)}, u32[]{:S(2)}, u32[]{:S(2)}) collective-permute-start(bf16[288,1024]{1,0:T(8,128)(2,1)S(1)} %collective-permute-done.3), channel_id=1, source_target_pairs={{0,12},{1,13},{2,14},{3,15},{4,8},{5,9},{6,10},{7,11},{8,4},{9,5},... | collective-permute-start | bytes 1769480 | tf_op jit(solution)/shard_map/ppermute | solution.py:32
  29.6 1.2 fusion.13
  30.8 1.3 add_add_fusion.part_ref
  32.1 1.5 %collective-permute-done.6.refs_1_ = bf16[288,1024]{1,0:T(8,128)(2,1)S(1)} collective-permute-done((bf16[288,1024]{1,0:T(8,128)(2,1)S(1)}, bf16[288,1024]{1,0:T(8,128)(2,1)S(1)}, u32[]{:S(2)}, u32[]{:S(2)}) %collective-permute-start.6) | collective-permute-done | bytes 589856 | tf_op jit(solution)/shard_map/ppermute | solution.py:32
  33.6 2.8 %shard_map.78.part_ref = f32[1024,896]{1,0:T(8,128)S(1)} custom-call(s32[3]{0:T(128)S(1)} %get-tuple-element.30.at_ref, f32[1024,896]{1,0:T(8,128)S(1)} %add_add_fusion.part_ref, bf16[288,1024]{1,0:T(8,128)(2,1)S(1)} %collective-permute-done.5.refs_0_, bf16[288,1024]{1,0:T(8,128)(2,1)S(1)} %collective-permute-done.6.refs_1_, bf16[2304,896]{1,0:T(8,128)(2,1)S(1)} %bitcast.55), custom_call_target="tpu_custom_call" | custom-call | tf_op jit(solution)/shard_map/pallas_call | solution.py:91
  36.4 0.8 collective-permute-done.7.refs_0_
  37.2 2.7 %collective-permute-done.8.refs_1_ = bf16[288,1024]{1,0:T(8,128)(2,1)S(1)} collective-permute-done((bf16[288,1024]{1,0:T(8,128)(2,1)S(1)}, bf16[288,1024]{1,0:T(8,128)(2,1)S(1)}, u32[]{:S(2)}, u32[]{:S(2)}) %collective-permute-start.8) | collective-permute-done | bytes 589856 | tf_op jit(solution)/shard_map/ppermute | solution.py:32
  39.9 1.8 %shard_map.80 = bf16[512,896]{1,0:T(8,128)(2,1)S(1)} custom-call(s32[3]{0:T(128)S(1)} %get-tuple-element.31.at_ref, f32[1024,896]{1,0:T(8,128)S(1)} %shard_map.78.part_ref, bf16[288,1024]{1,0:T(8,128)(2,1)S(1)} %collective-permute-done.7.refs_0_, bf16[288,1024]{1,0:T(8,128)(2,1)S(1)} %collective-permute-done.8.refs_1_, bf16[2304,896]{1,0:T(8,128)(2,1)S(1)} %bitcast.56), custom_call_target="tpu_custom_call" | custom-call | tf_op jit(solution)/shard_map/pallas_call | solution.py:91
  42.1 1.8 %shard_map.79 = f32[512,896]{1,0:T(8,128)S(1)} custom-call(s32[3]{0:T(128)S(1)} %add_add_fusion.1.at_ref, f32[1024,896]{1,0:T(8,128)S(1)} %shard_map.78.part_ref, bf16[288,1024]{1,0:T(8,128)(2,1)S(1)} %collective-permute-done.7.refs_0_, bf16[288,1024]{1,0:T(8,128)(2,1)S(1)} %collective-permute-done.8.refs_1_, bf16[2304,896]{1,0:T(8,128)(2,1)S(1)} %bitcast.57), custom_call_target="tpu_custom_call" | custom-call | tf_op jit(solution)/shard_map/pallas_call | solution.py:91
  44.6 26.7 %all_to_all.10 = bf16[64,8,896]{2,1,0:T(8,128)(2,1)S(1)} all-to-all(bf16[64,8,896]{2,1,0:T(8,128)(2,1)S(1)} %fusion.6), channel_id=1, replica_groups=mesh['x'=4,'c'=2,'y'=4,'z'=4] {'x','y','z'}, dimensions={0} | all-to-all | bytes 1835008 | tf_op jit(solution)/shard_map/all_to_all | solution.py:207
  71.9 3.8 %fusion.42 = (f32[8,48]{1,0:T(8,128)S(1)}, f32[8,48,1024]{2,1,0:T(8,128)S(1)}) fusion(bf16[8,48,256]{2,1,0:T(8,128)(2,1)S(1)} %reshape.54, bf16[8,1024,256]{2,1,0:T(8,128)(2,1)} %param.10), kind=kOutput, calls=%fused_computation.70 | convolution fusion | flops 202112640 | bytes 5965312 | tf_op jit(solution)/shard_map/bhe,bte->bht/dot_general | solution.py:215
  76.1 0.9 fusion.5
  77.2 0.9 broadcast_in_dim.2
  78.1 4.8 %all-to-all-start.1 = ((bf16[64,8,768]{2,1,0:T(8,128)(2,1)}), bf16[64,8,768]{2,1,0:T(8,128)(2,1)S(1)}, u32[]{:S(2)}, u32[]{:S(2)}) async-start(bf16[64,8,768]{2,1,0:T(8,128)(2,1)} %bitcast.22), calls=%async_computation.1 | async-start | bytes 1572864 | tf_op jit(solution)/shard_map/all_to_all | solution.py:228
  82.9 5.8 %copy.24 = bf16[768,2304]{0,1:T(8,128)(2,1)} copy(bf16[768,2304]{1,0:T(8,128)(2,1)} %param.9) | data formatting | bytes 7077888 | tf_op args[3]
  88.7 5.2 %bitcast_select_fusion.1 = bf16[4,4,144,768]{3,2,1,0:T(8,128)(2,1)} fusion(bf16[4,4,144,768]{3,2,1,0:T(8,128)(2,1)} %bitcast.65, pred[]{:T(512)S(6)} %eq.2), kind=kLoop, calls=%fused_computation.5 | loop fusion | flops 1769472 | bytes 7077889 | tf_op jit(solution)/shard_map/jit(_where)/select_n | solution.py:184
  93.8 3.8 %all-to-all-done.1 = bf16[64,8,768]{2,1,0:T(8,128)(2,1)S(1)} async-done(((bf16[64,8,768]{2,1,0:T(8,128)(2,1)}), bf16[64,8,768]{2,1,0:T(8,128)(2,1)S(1)}, u32[]{:S(2)}, u32[]{:S(2)}) %all-to-all-start.1) | async-done | bytes 786464 | tf_op jit(solution)/shard_map/all_to_all | solution.py:228
  97.7 2.3 %collective-permute-done.10.a_ref = bf16[512,768]{1,0:T(8,128)(2,1)S(1)} collective-permute-done((bf16[512,768]{1,0:T(8,128)(2,1)S(1)}, bf16[512,768]{1,0:T(8,128)(2,1)S(1)}, u32[]{:S(2)}, u32[]{:S(2)}) %collective-permute-start.10) | collective-permute-done | bytes 786464 | tf_op jit(solution)/shard_map/ppermute | solution.py:36
  100.1 1.7 %convolution_convert_fusion.1 = bf16[288,1024]{1,0:T(8,128)(2,1)S(1)} fusion(bf16[1024,768]{1,0:T(8,128)(2,1)S(1)} %shard_map.81, bf16[2304,768]{1,0:T(8,128)(2,1)} %bitcast.67, s32[]{:T(128)S(6)} %select_n.67), kind=kOutput, calls=%fused_computation.15 | convolution fusion | flops 453279744 | bytes 2605060 | tf_op jit(solution)/shard_map/dot_general | solution.py:235
  102.2 0.7 convolution_convert_fusion.3
  103.7 2.8 %collective-permute-start.16 = (bf16[288,1024]{1,0:T(8,128)(2,1)S(1)}, bf16[288,1024]{1,0:T(8,128)(2,1)S(1)}, u32[]{:S(2)}, u32[]{:S(2)}) collective-permute-start(bf16[288,1024]{1,0:T(8,128)(2,1)S(1)} %convolution_convert_fusion), channel_id=1, source_target_pairs={{0,12},{1,13},{2,14},{3,15},{4,8},{5,9},{6,10},{7,11},{8,4},{9,5},... | collective-permute-start | bytes 1769480 | tf_op jit(solution)/shard_map/ppermute | solution.py:32
  107.2 1.5 %collective-permute-start.11 = (bf16[288,1024]{1,0:T(8,128)(2,1)S(1)}, bf16[288,1024]{1,0:T(8,128)(2,1)S(1)}, u32[]{:S(2)}, u32[]{:S(2)}) collective-permute-start(bf16[288,1024]{1,0:T(8,128)(2,1)S(1)} %convolution_convert_fusion.4), channel_id=1, source_target_pairs={{0,4},{1,5},{2,6},{3,7},{4,0},{5,1},{6,2},{7,3},{8,12},{9,13},{10,... | collective-permute-start | bytes 1769480 | tf_op jit(solution)/shard_map/ppermute | solution.py:32
  108.7 4.2 %collective-permute-done.14 = bf16[288,1024]{1,0:T(8,128)(2,1)S(1)} collective-permute-done((bf16[288,1024]{1,0:T(8,128)(2,1)S(1)}, bf16[288,1024]{1,0:T(8,128)(2,1)S(1)}, u32[]{:S(2)}, u32[]{:S(2)}) %collective-permute-start.14) | collective-permute-done | bytes 589856 | tf_op jit(solution)/shard_map/ppermute | solution.py:32
  112.9 0.7 fusion.4
  113.7 0.7 fusion.3
  114.4 2.1 %collective-permute-start.13 = (bf16[288,1024]{1,0:T(8,128)(2,1)S(1)}, bf16[288,1024]{1,0:T(8,128)(2,1)S(1)}, u32[]{:S(2)}, u32[]{:S(2)}) collective-permute-start(bf16[288,1024]{1,0:T(8,128)(2,1)S(1)} %fusion.3), channel_id=1, source_target_pairs={{0,12},{1,13},{2,14},{3,15},{4,8},{5,9},{6,10},{7,11},{8,4},{9,5},... | collective-permute-start | bytes 1769480 | tf_op jit(solution)/shard_map/ppermute | solution.py:32
  117.1 0.7 convolution_convert_fusion.5.refs_0_
  117.8 1.5 %collective-permute-done.16.refs_5_ = bf16[288,1024]{1,0:T(8,128)(2,1)S(1)} collective-permute-done((bf16[288,1024]{1,0:T(8,128)(2,1)S(1)}, bf16[288,1024]{1,0:T(8,128)(2,1)S(1)}, u32[]{:S(2)}, u32[]{:S(2)}) %collective-permute-start.16) | collective-permute-done | bytes 589856 | tf_op jit(solution)/shard_map/ppermute | solution.py:32
  119.2 6.3 %collective-permute-done.15.refs_4_ = bf16[288,1024]{1,0:T(8,128)(2,1)S(1)} collective-permute-done((bf16[288,1024]{1,0:T(8,128)(2,1)S(1)}, bf16[288,1024]{1,0:T(8,128)(2,1)S(1)}, u32[]{:S(2)}, u32[]{:S(2)}) %collective-permute-start.15) | collective-permute-done | bytes 589856 | tf_op jit(solution)/shard_map/ppermute | solution.py:32
  125.6 1.0 shard_map.82
  126.6 1.6 %collective-permute-start.17 = (bf16[144,1024]{1,0:T(8,128)(2,1)S(1)}, bf16[144,1024]{1,0:T(8,128)(2,1)S(1)}, u32[]{:S(2)}, u32[]{:S(2)}) collective-permute-start(bf16[144,1024]{1,0:T(8,128)(2,1)S(1)} %get-tuple-element.21), channel_id=1, source_target_pairs={{0,2},{1,3},{2,0},{3,1},{4,6},{5,7},{6,4},{7,5},{8,10},{9,11},{10,... | collective-permute-start | bytes 884744 | tf_op jit(solution)/shard_map/ppermute | solution.py:32
  128.2 1.0 collective-permute-start.18
  129.2 1.6 %collective-permute-start.19 = (bf16[144,1024]{1,0:T(8,128)(2,1)S(1)}, bf16[144,1024]{1,0:T(8,128)(2,1)S(1)}, u32[]{:S(2)}, u32[]{:S(2)}) collective-permute-start(bf16[144,1024]{1,0:T(8,128)(2,1)S(1)} %get-tuple-element.23), channel_id=1, source_target_pairs={{0,3},{1,2},{2,1},{3,0},{4,7},{5,6},{6,5},{7,4},{8,11},{9,10},{10,... | collective-permute-start | bytes 884744 | tf_op jit(solution)/shard_map/ppermute | solution.py:32
  130.8 4.2 %collective-permute-done.17.refs_1_ = bf16[144,1024]{1,0:T(8,128)(2,1)S(1)} collective-permute-done((bf16[144,1024]{1,0:T(8,128)(2,1)S(1)}, bf16[144,1024]{1,0:T(8,128)(2,1)S(1)}, u32[]{:S(2)}, u32[]{:S(2)}) %collective-permute-start.17) | collective-permute-done | bytes 294944 | tf_op jit(solution)/shard_map/ppermute | solution.py:32
  135.0 2.1 %collective-permute-done.18.refs_2_ = bf16[144,1024]{1,0:T(8,128)(2,1)S(1)} collective-permute-done((bf16[144,1024]{1,0:T(8,128)(2,1)S(1)}, bf16[144,1024]{1,0:T(8,128)(2,1)S(1)}, u32[]{:S(2)}, u32[]{:S(2)}) %collective-permute-start.18) | collective-permute-done | bytes 294944 | tf_op jit(solution)/shard_map/ppermute | solution.py:32
  137.1 1.0 collective-permute-done.19.refs_3_
  138.1 0.9 shard_map.83
  (52 shorter events, 6.4 us)
Async XLA Ops:
  0.6 5.1 %copy-start = (bf16[2304,512]{1,0:T(8,128)(2,1)S(1)}, bf16[2304,512]{1,0:T(8,128)(2,1)}, u32[]{:S(2)}) copy-start(bf16[2304,512]{1,0:T(8,128)(2,1)} %param.8) | copy-start | bytes 7077892
  0.6 12.9 %collective-permute-start = (bf16[144,1024]{1,0:T(8,128)(2,1)}, bf16[144,1024]{1,0:T(8,128)(2,1)S(1)}, u32[]{:S(2)}, u32[]{:S(2)}) collective-permute-start(bf16[144,1024]{1,0:T(8,128)(2,1)} %bitcast.60), channel_id=1, source_target_pairs={{0,2},{1,3},{2,0},{3,1},{4,6},{5,7},{6,4},{7,5},{8,10},{9,11},{10,... | collective-permute-start | bytes 884744 | tf_op jit(solution)/shard_map/ppermute | solution.py:32
  4.7 9.1 %collective-permute-start.1 = (bf16[144,1024]{1,0:T(8,128)(2,1)}, bf16[144,1024]{1,0:T(8,128)(2,1)S(1)}, u32[]{:S(2)}, u32[]{:S(2)}) collective-permute-start(bf16[144,1024]{1,0:T(8,128)(2,1)} %bitcast.61), channel_id=1, source_target_pairs={{0,1},{1,0},{2,3},{3,2},{4,5},{5,4},{6,7},{7,6},{8,9},{9,8},{10,11... | collective-permute-start | bytes 884744 | tf_op jit(solution)/shard_map/ppermute | solution.py:32
  5.7 8.1 %collective-permute-start.2 = (bf16[144,1024]{1,0:T(8,128)(2,1)}, bf16[144,1024]{1,0:T(8,128)(2,1)S(1)}, u32[]{:S(2)}, u32[]{:S(2)}) collective-permute-start(bf16[144,1024]{1,0:T(8,128)(2,1)} %bitcast.62), channel_id=1, source_target_pairs={{0,3},{1,2},{2,1},{3,0},{4,7},{5,6},{6,5},{7,4},{8,11},{9,10},{10,... | collective-permute-start | bytes 884744 | tf_op jit(solution)/shard_map/ppermute | solution.py:32
  9.7 4.2 %copy-start.2 = (bf16[1024,144]{0,1:T(8,128)(2,1)S(1)}, bf16[1024,144]{0,1:T(8,128)(2,1)}, u32[]{:S(2)}) copy-start(bf16[1024,144]{0,1:T(8,128)(2,1)} %param.6) | copy-start | bytes 884740
  14.5 12.8 %collective-permute-start.3 = (bf16[288,1024]{1,0:T(8,128)(2,1)S(1)}, bf16[288,1024]{1,0:T(8,128)(2,1)S(1)}, u32[]{:S(2)}, u32[]{:S(2)}) collective-permute-start(bf16[288,1024]{1,0:T(8,128)(2,1)S(1)} %get-tuple-element.17), channel_id=1, source_target_pairs={{0,4},{1,5},{2,6},{3,7},{4,0},{5,1},{6,2},{7,3},{8,12},{9,13},{10,... | collective-permute-start | bytes 1769480 | tf_op jit(solution)/shard_map/ppermute | solution.py:32
  16.2 11.1 %collective-permute-start.4 = (bf16[288,1024]{1,0:T(8,128)(2,1)S(1)}, bf16[288,1024]{1,0:T(8,128)(2,1)S(1)}, u32[]{:S(2)}, u32[]{:S(2)}) collective-permute-start(bf16[288,1024]{1,0:T(8,128)(2,1)S(1)} %get-tuple-element.16), channel_id=1, source_target_pairs={{0,12},{1,13},{2,14},{3,15},{4,8},{5,9},{6,10},{7,11},{8,4},{9,5},... | collective-permute-start | bytes 1769480 | tf_op jit(solution)/shard_map/ppermute | solution.py:32
  20.9 11.1 %collective-permute-start.5 = (bf16[288,1024]{1,0:T(8,128)(2,1)S(1)}, bf16[288,1024]{1,0:T(8,128)(2,1)S(1)}, u32[]{:S(2)}, u32[]{:S(2)}) collective-permute-start(bf16[288,1024]{1,0:T(8,128)(2,1)S(1)} %get-tuple-element.16), channel_id=1, source_target_pairs={{0,4},{1,5},{2,6},{3,7},{4,0},{5,1},{6,2},{7,3},{8,12},{9,13},{10,... | collective-permute-start | bytes 1769480 | tf_op jit(solution)/shard_map/ppermute | solution.py:32
  21.7 11.9 %collective-permute-start.6 = (bf16[288,1024]{1,0:T(8,128)(2,1)S(1)}, bf16[288,1024]{1,0:T(8,128)(2,1)S(1)}, u32[]{:S(2)}, u32[]{:S(2)}) collective-permute-start(bf16[288,1024]{1,0:T(8,128)(2,1)S(1)} %get-tuple-element.17), channel_id=1, source_target_pairs={{0,12},{1,13},{2,14},{3,15},{4,8},{5,9},{6,10},{7,11},{8,4},{9,5},... | collective-permute-start | bytes 1769480 | tf_op jit(solution)/shard_map/ppermute | solution.py:32
  27.3 9.9 %collective-permute-start.7 = (bf16[288,1024]{1,0:T(8,128)(2,1)S(1)}, bf16[288,1024]{1,0:T(8,128)(2,1)S(1)}, u32[]{:S(2)}, u32[]{:S(2)}) collective-permute-start(bf16[288,1024]{1,0:T(8,128)(2,1)S(1)} %collective-permute-done.4), channel_id=1, source_target_pairs={{0,4},{1,5},{2,6},{3,7},{4,0},{5,1},{6,2},{7,3},{8,12},{9,13},{10,... | collective-permute-start | bytes 1769480 | tf_op jit(solution)/shard_map/ppermute | solution.py:32
  27.3 12.6 %collective-permute-start.8 = (bf16[288,1024]{1,0:T(8,128)(2,1)S(1)}, bf16[288,1024]{1,0:T(8,128)(2,1)S(1)}, u32[]{:S(2)}, u32[]{:S(2)}) collective-permute-start(bf16[288,1024]{1,0:T(8,128)(2,1)S(1)} %collective-permute-done.3), channel_id=1, source_target_pairs={{0,12},{1,13},{2,14},{3,15},{4,8},{5,9},{6,10},{7,11},{8,4},{9,5},... | collective-permute-start | bytes 1769480 | tf_op jit(solution)/shard_map/ppermute | solution.py:32
  41.7 2.7 %collective-permute-start.9 = (bf16[512,896]{1,0:T(8,128)(2,1)S(1)}, bf16[512,896]{1,0:T(8,128)(2,1)S(1)}, u32[]{:S(2)}, u32[]{:S(2)}) collective-permute-start(bf16[512,896]{1,0:T(8,128)(2,1)S(1)} %shard_map.80), channel_id=1, source_target_pairs={{0,16},{16,0},{1,17},{17,1},{2,18},{18,2},{3,19},{19,3},{4,20},{20... | collective-permute-start | bytes 2752520 | tf_op jit(solution)/shard_map/ppermute | solution.py:36
  71.7 4.4 %copy-start.4 = (bf16[8,512]{1,0:T(8,128)(2,1)}, bf16[8,512]{1,0:T(8,128)(2,1)S(1)}, u32[]{:S(2)}) copy-start(bf16[8,512]{1,0:T(8,128)(2,1)S(1)} %reshape.55) | copy-start | bytes 24580
  71.9 4.2 %copy-start.5 = (bf16[8,1024,256]{2,1,0:T(8,128)(2,1)S(1)}, bf16[8,1024,256]{2,1,0:T(8,128)(2,1)}, u32[]{:S(2)}) copy-start(bf16[8,1024,256]{2,1,0:T(8,128)(2,1)} %param.11) | copy-start | bytes 12582916
  78.1 19.6 %all-to-all-start.1 = ((bf16[64,8,768]{2,1,0:T(8,128)(2,1)}), bf16[64,8,768]{2,1,0:T(8,128)(2,1)S(1)}, u32[]{:S(2)}, u32[]{:S(2)}) async-start(bf16[64,8,768]{2,1,0:T(8,128)(2,1)} %bitcast.22), calls=%async_computation.1 | async-start | bytes 1572864 | tf_op jit(solution)/shard_map/all_to_all | solution.py:228
  97.7 2.3 %collective-permute-start.10 = (bf16[512,768]{1,0:T(8,128)(2,1)S(1)}, bf16[512,768]{1,0:T(8,128)(2,1)S(1)}, u32[]{:S(2)}, u32[]{:S(2)}) collective-permute-start(bf16[512,768]{1,0:T(8,128)(2,1)S(1)} %bitcast.58), channel_id=1, source_target_pairs={{0,16},{16,0},{1,17},{17,1},{2,18},{18,2},{3,19},{19,3},{4,20},{20... | collective-permute-start | bytes 2359304 | tf_op jit(solution)/shard_map/ppermute | solution.py:36
  97.7 4.6 %copy-start.3 = (bf16[4,4,144,768]{3,2,1,0:T(8,128)(2,1)S(1)}, bf16[4,4,144,768]{3,2,1,0:T(8,128)(2,1)}, u32[]{:S(2)}) copy-start(bf16[4,4,144,768]{3,2,1,0:T(8,128)(2,1)} %bitcast_select_fusion.1) | copy-start | bytes 10616836
  101.8 11.2 %collective-permute-start.14 = (bf16[288,1024]{1,0:T(8,128)(2,1)S(1)}, bf16[288,1024]{1,0:T(8,128)(2,1)S(1)}, u32[]{:S(2)}, u32[]{:S(2)}) collective-permute-start(bf16[288,1024]{1,0:T(8,128)(2,1)S(1)} %convolution_convert_fusion.1), channel_id=1, source_target_pairs={{0,12},{1,13},{2,14},{3,15},{4,8},{5,9},{6,10},{7,11},{8,4},{9,5},... | collective-permute-start | bytes 1769480 | tf_op jit(solution)/shard_map/ppermute | solution.py:32
  102.9 10.8 %collective-permute-start.12 = (bf16[288,1024]{1,0:T(8,128)(2,1)S(1)}, bf16[288,1024]{1,0:T(8,128)(2,1)S(1)}, u32[]{:S(2)}, u32[]{:S(2)}) collective-permute-start(bf16[288,1024]{1,0:T(8,128)(2,1)S(1)} %convolution_convert_fusion.3), channel_id=1, source_target_pairs={{0,4},{1,5},{2,6},{3,7},{4,0},{5,1},{6,2},{7,3},{8,12},{9,13},{10,... | collective-permute-start | bytes 1769480 | tf_op jit(solution)/shard_map/ppermute | solution.py:32
  103.7 15.5 %collective-permute-start.16 = (bf16[288,1024]{1,0:T(8,128)(2,1)S(1)}, bf16[288,1024]{1,0:T(8,128)(2,1)S(1)}, u32[]{:S(2)}, u32[]{:S(2)}) collective-permute-start(bf16[288,1024]{1,0:T(8,128)(2,1)S(1)} %convolution_convert_fusion), channel_id=1, source_target_pairs={{0,12},{1,13},{2,14},{3,15},{4,8},{5,9},{6,10},{7,11},{8,4},{9,5},... | collective-permute-start | bytes 1769480 | tf_op jit(solution)/shard_map/ppermute | solution.py:32
  107.2 12.0 %collective-permute-start.11 = (bf16[288,1024]{1,0:T(8,128)(2,1)S(1)}, bf16[288,1024]{1,0:T(8,128)(2,1)S(1)}, u32[]{:S(2)}, u32[]{:S(2)}) collective-permute-start(bf16[288,1024]{1,0:T(8,128)(2,1)S(1)} %convolution_convert_fusion.4), channel_id=1, source_target_pairs={{0,4},{1,5},{2,6},{3,7},{4,0},{5,1},{6,2},{7,3},{8,12},{9,13},{10,... | collective-permute-start | bytes 1769480 | tf_op jit(solution)/shard_map/ppermute | solution.py:32
  113.6 11.9 %collective-permute-start.15 = (bf16[288,1024]{1,0:T(8,128)(2,1)S(1)}, bf16[288,1024]{1,0:T(8,128)(2,1)S(1)}, u32[]{:S(2)}, u32[]{:S(2)}) collective-permute-start(bf16[288,1024]{1,0:T(8,128)(2,1)S(1)} %fusion.4), channel_id=1, source_target_pairs={{0,4},{1,5},{2,6},{3,7},{4,0},{5,1},{6,2},{7,3},{8,12},{9,13},{10,... | collective-permute-start | bytes 1769480 | tf_op jit(solution)/shard_map/ppermute | solution.py:32
  114.4 11.2 %collective-permute-start.13 = (bf16[288,1024]{1,0:T(8,128)(2,1)S(1)}, bf16[288,1024]{1,0:T(8,128)(2,1)S(1)}, u32[]{:S(2)}, u32[]{:S(2)}) collective-permute-start(bf16[288,1024]{1,0:T(8,128)(2,1)S(1)} %fusion.3), channel_id=1, source_target_pairs={{0,12},{1,13},{2,14},{3,15},{4,8},{5,9},{6,10},{7,11},{8,4},{9,5},... | collective-permute-start | bytes 1769480 | tf_op jit(solution)/shard_map/ppermute | solution.py:32
  116.4 22.6 %copy-start.1 = (bf16[2304,512]{1,0:T(8,128)(2,1)S(1)}, bf16[2304,512]{1,0:T(8,128)(2,1)}, u32[]{:S(2)}) copy-start(bf16[2304,512]{1,0:T(8,128)(2,1)} %param.8) | copy-start | bytes 7077892
  126.6 8.4 %collective-permute-start.17 = (bf16[144,1024]{1,0:T(8,128)(2,1)S(1)}, bf16[144,1024]{1,0:T(8,128)(2,1)S(1)}, u32[]{:S(2)}, u32[]{:S(2)}) collective-permute-start(bf16[144,1024]{1,0:T(8,128)(2,1)S(1)} %get-tuple-element.21), channel_id=1, source_target_pairs={{0,2},{1,3},{2,0},{3,1},{4,6},{5,7},{6,4},{7,5},{8,10},{9,11},{10,... | collective-permute-start | bytes 884744 | tf_op jit(solution)/shard_map/ppermute | solution.py:32
  128.2 8.9 %collective-permute-start.18 = (bf16[144,1024]{1,0:T(8,128)(2,1)S(1)}, bf16[144,1024]{1,0:T(8,128)(2,1)S(1)}, u32[]{:S(2)}, u32[]{:S(2)}) collective-permute-start(bf16[144,1024]{1,0:T(8,128)(2,1)S(1)} %get-tuple-element.22), channel_id=1, source_target_pairs={{0,1},{1,0},{2,3},{3,2},{4,5},{5,4},{6,7},{7,6},{8,9},{9,8},{10,11... | collective-permute-start | bytes 884744 | tf_op jit(solution)/shard_map/ppermute | solution.py:32
  129.2 8.9 %collective-permute-start.19 = (bf16[144,1024]{1,0:T(8,128)(2,1)S(1)}, bf16[144,1024]{1,0:T(8,128)(2,1)S(1)}, u32[]{:S(2)}, u32[]{:S(2)}) collective-permute-start(bf16[144,1024]{1,0:T(8,128)(2,1)S(1)} %get-tuple-element.23), channel_id=1, source_target_pairs={{0,3},{1,2},{2,1},{3,0},{4,7},{5,6},{6,5},{7,4},{8,11},{9,10},{10,... | collective-permute-start | bytes 884744 | tf_op jit(solution)/shard_map/ppermute | solution.py:32

commit v6 on v5

--- a/solution.py
+++ b/solution.py
@@ -226,18 +226,21 @@
 
     spread = jnp.broadcast_to(attended[None], (4, 16, rows_dev, q_cols)).reshape(64, rows_dev, q_cols)
     mine = lax.all_to_all(spread, ("x", "y", "z"), 0, 0, tiled=True).reshape(512, q_cols)
-    mine, w_out = lax.optimization_barrier((mine, w_out))
+    far = [lax.dynamic_slice_in_dim(w_out, seconds[3] * 4 * feat + skip, half, 0) for skip in (0, half)]
+    mine, w_out, far = lax.optimization_barrier((mine, w_out, far))
     theirs = core_swap(mine)
     rows = join(theirs, mine)
 
-    def outward(i, skip, rows=rows):
-        w = lax.dynamic_slice_in_dim(w_out, i * 4 * feat + skip, half, 0)
+    def times(w, rows=rows):
         return lax.dot_general(w, rows, (((1,), (1,)), ((), ())), preferred_element_type=F32)
+
+    def outward(i, skip):
+        return times(lax.dynamic_slice_in_dim(w_out, i * 4 * feat + skip, half, 0))
 
     def send(v, mask):
         return exchange(v.astype(BF16), 1, mask)
 
-    low2, high2 = send(outward(seconds[3], 0), 1), send(outward(seconds[3], half), 3)
+    low2, high2 = send(times(far[0]), 1), send(times(far[1]), 3)
     low1, high3 = send(outward(seconds[1], 0), 1), send(outward(seconds[2], half), 3)
     high1, low3 = send(outward(seconds[1], half) + high2.astype(F32), 1), send(outward(seconds[2], 0) + low2.astype(F32), 3)
     low, high = outward(seconds[0], 0).astype(BF16), outward(seconds[0], half).astype(BF16)

time: 139 us -> 138 us (level)
  other arithmetic: 13.6 us -> 11.8 us
  local copies, waits for them, and re-layouts: 7.38 us -> 9.16 us
    select_n x2, other arithmetic: 9.08 us -> 7.33 us  [by_blocks(): return jnp.where(c == 0, w, w.swapaxes(0, 1)).reshape(16 * feat, -1)]
    unnamed x13 -> x15, local copies, waits for them, and re-layouts: 5.8 us -> 7.52 us
  transfers between devices with their start and end apart: 21 -> 21, of which waited for: 15 -> 15; matrix products, arithmetic and copies ran while one was open for 21% -> 19% of each run, Pallas kernels for 3% -> 3%
where the time goes in v6:
time: 138 us
  waiting for transfers between devices  36.3 us (26%)
  starting transfers between devices  28.9 us (21%)
  blocking collectives  26.7 us (19%)
  matrix products  15.1 us (11%)
  other arithmetic  11.8 us (9%)
  local copies, waits for them, and re-layouts  9.16 us (7%)
  Pallas kernels  9.15 us (7%)
    ppermute x18, waiting for transfers between devices, exchange(): return lax.ppermute(v, AXES, partner_pairs(phase, mask))  29.6 us
    all_to_all x1, blocking collectives, shards(): lax.all_to_all(part.reshape(64, rows_dev, -1), ('x', 'y', 'z'), 0, 0, til...  26.7 us
    ppermute x18, starting transfers between devices, exchange(): return lax.ppermute(v, AXES, partner_pairs(phase, mask))  23.8 us
    unnamed x15, local copies, waits for them, and re-layouts  7.52 us
    select_n x2, other arithmetic, by_blocks(): return jnp.where(c == 0, w, w.swapaxes(0, 1)).reshape(16 * feat, -1)  7.33 us
    pallas_call x3, Pallas kernels, add_products(): pl.pallas_call(add_products_kernel, compiler_params=few(16), in_specs=[SM...  6.39 us
    dot_general x8, matrix products, times(): lax.dot_general(w, rows, (((1,), (1,)), ((), ())), preferred_element_type...  5.22 us
    dot_general x4, matrix products, product(): lax.dot_general(v, w, (((0,), (0,)), ((), ())), preferred_element_type=F32)  5.06 us
  transfers between devices with their start and end apart: 21, of which 15 were waited for; matrix products, arithmetic and copies ran while one was open for 19% of the time, Pallas kernels for 3%

profile of v6, /device:TPU:0, one launch (start us, length us, event | category | flops | bytes accessed | tf_op | source)
XLA Modules:
  0.0 138.0 jit_solution(9464956700869142022)
XLA Ops:
  0.6 4.0 %collective-permute-start = (bf16[144,1024]{1,0:T(8,128)(2,1)}, bf16[144,1024]{1,0:T(8,128)(2,1)S(1)}, u32[]{:S(2)}, u32[]{:S(2)}) collective-permute-start(bf16[144,1024]{1,0:T(8,128)(2,1)} %bitcast.62), channel_id=1, source_target_pairs={{0,2},{1,3},{2,0},{3,1},{4,6},{5,7},{6,4},{7,5},{8,10},{9,11},{10,... | collective-permute-start | bytes 884744 | tf_op jit(solution)/shard_map/ppermute | solution.py:32
  4.7 1.0 collective-permute-start.1
  5.9 3.6 %fusion.1 = bf16[2304,896]{1,0:T(8,128)(2,1)} fusion(bf16[2304,32]{1,0:T(8,128)(2,1)S(1)} %constant_dynamic-slice_fusion.2, bf16[2304,768]{1,0:T(8,128)(2,1)} %param.7), kind=kLoop, calls=%fused_computation.2 | loop fusion | flops 12386304 | bytes 7815168 | tf_op jit(solution)/shard_map/concatenate | solution.py:187
  9.7 3.9 %bitcast_select_fusion = bf16[4,4,144,896]{3,2,1,0:T(8,128)(2,1)S(1)} fusion(bf16[4,4,144,896]{3,2,1,0:T(8,128)(2,1)} %bitcast.66, pred[]{:T(512)S(6)} %eq.2), kind=kLoop, calls=%fused_computation.3 | loop fusion | flops 2064384 | bytes 8257537 | tf_op jit(solution)/shard_map/jit(_where)/select_n | solution.py:184
  13.9 0.7 shard_map.77
  14.5 1.7 %collective-permute-start.3 = (bf16[288,1024]{1,0:T(8,128)(2,1)S(1)}, bf16[288,1024]{1,0:T(8,128)(2,1)S(1)}, u32[]{:S(2)}, u32[]{:S(2)}) collective-permute-start(bf16[288,1024]{1,0:T(8,128)(2,1)S(1)} %get-tuple-element.19), channel_id=1, source_target_pairs={{0,4},{1,5},{2,6},{3,7},{4,0},{5,1},{6,2},{7,3},{8,12},{9,13},{10,... | collective-permute-start | bytes 1769480 | tf_op jit(solution)/shard_map/ppermute | solution.py:32
  16.2 2.2 %collective-permute-start.4 = (bf16[288,1024]{1,0:T(8,128)(2,1)S(1)}, bf16[288,1024]{1,0:T(8,128)(2,1)S(1)}, u32[]{:S(2)}, u32[]{:S(2)}) collective-permute-start(bf16[288,1024]{1,0:T(8,128)(2,1)S(1)} %get-tuple-element.18), channel_id=1, source_target_pairs={{0,12},{1,13},{2,14},{3,15},{4,8},{5,9},{6,10},{7,11},{8,4},{9,5},... | collective-permute-start | bytes 1769480 | tf_op jit(solution)/shard_map/ppermute | solution.py:32
  18.4 1.2 fusion.15
  19.6 1.3 convolution_add_fusion
  20.9 0.8 collective-permute-start.5
  22.3 5.0 %collective-permute-done.4 = bf16[288,1024]{1,0:T(8,128)(2,1)S(1)} collective-permute-done((bf16[288,1024]{1,0:T(8,128)(2,1)S(1)}, bf16[288,1024]{1,0:T(8,128)(2,1)S(1)}, u32[]{:S(2)}, u32[]{:S(2)}) %collective-permute-start.4) | collective-permute-done | bytes 589856 | tf_op jit(solution)/shard_map/ppermute | solution.py:32
  27.3 2.3 %collective-permute-start.8 = (bf16[288,1024]{1,0:T(8,128)(2,1)S(1)}, bf16[288,1024]{1,0:T(8,128)(2,1)S(1)}, u32[]{:S(2)}, u32[]{:S(2)}) collective-permute-start(bf16[288,1024]{1,0:T(8,128)(2,1)S(1)} %collective-permute-done.3), channel_id=1, source_target_pairs={{0,12},{1,13},{2,14},{3,15},{4,8},{5,9},{6,10},{7,11},{8,4},{9,5},... | collective-permute-start | bytes 1769480 | tf_op jit(solution)/shard_map/ppermute | solution.py:32
  29.6 1.2 fusion.13
  30.8 1.3 add_add_fusion.part_ref
  32.1 1.5 %collective-permute-done.6.refs_1_ = bf16[288,1024]{1,0:T(8,128)(2,1)S(1)} collective-permute-done((bf16[288,1024]{1,0:T(8,128)(2,1)S(1)}, bf16[288,1024]{1,0:T(8,128)(2,1)S(1)}, u32[]{:S(2)}, u32[]{:S(2)}) %collective-permute-start.6) | collective-permute-done | bytes 589856 | tf_op jit(solution)/shard_map/ppermute | solution.py:32
  33.6 2.8 %shard_map.78.part_ref = f32[1024,896]{1,0:T(8,128)S(1)} custom-call(s32[3]{0:T(128)S(1)} %get-tuple-element.36.at_ref, f32[1024,896]{1,0:T(8,128)S(1)} %add_add_fusion.part_ref, bf16[288,1024]{1,0:T(8,128)(2,1)S(1)} %collective-permute-done.5.refs_0_, bf16[288,1024]{1,0:T(8,128)(2,1)S(1)} %collective-permute-done.6.refs_1_, bf16[2304,896]{1,0:T(8,128)(2,1)S(1)} %bitcast.57), custom_call_target="tpu_custom_call" | custom-call | tf_op jit(solution)/shard_map/pallas_call | solution.py:91
  36.4 0.8 collective-permute-done.7.refs_0_
  37.2 2.7 %collective-permute-done.8.refs_1_ = bf16[288,1024]{1,0:T(8,128)(2,1)S(1)} collective-permute-done((bf16[288,1024]{1,0:T(8,128)(2,1)S(1)}, bf16[288,1024]{1,0:T(8,128)(2,1)S(1)}, u32[]{:S(2)}, u32[]{:S(2)}) %collective-permute-start.8) | collective-permute-done | bytes 589856 | tf_op jit(solution)/shard_map/ppermute | solution.py:32
  39.9 1.8 %shard_map.80 = bf16[512,896]{1,0:T(8,128)(2,1)S(1)} custom-call(s32[3]{0:T(128)S(1)} %get-tuple-element.37.at_ref, f32[1024,896]{1,0:T(8,128)S(1)} %shard_map.78.part_ref, bf16[288,1024]{1,0:T(8,128)(2,1)S(1)} %collective-permute-done.7.refs_0_, bf16[288,1024]{1,0:T(8,128)(2,1)S(1)} %collective-permute-done.8.refs_1_, bf16[2304,896]{1,0:T(8,128)(2,1)S(1)} %bitcast.58), custom_call_target="tpu_custom_call" | custom-call | tf_op jit(solution)/shard_map/pallas_call | solution.py:91
  42.1 1.8 %shard_map.79 = f32[512,896]{1,0:T(8,128)S(1)} custom-call(s32[3]{0:T(128)S(1)} %add_add_fusion.1.at_ref, f32[1024,896]{1,0:T(8,128)S(1)} %shard_map.78.part_ref, bf16[288,1024]{1,0:T(8,128)(2,1)S(1)} %collective-permute-done.7.refs_0_, bf16[288,1024]{1,0:T(8,128)(2,1)S(1)} %collective-permute-done.8.refs_1_, bf16[2304,896]{1,0:T(8,128)(2,1)S(1)} %bitcast.59), custom_call_target="tpu_custom_call" | custom-call | tf_op jit(solution)/shard_map/pallas_call | solution.py:91
  44.6 26.7 %all_to_all.10 = bf16[64,8,896]{2,1,0:T(8,128)(2,1)S(1)} all-to-all(bf16[64,8,896]{2,1,0:T(8,128)(2,1)S(1)} %fusion.6), channel_id=1, replica_groups=mesh['x'=4,'c'=2,'y'=4,'z'=4] {'x','y','z'}, dimensions={0} | all-to-all | bytes 1835008 | tf_op jit(solution)/shard_map/all_to_all | solution.py:207
  71.9 3.8 %fusion.38 = (f32[8,48]{1,0:T(8,128)S(1)}, f32[8,48,1024]{2,1,0:T(8,128)S(1)}) fusion(bf16[8,48,256]{2,1,0:T(8,128)(2,1)S(1)} %reshape.54, bf16[8,1024,256]{2,1,0:T(8,128)(2,1)} %param.10), kind=kOutput, calls=%fused_computation.68 | convolution fusion | flops 202112640 | bytes 5965312 | tf_op jit(solution)/shard_map/bhe,bte->bht/dot_general | solution.py:215
  76.1 0.9 fusion.5
  77.2 0.9 broadcast_in_dim.2
  78.1 4.8 %all-to-all-start.1 = ((bf16[64,8,768]{2,1,0:T(8,128)(2,1)}), bf16[64,8,768]{2,1,0:T(8,128)(2,1)S(1)}, u32[]{:S(2)}, u32[]{:S(2)}) async-start(bf16[64,8,768]{2,1,0:T(8,128)(2,1)} %bitcast.22), calls=%async_computation.1 | async-start | bytes 1572864 | tf_op jit(solution)/shard_map/all_to_all | solution.py:228
  82.9 5.8 %copy.24 = bf16[768,2304]{0,1:T(8,128)(2,1)} copy(bf16[768,2304]{1,0:T(8,128)(2,1)} %param.9) | data formatting | bytes 7077888 | tf_op args[3]
  88.7 3.4 %bitcast_select_fusion.1 = bf16[4,4,144,768]{3,2,1,0:T(8,128)(2,1)S(1)} fusion(bf16[4,4,144,768]{3,2,1,0:T(8,128)(2,1)} %bitcast.67, pred[]{:T(512)S(6)} %eq.2), kind=kLoop, calls=%fused_computation.5 | loop fusion | flops 1769472 | bytes 7077889 | tf_op jit(solution)/shard_map/jit(_where)/select_n | solution.py:184
  92.1 1.7 %copy-done.3 = bf16[4,4,144,768]{3,2,1,0:T(8,128)(2,1)} copy-done((bf16[4,4,144,768]{3,2,1,0:T(8,128)(2,1)}, bf16[4,4,144,768]{3,2,1,0:T(8,128)(2,1)S(1)}, u32[]{:S(2)}) %copy-start.3) | copy-done | bytes 3538968
  93.9 3.8 %all-to-all-done.1 = bf16[64,8,768]{2,1,0:T(8,128)(2,1)S(1)} async-done(((bf16[64,8,768]{2,1,0:T(8,128)(2,1)}), bf16[64,8,768]{2,1,0:T(8,128)(2,1)S(1)}, u32[]{:S(2)}, u32[]{:S(2)}) %all-to-all-start.1) | async-done | bytes 786464 | tf_op jit(solution)/shard_map/all_to_all | solution.py:228
  97.7 2.3 %collective-permute-done.10.a_ref = bf16[512,768]{1,0:T(8,128)(2,1)S(1)} collective-permute-done((bf16[512,768]{1,0:T(8,128)(2,1)S(1)}, bf16[512,768]{1,0:T(8,128)(2,1)S(1)}, u32[]{:S(2)}, u32[]{:S(2)}) %collective-permute-start.10) | collective-permute-done | bytes 786464 | tf_op jit(solution)/shard_map/ppermute | solution.py:36
  100.1 0.7 convolution_convert_fusion.1
  102.1 0.7 convolution_convert_fusion
  102.7 2.8 %collective-permute-start.16 = (bf16[288,1024]{1,0:T(8,128)(2,1)S(1)}, bf16[288,1024]{1,0:T(8,128)(2,1)S(1)}, u32[]{:S(2)}, u32[]{:S(2)}) collective-permute-start(bf16[288,1024]{1,0:T(8,128)(2,1)S(1)} %convolution_convert_fusion), channel_id=1, source_target_pairs={{0,12},{1,13},{2,14},{3,15},{4,8},{5,9},{6,10},{7,11},{8,4},{9,5},... | collective-permute-start | bytes 1769480 | tf_op jit(solution)/shard_map/ppermute | solution.py:32
  106.2 1.5 %collective-permute-start.11 = (bf16[288,1024]{1,0:T(8,128)(2,1)S(1)}, bf16[288,1024]{1,0:T(8,128)(2,1)S(1)}, u32[]{:S(2)}, u32[]{:S(2)}) collective-permute-start(bf16[288,1024]{1,0:T(8,128)(2,1)S(1)} %convolution_convert_fusion.4), channel_id=1, source_target_pairs={{0,4},{1,5},{2,6},{3,7},{4,0},{5,1},{6,2},{7,3},{8,12},{9,13},{10,... | collective-permute-start | bytes 1769480 | tf_op jit(solution)/shard_map/ppermute | solution.py:32
  107.7 4.2 %collective-permute-done.14 = bf16[288,1024]{1,0:T(8,128)(2,1)S(1)} collective-permute-done((bf16[288,1024]{1,0:T(8,128)(2,1)S(1)}, bf16[288,1024]{1,0:T(8,128)(2,1)S(1)}, u32[]{:S(2)}, u32[]{:S(2)}) %collective-permute-start.14) | collective-permute-done | bytes 589856 | tf_op jit(solution)/shard_map/ppermute | solution.py:32
  112.7 0.7 fusion.3
  113.3 2.1 %collective-permute-start.13 = (bf16[288,1024]{1,0:T(8,128)(2,1)S(1)}, bf16[288,1024]{1,0:T(8,128)(2,1)S(1)}, u32[]{:S(2)}, u32[]{:S(2)}) collective-permute-start(bf16[288,1024]{1,0:T(8,128)(2,1)S(1)} %fusion.3), channel_id=1, source_target_pairs={{0,12},{1,13},{2,14},{3,15},{4,8},{5,9},{6,10},{7,11},{8,4},{9,5},... | collective-permute-start | bytes 1769480 | tf_op jit(solution)/shard_map/ppermute | solution.py:32
  116.1 0.7 convolution_convert_fusion.5.refs_0_
  116.7 1.5 %collective-permute-done.16.refs_5_ = bf16[288,1024]{1,0:T(8,128)(2,1)S(1)} collective-permute-done((bf16[288,1024]{1,0:T(8,128)(2,1)S(1)}, bf16[288,1024]{1,0:T(8,128)(2,1)S(1)}, u32[]{:S(2)}, u32[]{:S(2)}) %collective-permute-start.16) | collective-permute-done | bytes 589856 | tf_op jit(solution)/shard_map/ppermute | solution.py:32
  118.2 6.3 %collective-permute-done.15.refs_4_ = bf16[288,1024]{1,0:T(8,128)(2,1)S(1)} collective-permute-done((bf16[288,1024]{1,0:T(8,128)(2,1)S(1)}, bf16[288,1024]{1,0:T(8,128)(2,1)S(1)}, u32[]{:S(2)}, u32[]{:S(2)}) %collective-permute-start.15) | collective-permute-done | bytes 589856 | tf_op jit(solution)/shard_map/ppermute | solution.py:32
  124.6 1.0 shard_map.82
  125.6 1.7 %collective-permute-start.17 = (bf16[144,1024]{1,0:T(8,128)(2,1)S(1)}, bf16[144,1024]{1,0:T(8,128)(2,1)S(1)}, u32[]{:S(2)}, u32[]{:S(2)}) collective-permute-start(bf16[144,1024]{1,0:T(8,128)(2,1)S(1)} %get-tuple-element.25), channel_id=1, source_target_pairs={{0,2},{1,3},{2,0},{3,1},{4,6},{5,7},{6,4},{7,5},{8,10},{9,11},{10,... | collective-permute-start | bytes 884744 | tf_op jit(solution)/shard_map/ppermute | solution.py:32
  127.3 0.9 collective-permute-start.18
  128.2 1.6 %collective-permute-start.19 = (bf16[144,1024]{1,0:T(8,128)(2,1)S(1)}, bf16[144,1024]{1,0:T(8,128)(2,1)S(1)}, u32[]{:S(2)}, u32[]{:S(2)}) collective-permute-start(bf16[144,1024]{1,0:T(8,128)(2,1)S(1)} %get-tuple-element.27), channel_id=1, source_target_pairs={{0,3},{1,2},{2,1},{3,0},{4,7},{5,6},{6,5},{7,4},{8,11},{9,10},{10,... | collective-permute-start | bytes 884744 | tf_op jit(solution)/shard_map/ppermute | solution.py:32
  129.8 4.2 %collective-permute-done.17.refs_1_ = bf16[144,1024]{1,0:T(8,128)(2,1)S(1)} collective-permute-done((bf16[144,1024]{1,0:T(8,128)(2,1)S(1)}, bf16[144,1024]{1,0:T(8,128)(2,1)S(1)}, u32[]{:S(2)}, u32[]{:S(2)}) %collective-permute-start.17) | collective-permute-done | bytes 294944 | tf_op jit(solution)/shard_map/ppermute | solution.py:32
  134.0 2.1 %collective-permute-done.18.refs_2_ = bf16[144,1024]{1,0:T(8,128)(2,1)S(1)} collective-permute-done((bf16[144,1024]{1,0:T(8,128)(2,1)S(1)}, bf16[144,1024]{1,0:T(8,128)(2,1)S(1)}, u32[]{:S(2)}, u32[]{:S(2)}) %collective-permute-start.18) | collective-permute-done | bytes 294944 | tf_op jit(solution)/shard_map/ppermute | solution.py:32
  136.1 1.0 collective-permute-done.19.refs_3_
  137.1 0.9 shard_map.83
  (55 shorter events, 7.1 us)
Async XLA Ops:
  0.6 5.1 %copy-start = (bf16[2304,512]{1,0:T(8,128)(2,1)S(1)}, bf16[2304,512]{1,0:T(8,128)(2,1)}, u32[]{:S(2)}) copy-start(bf16[2304,512]{1,0:T(8,128)(2,1)} %param.8) | copy-start | bytes 7077892
  0.6 12.9 %collective-permute-start = (bf16[144,1024]{1,0:T(8,128)(2,1)}, bf16[144,1024]{1,0:T(8,128)(2,1)S(1)}, u32[]{:S(2)}, u32[]{:S(2)}) collective-permute-start(bf16[144,1024]{1,0:T(8,128)(2,1)} %bitcast.62), channel_id=1, source_target_pairs={{0,2},{1,3},{2,0},{3,1},{4,6},{5,7},{6,4},{7,5},{8,10},{9,11},{10,... | collective-permute-start | bytes 884744 | tf_op jit(solution)/shard_map/ppermute | solution.py:32
  4.7 9.1 %collective-permute-start.1 = (bf16[144,1024]{1,0:T(8,128)(2,1)}, bf16[144,1024]{1,0:T(8,128)(2,1)S(1)}, u32[]{:S(2)}, u32[]{:S(2)}) collective-permute-start(bf16[144,1024]{1,0:T(8,128)(2,1)} %bitcast.63), channel_id=1, source_target_pairs={{0,1},{1,0},{2,3},{3,2},{4,5},{5,4},{6,7},{7,6},{8,9},{9,8},{10,11... | collective-permute-start | bytes 884744 | tf_op jit(solution)/shard_map/ppermute | solution.py:32
  5.7 8.1 %collective-permute-start.2 = (bf16[144,1024]{1,0:T(8,128)(2,1)}, bf16[144,1024]{1,0:T(8,128)(2,1)S(1)}, u32[]{:S(2)}, u32[]{:S(2)}) collective-permute-start(bf16[144,1024]{1,0:T(8,128)(2,1)} %bitcast.64), channel_id=1, source_target_pairs={{0,3},{1,2},{2,1},{3,0},{4,7},{5,6},{6,5},{7,4},{8,11},{9,10},{10,... | collective-permute-start | bytes 884744 | tf_op jit(solution)/shard_map/ppermute | solution.py:32
  9.7 4.2 %copy-start.2 = (bf16[1024,144]{0,1:T(8,128)(2,1)S(1)}, bf16[1024,144]{0,1:T(8,128)(2,1)}, u32[]{:S(2)}) copy-start(bf16[1024,144]{0,1:T(8,128)(2,1)} %param.6) | copy-start | bytes 884740
  14.5 12.8 %collective-permute-start.3 = (bf16[288,1024]{1,0:T(8,128)(2,1)S(1)}, bf16[288,1024]{1,0:T(8,128)(2,1)S(1)}, u32[]{:S(2)}, u32[]{:S(2)}) collective-permute-start(bf16[288,1024]{1,0:T(8,128)(2,1)S(1)} %get-tuple-element.19), channel_id=1, source_target_pairs={{0,4},{1,5},{2,6},{3,7},{4,0},{5,1},{6,2},{7,3},{8,12},{9,13},{10,... | collective-permute-start | bytes 1769480 | tf_op jit(solution)/shard_map/ppermute | solution.py:32
  16.2 11.1 %collective-permute-start.4 = (bf16[288,1024]{1,0:T(8,128)(2,1)S(1)}, bf16[288,1024]{1,0:T(8,128)(2,1)S(1)}, u32[]{:S(2)}, u32[]{:S(2)}) collective-permute-start(bf16[288,1024]{1,0:T(8,128)(2,1)S(1)} %get-tuple-element.18), channel_id=1, source_target_pairs={{0,12},{1,13},{2,14},{3,15},{4,8},{5,9},{6,10},{7,11},{8,4},{9,5},... | collective-permute-start | bytes 1769480 | tf_op jit(solution)/shard_map/ppermute | solution.py:32
  20.9 11.1 %collective-permute-start.5 = (bf16[288,1024]{1,0:T(8,128)(2,1)S(1)}, bf16[288,1024]{1,0:T(8,128)(2,1)S(1)}, u32[]{:S(2)}, u32[]{:S(2)}) collective-permute-start(bf16[288,1024]{1,0:T(8,128)(2,1)S(1)} %get-tuple-element.18), channel_id=1, source_target_pairs={{0,4},{1,5},{2,6},{3,7},{4,0},{5,1},{6,2},{7,3},{8,12},{9,13},{10,... | collective-permute-start | bytes 1769480 | tf_op jit(solution)/shard_map/ppermute | solution.py:32
  21.7 11.9 %collective-permute-start.6 = (bf16[288,1024]{1,0:T(8,128)(2,1)S(1)}, bf16[288,1024]{1,0:T(8,128)(2,1)S(1)}, u32[]{:S(2)}, u32[]{:S(2)}) collective-permute-start(bf16[288,1024]{1,0:T(8,128)(2,1)S(1)} %get-tuple-element.19), channel_id=1, source_target_pairs={{0,12},{1,13},{2,14},{3,15},{4,8},{5,9},{6,10},{7,11},{8,4},{9,5},... | collective-permute-start | bytes 1769480 | tf_op jit(solution)/shard_map/ppermute | solution.py:32
  27.3 9.9 %collective-permute-start.7 = (bf16[288,1024]{1,0:T(8,128)(2,1)S(1)}, bf16[288,1024]{1,0:T(8,128)(2,1)S(1)}, u32[]{:S(2)}, u32[]{:S(2)}) collective-permute-start(bf16[288,1024]{1,0:T(8,128)(2,1)S(1)} %collective-permute-done.4), channel_id=1, source_target_pairs={{0,4},{1,5},{2,6},{3,7},{4,0},{5,1},{6,2},{7,3},{8,12},{9,13},{10,... | collective-permute-start | bytes 1769480 | tf_op jit(solution)/shard_map/ppermute | solution.py:32
  27.3 12.6 %collective-permute-start.8 = (bf16[288,1024]{1,0:T(8,128)(2,1)S(1)}, bf16[288,1024]{1,0:T(8,128)(2,1)S(1)}, u32[]{:S(2)}, u32[]{:S(2)}) collective-permute-start(bf16[288,1024]{1,0:T(8,128)(2,1)S(1)} %collective-permute-done.3), channel_id=1, source_target_pairs={{0,12},{1,13},{2,14},{3,15},{4,8},{5,9},{6,10},{7,11},{8,4},{9,5},... | collective-permute-start | bytes 1769480 | tf_op jit(solution)/shard_map/ppermute | solution.py:32
  41.7 2.7 %collective-permute-start.9 = (bf16[512,896]{1,0:T(8,128)(2,1)S(1)}, bf16[512,896]{1,0:T(8,128)(2,1)S(1)}, u32[]{:S(2)}, u32[]{:S(2)}) collective-permute-start(bf16[512,896]{1,0:T(8,128)(2,1)S(1)} %shard_map.80), channel_id=1, source_target_pairs={{0,16},{16,0},{1,17},{17,1},{2,18},{18,2},{3,19},{19,3},{4,20},{20... | collective-permute-start | bytes 2752520 | tf_op jit(solution)/shard_map/ppermute | solution.py:36
  71.7 4.4 %copy-start.5 = (bf16[8,512]{1,0:T(8,128)(2,1)}, bf16[8,512]{1,0:T(8,128)(2,1)S(1)}, u32[]{:S(2)}) copy-start(bf16[8,512]{1,0:T(8,128)(2,1)S(1)} %reshape.55) | copy-start | bytes 24580
  71.9 4.2 %copy-start.6 = (bf16[8,1024,256]{2,1,0:T(8,128)(2,1)S(1)}, bf16[8,1024,256]{2,1,0:T(8,128)(2,1)}, u32[]{:S(2)}) copy-start(bf16[8,1024,256]{2,1,0:T(8,128)(2,1)} %param.11) | copy-start | bytes 12582916
  78.1 19.6 %all-to-all-start.1 = ((bf16[64,8,768]{2,1,0:T(8,128)(2,1)}), bf16[64,8,768]{2,1,0:T(8,128)(2,1)S(1)}, u32[]{:S(2)}, u32[]{:S(2)}) async-start(bf16[64,8,768]{2,1,0:T(8,128)(2,1)} %bitcast.22), calls=%async_computation.1 | async-start | bytes 1572864 | tf_op jit(solution)/shard_map/all_to_all | solution.py:228
  92.1 1.7 %copy-start.3 = (bf16[4,4,144,768]{3,2,1,0:T(8,128)(2,1)}, bf16[4,4,144,768]{3,2,1,0:T(8,128)(2,1)S(1)}, u32[]{:S(2)}) copy-start(bf16[4,4,144,768]{3,2,1,0:T(8,128)(2,1)S(1)} %bitcast_select_fusion.1) | copy-start | bytes 10616836
  97.7 2.3 %collective-permute-start.10 = (bf16[512,768]{1,0:T(8,128)(2,1)S(1)}, bf16[512,768]{1,0:T(8,128)(2,1)S(1)}, u32[]{:S(2)}, u32[]{:S(2)}) collective-permute-start(bf16[512,768]{1,0:T(8,128)(2,1)S(1)} %bitcast.60), channel_id=1, source_target_pairs={{0,16},{16,0},{1,17},{17,1},{2,18},{18,2},{3,19},{19,3},{4,20},{20... | collective-permute-start | bytes 2359304 | tf_op jit(solution)/shard_map/ppermute | solution.py:36
  100.1 2.0 %copy-start.4 = (bf16[4,4,144,768]{3,2,1,0:T(8,128)(2,1)S(1)}, bf16[4,4,144,768]{3,2,1,0:T(8,128)(2,1)}, u32[]{:S(2)}) copy-start(bf16[4,4,144,768]{3,2,1,0:T(8,128)(2,1)} %copy-done.3) | copy-start | bytes 10616836
  100.7 11.2 %collective-permute-start.14 = (bf16[288,1024]{1,0:T(8,128)(2,1)S(1)}, bf16[288,1024]{1,0:T(8,128)(2,1)S(1)}, u32[]{:S(2)}, u32[]{:S(2)}) collective-permute-start(bf16[288,1024]{1,0:T(8,128)(2,1)S(1)} %convolution_convert_fusion.1), channel_id=1, source_target_pairs={{0,12},{1,13},{2,14},{3,15},{4,8},{5,9},{6,10},{7,11},{8,4},{9,5},... | collective-permute-start | bytes 1769480 | tf_op jit(solution)/shard_map/ppermute | solution.py:32
  101.9 10.8 %collective-permute-start.12 = (bf16[288,1024]{1,0:T(8,128)(2,1)S(1)}, bf16[288,1024]{1,0:T(8,128)(2,1)S(1)}, u32[]{:S(2)}, u32[]{:S(2)}) collective-permute-start(bf16[288,1024]{1,0:T(8,128)(2,1)S(1)} %convolution_convert_fusion.3), channel_id=1, source_target_pairs={{0,4},{1,5},{2,6},{3,7},{4,0},{5,1},{6,2},{7,3},{8,12},{9,13},{10,... | collective-permute-start | bytes 1769480 | tf_op jit(solution)/shard_map/ppermute | solution.py:32
  102.7 15.5 %collective-permute-start.16 = (bf16[288,1024]{1,0:T(8,128)(2,1)S(1)}, bf16[288,1024]{1,0:T(8,128)(2,1)S(1)}, u32[]{:S(2)}, u32[]{:S(2)}) collective-permute-start(bf16[288,1024]{1,0:T(8,128)(2,1)S(1)} %convolution_convert_fusion), channel_id=1, source_target_pairs={{0,12},{1,13},{2,14},{3,15},{4,8},{5,9},{6,10},{7,11},{8,4},{9,5},... | collective-permute-start | bytes 1769480 | tf_op jit(solution)/shard_map/ppermute | solution.py:32
  106.2 12.0 %collective-permute-start.11 = (bf16[288,1024]{1,0:T(8,128)(2,1)S(1)}, bf16[288,1024]{1,0:T(8,128)(2,1)S(1)}, u32[]{:S(2)}, u32[]{:S(2)}) collective-permute-start(bf16[288,1024]{1,0:T(8,128)(2,1)S(1)} %convolution_convert_fusion.4), channel_id=1, source_target_pairs={{0,4},{1,5},{2,6},{3,7},{4,0},{5,1},{6,2},{7,3},{8,12},{9,13},{10,... | collective-permute-start | bytes 1769480 | tf_op jit(solution)/shard_map/ppermute | solution.py:32
  112.6 11.9 %collective-permute-start.15 = (bf16[288,1024]{1,0:T(8,128)(2,1)S(1)}, bf16[288,1024]{1,0:T(8,128)(2,1)S(1)}, u32[]{:S(2)}, u32[]{:S(2)}) collective-permute-start(bf16[288,1024]{1,0:T(8,128)(2,1)S(1)} %fusion.4), channel_id=1, source_target_pairs={{0,4},{1,5},{2,6},{3,7},{4,0},{5,1},{6,2},{7,3},{8,12},{9,13},{10,... | collective-permute-start | bytes 1769480 | tf_op jit(solution)/shard_map/ppermute | solution.py:32
  113.3 11.2 %collective-permute-start.13 = (bf16[288,1024]{1,0:T(8,128)(2,1)S(1)}, bf16[288,1024]{1,0:T(8,128)(2,1)S(1)}, u32[]{:S(2)}, u32[]{:S(2)}) collective-permute-start(bf16[288,1024]{1,0:T(8,128)(2,1)S(1)} %fusion.3), channel_id=1, source_target_pairs={{0,12},{1,13},{2,14},{3,15},{4,8},{5,9},{6,10},{7,11},{8,4},{9,5},... | collective-permute-start | bytes 1769480 | tf_op jit(solution)/shard_map/ppermute | solution.py:32
  115.4 22.6 %copy-start.1 = (bf16[2304,512]{1,0:T(8,128)(2,1)S(1)}, bf16[2304,512]{1,0:T(8,128)(2,1)}, u32[]{:S(2)}) copy-start(bf16[2304,512]{1,0:T(8,128)(2,1)} %param.8) | copy-start | bytes 7077892
  125.6 8.4 %collective-permute-start.17 = (bf16[144,1024]{1,0:T(8,128)(2,1)S(1)}, bf16[144,1024]{1,0:T(8,128)(2,1)S(1)}, u32[]{:S(2)}, u32[]{:S(2)}) collective-permute-start(bf16[144,1024]{1,0:T(8,128)(2,1)S(1)} %get-tuple-element.25), channel_id=1, source_target_pairs={{0,2},{1,3},{2,0},{3,1},{4,6},{5,7},{6,4},{7,5},{8,10},{9,11},{10,... | collective-permute-start | bytes 884744 | tf_op jit(solution)/shard_map/ppermute | solution.py:32
  127.3 8.8 %collective-permute-start.18 = (bf16[144,1024]{1,0:T(8,128)(2,1)S(1)}, bf16[144,1024]{1,0:T(8,128)(2,1)S(1)}, u32[]{:S(2)}, u32[]{:S(2)}) collective-permute-start(bf16[144,1024]{1,0:T(8,128)(2,1)S(1)} %get-tuple-element.26), channel_id=1, source_target_pairs={{0,1},{1,0},{2,3},{3,2},{4,5},{5,4},{6,7},{7,6},{8,9},{9,8},{10,11... | collective-permute-start | bytes 884744 | tf_op jit(solution)/shard_map/ppermute | solution.py:32
  128.2 8.9 %collective-permute-start.19 = (bf16[144,1024]{1,0:T(8,128)(2,1)S(1)}, bf16[144,1024]{1,0:T(8,128)(2,1)S(1)}, u32[]{:S(2)}, u32[]{:S(2)}) collective-permute-start(bf16[144,1024]{1,0:T(8,128)(2,1)S(1)} %get-tuple-element.27), channel_id=1, source_target_pairs={{0,3},{1,2},{2,1},{3,0},{4,7},{5,6},{6,5},{7,4},{8,11},{9,10},{10,... | collective-permute-start | bytes 884744 | tf_op jit(solution)/shard_map/ppermute | solution.py:32

commit v7 on v6

--- a/solution.py
+++ b/solution.py
@@ -231,19 +231,26 @@
     theirs = core_swap(mine)
     rows = join(theirs, mine)
 
-    def times(w, rows=rows):
+    def times(w, rows):
         return lax.dot_general(w, rows, (((1,), (1,)), ((), ())), preferred_element_type=F32)
 
-    def outward(i, skip):
-        return times(lax.dynamic_slice_in_dim(w_out, i * 4 * feat + skip, half, 0))
+    def outward(i, skip, rows):
+        return times(lax.dynamic_slice_in_dim(w_out, i * 4 * feat + skip, half, 0), rows)
 
     def send(v, mask):
         return exchange(v.astype(BF16), 1, mask)
 
-    low2, high2 = send(times(far[0]), 1), send(times(far[1]), 3)
-    low1, high3 = send(outward(seconds[1], 0), 1), send(outward(seconds[2], half), 3)
-    high1, low3 = send(outward(seconds[1], half) + high2.astype(F32), 1), send(outward(seconds[2], 0) + low2.astype(F32), 3)
-    low, high = outward(seconds[0], 0).astype(BF16), outward(seconds[0], half).astype(BF16)
+    def added(v, theirs, mine):
+        return v + jnp.concatenate([theirs, mine], 1).astype(F32)
+
+    low_mine, high_mine = send(times(far[0], mine), 1), send(times(far[1], mine), 3)
+    low_theirs, high_theirs = times(far[0], theirs).astype(BF16), times(far[1], theirs).astype(BF16)
+    low_theirs, high_theirs, rows = lax.optimization_barrier((low_theirs, high_theirs, rows))
+    low_theirs, high_theirs = exchange(low_theirs, 1, 1), exchange(high_theirs, 1, 3)
+    low1, high3 = send(outward(seconds[1], 0, rows), 1), send(outward(seconds[2], half, rows), 3)
+    high1 = send(added(outward(seconds[1], half, rows), high_theirs, high_mine), 1)
+    low3 = send(added(outward(seconds[2], 0, rows), low_theirs, low_mine), 3)
+    low, high = outward(seconds[0], 0, rows).astype(BF16), outward(seconds[0], half, rows).astype(BF16)
     keep, *away = add_and_part(firsts, low, low1, low3, high, high1, high3)
     out = merge_cores(c, keep, *[exchange(v, 0, m) for v, m in zip(away, MASKS)])
     return out.T, new_keyvalue

time: 138 us -> 138 us (level)
  waiting for transfers between devices: 36.3 us -> 34.5 us
    ppermute x2, waiting for transfers between devices: 2.87 us -> 1.31 us  [core_swap(): return lax.ppermute(v, 'c', [(0, 1), (1, 0)])]
    ppermute x18 -> x20, starting transfers between devices: 23.8 us -> 25.1 us  [exchange(): return lax.ppermute(v, AXES, partner_pairs(phase, mask))]
    dot_general x8 -> x10, matrix products: 5.22 us -> 5.62 us  [times(): lax.dot_general(w, rows, (((1,), (1,)), ((), ())), preferred_element_type...]
    ppermute x18 -> x20, waiting for transfers between devices: 29.6 us -> 29.4 us  [exchange(): return lax.ppermute(v, AXES, partner_pairs(phase, mask))]
  transfers between devices with their start and end apart: 21 -> 23, of which waited for: 15 -> 16; matrix products, arithmetic and copies ran while one was open for 19% -> 20% of each run, Pallas kernels for 3% -> 3%
where the time goes in v7:
time: 138 us
  waiting for transfers between devices  34.5 us (25%)
  starting transfers between devices  30.1 us (22%)
  blocking collectives  26.7 us (19%)
  matrix products  15.4 us (11%)
  other arithmetic  11.8 us (9%)
  Pallas kernels  9.19 us (7%)
  local copies, waits for them, and re-layouts  9.16 us (7%)
    ppermute x20, waiting for transfers between devices, exchange(): return lax.ppermute(v, AXES, partner_pairs(phase, mask))  29.4 us
    all_to_all x1, blocking collectives, shards(): lax.all_to_all(part.reshape(64, rows_dev, -1), ('x', 'y', 'z'), 0, 0, til...  26.7 us
    ppermute x20, starting transfers between devices, exchange(): return lax.ppermute(v, AXES, partner_pairs(phase, mask))  25.1 us
    unnamed x15, local copies, waits for them, and re-layouts  7.51 us
    select_n x2, other arithmetic, by_blocks(): return jnp.where(c == 0, w, w.swapaxes(0, 1)).reshape(16 * feat, -1)  7.33 us
    pallas_call x3, Pallas kernels, add_products(): pl.pallas_call(add_products_kernel, compiler_params=few(16), in_specs=[SM...  6.43 us
    dot_general x10, matrix products, times(): lax.dot_general(w, rows, (((1,), (1,)), ((), ())), preferred_element_type...  5.62 us
    dot_general x4, matrix products, product(): lax.dot_general(v, w, (((0,), (0,)), ((), ())), preferred_element_type=F32)  4.97 us
  transfers between devices with their start and end apart: 23, of which 16 were waited for; matrix products, arithmetic and copies ran while one was open for 20% of the time, Pallas kernels for 3%

profile of v7, /device:TPU:0, one launch (start us, length us, event | category | flops | bytes accessed | tf_op | source)
XLA Modules:
  0.0 137.8 jit_solution(8426647940944536033)
XLA Ops:
  0.6 4.0 %collective-permute-start = (bf16[144,1024]{1,0:T(8,128)(2,1)}, bf16[144,1024]{1,0:T(8,128)(2,1)S(1)}, u32[]{:S(2)}, u32[]{:S(2)}) collective-permute-start(bf16[144,1024]{1,0:T(8,128)(2,1)} %bitcast.68), channel_id=1, source_target_pairs={{0,2},{1,3},{2,0},{3,1},{4,6},{5,7},{6,4},{7,5},{8,10},{9,11},{10,... | collective-permute-start | bytes 884744 | tf_op jit(solution)/shard_map/ppermute | solution.py:32
  4.7 1.0 collective-permute-start.1
  5.9 3.6 %fusion.1 = bf16[2304,896]{1,0:T(8,128)(2,1)} fusion(bf16[2304,32]{1,0:T(8,128)(2,1)S(1)} %constant_dynamic-slice_fusion.2, bf16[2304,768]{1,0:T(8,128)(2,1)} %param.7), kind=kLoop, calls=%fused_computation.2 | loop fusion | flops 12386304 | bytes 7815168 | tf_op jit(solution)/shard_map/concatenate | solution.py:187
  9.7 3.9 %bitcast_select_fusion = bf16[4,4,144,896]{3,2,1,0:T(8,128)(2,1)S(1)} fusion(bf16[4,4,144,896]{3,2,1,0:T(8,128)(2,1)} %bitcast.72, pred[]{:T(512)S(6)} %eq.2), kind=kLoop, calls=%fused_computation.3 | loop fusion | flops 2064384 | bytes 8257537 | tf_op jit(solution)/shard_map/jit(_where)/select_n | solution.py:184
  13.9 0.7 shard_map.77
  14.5 1.7 %collective-permute-start.3 = (bf16[288,1024]{1,0:T(8,128)(2,1)S(1)}, bf16[288,1024]{1,0:T(8,128)(2,1)S(1)}, u32[]{:S(2)}, u32[]{:S(2)}) collective-permute-start(bf16[288,1024]{1,0:T(8,128)(2,1)S(1)} %get-tuple-element.22), channel_id=1, source_target_pairs={{0,4},{1,5},{2,6},{3,7},{4,0},{5,1},{6,2},{7,3},{8,12},{9,13},{10,... | collective-permute-start | bytes 1769480 | tf_op jit(solution)/shard_map/ppermute | solution.py:32
  16.2 2.2 %collective-permute-start.4 = (bf16[288,1024]{1,0:T(8,128)(2,1)S(1)}, bf16[288,1024]{1,0:T(8,128)(2,1)S(1)}, u32[]{:S(2)}, u32[]{:S(2)}) collective-permute-start(bf16[288,1024]{1,0:T(8,128)(2,1)S(1)} %get-tuple-element.21), channel_id=1, source_target_pairs={{0,12},{1,13},{2,14},{3,15},{4,8},{5,9},{6,10},{7,11},{8,4},{9,5},... | collective-permute-start | bytes 1769480 | tf_op jit(solution)/shard_map/ppermute | solution.py:32
  18.4 1.2 fusion.15
  19.6 1.3 convolution_add_fusion
  20.9 0.8 collective-permute-start.5
  22.2 5.1 %collective-permute-done.4 = bf16[288,1024]{1,0:T(8,128)(2,1)S(1)} collective-permute-done((bf16[288,1024]{1,0:T(8,128)(2,1)S(1)}, bf16[288,1024]{1,0:T(8,128)(2,1)S(1)}, u32[]{:S(2)}, u32[]{:S(2)}) %collective-permute-start.4) | collective-permute-done | bytes 589856 | tf_op jit(solution)/shard_map/ppermute | solution.py:32
  27.3 2.3 %collective-permute-start.8 = (bf16[288,1024]{1,0:T(8,128)(2,1)S(1)}, bf16[288,1024]{1,0:T(8,128)(2,1)S(1)}, u32[]{:S(2)}, u32[]{:S(2)}) collective-permute-start(bf16[288,1024]{1,0:T(8,128)(2,1)S(1)} %collective-permute-done.3), channel_id=1, source_target_pairs={{0,12},{1,13},{2,14},{3,15},{4,8},{5,9},{6,10},{7,11},{8,4},{9,5},... | collective-permute-start | bytes 1769480 | tf_op jit(solution)/shard_map/ppermute | solution.py:32
  29.6 1.2 fusion.13
  30.8 1.3 add_add_fusion.part_ref
  32.1 1.5 %collective-permute-done.6.refs_1_ = bf16[288,1024]{1,0:T(8,128)(2,1)S(1)} collective-permute-done((bf16[288,1024]{1,0:T(8,128)(2,1)S(1)}, bf16[288,1024]{1,0:T(8,128)(2,1)S(1)}, u32[]{:S(2)}, u32[]{:S(2)}) %collective-permute-start.6) | collective-permute-done | bytes 589856 | tf_op jit(solution)/shard_map/ppermute | solution.py:32
  33.6 2.8 %shard_map.78.part_ref = f32[1024,896]{1,0:T(8,128)S(1)} custom-call(s32[3]{0:T(128)S(1)} %get-tuple-element.42.at_ref, f32[1024,896]{1,0:T(8,128)S(1)} %add_add_fusion.part_ref, bf16[288,1024]{1,0:T(8,128)(2,1)S(1)} %collective-permute-done.5.refs_0_, bf16[288,1024]{1,0:T(8,128)(2,1)S(1)} %collective-permute-done.6.refs_1_, bf16[2304,896]{1,0:T(8,128)(2,1)S(1)} %bitcast.61), custom_call_target="tpu_custom_call" | custom-call | tf_op jit(solution)/shard_map/pallas_call | solution.py:91
  36.5 0.7 collective-permute-done.7.refs_0_
  37.2 2.8 %collective-permute-done.8.refs_1_ = bf16[288,1024]{1,0:T(8,128)(2,1)S(1)} collective-permute-done((bf16[288,1024]{1,0:T(8,128)(2,1)S(1)}, bf16[288,1024]{1,0:T(8,128)(2,1)S(1)}, u32[]{:S(2)}, u32[]{:S(2)}) %collective-permute-start.8) | collective-permute-done | bytes 589856 | tf_op jit(solution)/shard_map/ppermute | solution.py:32
  39.9 1.8 %shard_map.80 = bf16[512,896]{1,0:T(8,128)(2,1)S(1)} custom-call(s32[3]{0:T(128)S(1)} %get-tuple-element.43.at_ref, f32[1024,896]{1,0:T(8,128)S(1)} %shard_map.78.part_ref, bf16[288,1024]{1,0:T(8,128)(2,1)S(1)} %collective-permute-done.7.refs_0_, bf16[288,1024]{1,0:T(8,128)(2,1)S(1)} %collective-permute-done.8.refs_1_, bf16[2304,896]{1,0:T(8,128)(2,1)S(1)} %bitcast.62), custom_call_target="tpu_custom_call" | custom-call | tf_op jit(solution)/shard_map/pallas_call | solution.py:91
  42.1 1.8 %shard_map.79 = f32[512,896]{1,0:T(8,128)S(1)} custom-call(s32[3]{0:T(128)S(1)} %add_add_fusion.1.at_ref, f32[1024,896]{1,0:T(8,128)S(1)} %shard_map.78.part_ref, bf16[288,1024]{1,0:T(8,128)(2,1)S(1)} %collective-permute-done.7.refs_0_, bf16[288,1024]{1,0:T(8,128)(2,1)S(1)} %collective-permute-done.8.refs_1_, bf16[2304,896]{1,0:T(8,128)(2,1)S(1)} %bitcast.63), custom_call_target="tpu_custom_call" | custom-call | tf_op jit(solution)/shard_map/pallas_call | solution.py:91
  44.6 26.7 %all_to_all.10 = bf16[64,8,896]{2,1,0:T(8,128)(2,1)S(1)} all-to-all(bf16[64,8,896]{2,1,0:T(8,128)(2,1)S(1)} %fusion.6), channel_id=1, replica_groups=mesh['x'=4,'c'=2,'y'=4,'z'=4] {'x','y','z'}, dimensions={0} | all-to-all | bytes 1835008 | tf_op jit(solution)/shard_map/all_to_all | solution.py:207
  71.9 3.8 %fusion.38 = (f32[8,48]{1,0:T(8,128)S(1)}, f32[8,48,1024]{2,1,0:T(8,128)S(1)}) fusion(bf16[8,48,256]{2,1,0:T(8,128)(2,1)S(1)} %reshape.54, bf16[8,1024,256]{2,1,0:T(8,128)(2,1)} %param.10), kind=kOutput, calls=%fused_computation.70 | convolution fusion | flops 202112640 | bytes 5965312 | tf_op jit(solution)/shard_map/bhe,bte->bht/dot_general | solution.py:215
  76.1 0.8 fusion.5
  77.2 0.9 broadcast_in_dim.2
  78.1 4.8 %all-to-all-start.1 = ((bf16[64,8,768]{2,1,0:T(8,128)(2,1)}), bf16[64,8,768]{2,1,0:T(8,128)(2,1)S(1)}, u32[]{:S(2)}, u32[]{:S(2)}) async-start(bf16[64,8,768]{2,1,0:T(8,128)(2,1)} %bitcast.22), calls=%async_computation.1 | async-start | bytes 1572864 | tf_op jit(solution)/shard_map/all_to_all | solution.py:228
  82.9 5.7 %copy.24 = bf16[768,2304]{0,1:T(8,128)(2,1)} copy(bf16[768,2304]{1,0:T(8,128)(2,1)} %param.9) | data formatting | bytes 7077888 | tf_op args[3]
  88.7 3.4 %bitcast_select_fusion.1 = bf16[4,4,144,768]{3,2,1,0:T(8,128)(2,1)S(1)} fusion(bf16[4,4,144,768]{3,2,1,0:T(8,128)(2,1)} %bitcast.73, pred[]{:T(512)S(6)} %eq.2), kind=kLoop, calls=%fused_computation.5 | loop fusion | flops 1769472 | bytes 7077889 | tf_op jit(solution)/shard_map/jit(_where)/select_n | solution.py:184
  92.1 1.7 %copy-done.3 = bf16[4,4,144,768]{3,2,1,0:T(8,128)(2,1)} copy-done((bf16[4,4,144,768]{3,2,1,0:T(8,128)(2,1)}, bf16[4,4,144,768]{3,2,1,0:T(8,128)(2,1)S(1)}, u32[]{:S(2)}) %copy-start.3) | copy-done | bytes 3538968
  93.9 3.8 %all-to-all-done.1 = bf16[64,8,768]{2,1,0:T(8,128)(2,1)S(1)} async-done(((bf16[64,8,768]{2,1,0:T(8,128)(2,1)}), bf16[64,8,768]{2,1,0:T(8,128)(2,1)S(1)}, u32[]{:S(2)}, u32[]{:S(2)}) %all-to-all-start.1) | async-done | bytes 786464 | tf_op jit(solution)/shard_map/all_to_all | solution.py:228
  99.2 0.7 collective-permute-done.10.a_ref
  100.9 2.1 %collective-permute-start.15 = (bf16[288,512]{1,0:T(8,128)(2,1)S(1)}, bf16[288,512]{1,0:T(8,128)(2,1)S(1)}, u32[]{:S(2)}, u32[]{:S(2)}) collective-permute-start(bf16[288,512]{1,0:T(8,128)(2,1)S(1)} %convolution_convert_fusion.6), channel_id=1, source_target_pairs={{0,12},{1,13},{2,14},{3,15},{4,8},{5,9},{6,10},{7,11},{8,4},{9,5},... | collective-permute-start | bytes 884744 | tf_op jit(solution)/shard_map/ppermute | solution.py:32
  103.7 1.3 collective-permute-start.18
  106.1 1.6 %collective-permute-start.11 = (bf16[288,1024]{1,0:T(8,128)(2,1)S(1)}, bf16[288,1024]{1,0:T(8,128)(2,1)S(1)}, u32[]{:S(2)}, u32[]{:S(2)}) collective-permute-start(bf16[288,1024]{1,0:T(8,128)(2,1)S(1)} %convolution_convert_fusion.2), channel_id=1, source_target_pairs={{0,4},{1,5},{2,6},{3,7},{4,0},{5,1},{6,2},{7,3},{8,12},{9,13},{10,... | collective-permute-start | bytes 1769480 | tf_op jit(solution)/shard_map/ppermute | solution.py:32
  107.8 1.5 %collective-permute-done.15 = bf16[288,512]{1,0:T(8,128)(2,1)S(1)} collective-permute-done((bf16[288,512]{1,0:T(8,128)(2,1)S(1)}, bf16[288,512]{1,0:T(8,128)(2,1)S(1)}, u32[]{:S(2)}, u32[]{:S(2)}) %collective-permute-start.15) | collective-permute-done | bytes 294944 | tf_op jit(solution)/shard_map/ppermute | solution.py:32
  109.3 0.7 fusion.4
  110.1 1.7 %collective-permute-done.12 = bf16[288,512]{1,0:T(8,128)(2,1)S(1)} collective-permute-done((bf16[288,512]{1,0:T(8,128)(2,1)S(1)}, bf16[288,512]{1,0:T(8,128)(2,1)S(1)}, u32[]{:S(2)}, u32[]{:S(2)}) %collective-permute-start.12) | collective-permute-done | bytes 294944 | tf_op jit(solution)/shard_map/ppermute | solution.py:32
  111.7 0.7 fusion.3
  112.4 2.3 %collective-permute-start.14 = (bf16[288,1024]{1,0:T(8,128)(2,1)S(1)}, bf16[288,1024]{1,0:T(8,128)(2,1)S(1)}, u32[]{:S(2)}, u32[]{:S(2)}) collective-permute-start(bf16[288,1024]{1,0:T(8,128)(2,1)S(1)} %fusion.3), channel_id=1, source_target_pairs={{0,12},{1,13},{2,14},{3,15},{4,8},{5,9},{6,10},{7,11},{8,4},{9,5},... | collective-permute-start | bytes 1769480 | tf_op jit(solution)/shard_map/ppermute | solution.py:32
  115.4 0.7 convolution_convert_fusion.3.refs_0_
  116.0 2.0 %collective-permute-done.11.refs_1_ = bf16[288,1024]{1,0:T(8,128)(2,1)S(1)} collective-permute-done((bf16[288,1024]{1,0:T(8,128)(2,1)S(1)}, bf16[288,1024]{1,0:T(8,128)(2,1)S(1)}, u32[]{:S(2)}, u32[]{:S(2)}) %collective-permute-start.11) | collective-permute-done | bytes 589856 | tf_op jit(solution)/shard_map/ppermute | solution.py:32
  118.0 6.3 %collective-permute-done.17.refs_4_ = bf16[288,1024]{1,0:T(8,128)(2,1)S(1)} collective-permute-done((bf16[288,1024]{1,0:T(8,128)(2,1)S(1)}, bf16[288,1024]{1,0:T(8,128)(2,1)S(1)}, u32[]{:S(2)}, u32[]{:S(2)}) %collective-permute-start.17) | collective-permute-done | bytes 589856 | tf_op jit(solution)/shard_map/ppermute | solution.py:32
  124.4 1.0 shard_map.82
  125.4 1.4 %collective-permute-start.19 = (bf16[144,1024]{1,0:T(8,128)(2,1)S(1)}, bf16[144,1024]{1,0:T(8,128)(2,1)S(1)}, u32[]{:S(2)}, u32[]{:S(2)}) collective-permute-start(bf16[144,1024]{1,0:T(8,128)(2,1)S(1)} %get-tuple-element.31), channel_id=1, source_target_pairs={{0,2},{1,3},{2,0},{3,1},{4,6},{5,7},{6,4},{7,5},{8,10},{9,11},{10,... | collective-permute-start | bytes 884744 | tf_op jit(solution)/shard_map/ppermute | solution.py:32
  127.3 2.3 %collective-permute-start.21 = (bf16[144,1024]{1,0:T(8,128)(2,1)S(1)}, bf16[144,1024]{1,0:T(8,128)(2,1)S(1)}, u32[]{:S(2)}, u32[]{:S(2)}) collective-permute-start(bf16[144,1024]{1,0:T(8,128)(2,1)S(1)} %get-tuple-element.33), channel_id=1, source_target_pairs={{0,3},{1,2},{2,1},{3,0},{4,7},{5,6},{6,5},{7,4},{8,11},{9,10},{10,... | collective-permute-start | bytes 884744 | tf_op jit(solution)/shard_map/ppermute | solution.py:32
  129.6 4.2 %collective-permute-done.19.refs_1_ = bf16[144,1024]{1,0:T(8,128)(2,1)S(1)} collective-permute-done((bf16[144,1024]{1,0:T(8,128)(2,1)S(1)}, bf16[144,1024]{1,0:T(8,128)(2,1)S(1)}, u32[]{:S(2)}, u32[]{:S(2)}) %collective-permute-start.19) | collective-permute-done | bytes 294944 | tf_op jit(solution)/shard_map/ppermute | solution.py:32
  133.8 1.3 collective-permute-done.20.refs_2_
  135.1 1.8 %collective-permute-done.21.refs_3_ = bf16[144,1024]{1,0:T(8,128)(2,1)S(1)} collective-permute-done((bf16[144,1024]{1,0:T(8,128)(2,1)S(1)}, bf16[144,1024]{1,0:T(8,128)(2,1)S(1)}, u32[]{:S(2)}, u32[]{:S(2)}) %collective-permute-start.21) | collective-permute-done | bytes 294944 | tf_op jit(solution)/shard_map/ppermute | solution.py:32
  136.9 0.9 shard_map.83
  (61 shorter events, 9.0 us)
Async XLA Ops:
  0.6 5.1 %copy-start = (bf16[2304,512]{1,0:T(8,128)(2,1)S(1)}, bf16[2304,512]{1,0:T(8,128)(2,1)}, u32[]{:S(2)}) copy-start(bf16[2304,512]{1,0:T(8,128)(2,1)} %param.8) | copy-start | bytes 7077892
  0.6 12.9 %collective-permute-start = (bf16[144,1024]{1,0:T(8,128)(2,1)}, bf16[144,1024]{1,0:T(8,128)(2,1)S(1)}, u32[]{:S(2)}, u32[]{:S(2)}) collective-permute-start(bf16[144,1024]{1,0:T(8,128)(2,1)} %bitcast.68), channel_id=1, source_target_pairs={{0,2},{1,3},{2,0},{3,1},{4,6},{5,7},{6,4},{7,5},{8,10},{9,11},{10,... | collective-permute-start | bytes 884744 | tf_op jit(solution)/shard_map/ppermute | solution.py:32
  4.7 9.1 %collective-permute-start.1 = (bf16[144,1024]{1,0:T(8,128)(2,1)}, bf16[144,1024]{1,0:T(8,128)(2,1)S(1)}, u32[]{:S(2)}, u32[]{:S(2)}) collective-permute-start(bf16[144,1024]{1,0:T(8,128)(2,1)} %bitcast.69), channel_id=1, source_target_pairs={{0,1},{1,0},{2,3},{3,2},{4,5},{5,4},{6,7},{7,6},{8,9},{9,8},{10,11... | collective-permute-start | bytes 884744 | tf_op jit(solution)/shard_map/ppermute | solution.py:32
  5.7 8.1 %collective-permute-start.2 = (bf16[144,1024]{1,0:T(8,128)(2,1)}, bf16[144,1024]{1,0:T(8,128)(2,1)S(1)}, u32[]{:S(2)}, u32[]{:S(2)}) collective-permute-start(bf16[144,1024]{1,0:T(8,128)(2,1)} %bitcast.70), channel_id=1, source_target_pairs={{0,3},{1,2},{2,1},{3,0},{4,7},{5,6},{6,5},{7,4},{8,11},{9,10},{10,... | collective-permute-start | bytes 884744 | tf_op jit(solution)/shard_map/ppermute | solution.py:32
  9.7 4.2 %copy-start.2 = (bf16[1024,144]{0,1:T(8,128)(2,1)S(1)}, bf16[1024,144]{0,1:T(8,128)(2,1)}, u32[]{:S(2)}) copy-start(bf16[1024,144]{0,1:T(8,128)(2,1)} %param.6) | copy-start | bytes 884740
  14.5 12.8 %collective-permute-start.3 = (bf16[288,1024]{1,0:T(8,128)(2,1)S(1)}, bf16[288,1024]{1,0:T(8,128)(2,1)S(1)}, u32[]{:S(2)}, u32[]{:S(2)}) collective-permute-start(bf16[288,1024]{1,0:T(8,128)(2,1)S(1)} %get-tuple-element.22), channel_id=1, source_target_pairs={{0,4},{1,5},{2,6},{3,7},{4,0},{5,1},{6,2},{7,3},{8,12},{9,13},{10,... | collective-permute-start | bytes 1769480 | tf_op jit(solution)/shard_map/ppermute | solution.py:32
  16.2 11.1 %collective-permute-start.4 = (bf16[288,1024]{1,0:T(8,128)(2,1)S(1)}, bf16[288,1024]{1,0:T(8,128)(2,1)S(1)}, u32[]{:S(2)}, u32[]{:S(2)}) collective-permute-start(bf16[288,1024]{1,0:T(8,128)(2,1)S(1)} %get-tuple-element.21), channel_id=1, source_target_pairs={{0,12},{1,13},{2,14},{3,15},{4,8},{5,9},{6,10},{7,11},{8,4},{9,5},... | collective-permute-start | bytes 1769480 | tf_op jit(solution)/shard_map/ppermute | solution.py:32
  20.9 11.2 %collective-permute-start.5 = (bf16[288,1024]{1,0:T(8,128)(2,1)S(1)}, bf16[288,1024]{1,0:T(8,128)(2,1)S(1)}, u32[]{:S(2)}, u32[]{:S(2)}) collective-permute-start(bf16[288,1024]{1,0:T(8,128)(2,1)S(1)} %get-tuple-element.21), channel_id=1, source_target_pairs={{0,4},{1,5},{2,6},{3,7},{4,0},{5,1},{6,2},{7,3},{8,12},{9,13},{10,... | collective-permute-start | bytes 1769480 | tf_op jit(solution)/shard_map/ppermute | solution.py:32
  21.6 12.0 %collective-permute-start.6 = (bf16[288,1024]{1,0:T(8,128)(2,1)S(1)}, bf16[288,1024]{1,0:T(8,128)(2,1)S(1)}, u32[]{:S(2)}, u32[]{:S(2)}) collective-permute-start(bf16[288,1024]{1,0:T(8,128)(2,1)S(1)} %get-tuple-element.22), channel_id=1, source_target_pairs={{0,12},{1,13},{2,14},{3,15},{4,8},{5,9},{6,10},{7,11},{8,4},{9,5},... | collective-permute-start | bytes 1769480 | tf_op jit(solution)/shard_map/ppermute | solution.py:32
  27.3 9.9 %collective-permute-start.7 = (bf16[288,1024]{1,0:T(8,128)(2,1)S(1)}, bf16[288,1024]{1,0:T(8,128)(2,1)S(1)}, u32[]{:S(2)}, u32[]{:S(2)}) collective-permute-start(bf16[288,1024]{1,0:T(8,128)(2,1)S(1)} %collective-permute-done.4), channel_id=1, source_target_pairs={{0,4},{1,5},{2,6},{3,7},{4,0},{5,1},{6,2},{7,3},{8,12},{9,13},{10,... | collective-permute-start | bytes 1769480 | tf_op jit(solution)/shard_map/ppermute | solution.py:32
  27.3 12.6 %collective-permute-start.8 = (bf16[288,1024]{1,0:T(8,128)(2,1)S(1)}, bf16[288,1024]{1,0:T(8,128)(2,1)S(1)}, u32[]{:S(2)}, u32[]{:S(2)}) collective-permute-start(bf16[288,1024]{1,0:T(8,128)(2,1)S(1)} %collective-permute-done.3), channel_id=1, source_target_pairs={{0,12},{1,13},{2,14},{3,15},{4,8},{5,9},{6,10},{7,11},{8,4},{9,5},... | collective-permute-start | bytes 1769480 | tf_op jit(solution)/shard_map/ppermute | solution.py:32
  41.7 2.7 %collective-permute-start.9 = (bf16[512,896]{1,0:T(8,128)(2,1)S(1)}, bf16[512,896]{1,0:T(8,128)(2,1)S(1)}, u32[]{:S(2)}, u32[]{:S(2)}) collective-permute-start(bf16[512,896]{1,0:T(8,128)(2,1)S(1)} %shard_map.80), channel_id=1, source_target_pairs={{0,16},{16,0},{1,17},{17,1},{2,18},{18,2},{3,19},{19,3},{4,20},{20... | collective-permute-start | bytes 2752520 | tf_op jit(solution)/shard_map/ppermute | solution.py:36
  71.7 4.4 %copy-start.5 = (bf16[8,512]{1,0:T(8,128)(2,1)}, bf16[8,512]{1,0:T(8,128)(2,1)S(1)}, u32[]{:S(2)}) copy-start(bf16[8,512]{1,0:T(8,128)(2,1)S(1)} %reshape.55) | copy-start | bytes 24580
  71.9 4.2 %copy-start.6 = (bf16[8,1024,256]{2,1,0:T(8,128)(2,1)S(1)}, bf16[8,1024,256]{2,1,0:T(8,128)(2,1)}, u32[]{:S(2)}) copy-start(bf16[8,1024,256]{2,1,0:T(8,128)(2,1)} %param.11) | copy-start | bytes 12582916
  78.1 19.6 %all-to-all-start.1 = ((bf16[64,8,768]{2,1,0:T(8,128)(2,1)}), bf16[64,8,768]{2,1,0:T(8,128)(2,1)S(1)}, u32[]{:S(2)}, u32[]{:S(2)}) async-start(bf16[64,8,768]{2,1,0:T(8,128)(2,1)} %bitcast.22), calls=%async_computation.1 | async-start | bytes 1572864 | tf_op jit(solution)/shard_map/all_to_all | solution.py:228
  92.1 1.7 %copy-start.3 = (bf16[4,4,144,768]{3,2,1,0:T(8,128)(2,1)}, bf16[4,4,144,768]{3,2,1,0:T(8,128)(2,1)S(1)}, u32[]{:S(2)}) copy-start(bf16[4,4,144,768]{3,2,1,0:T(8,128)(2,1)S(1)} %bitcast_select_fusion.1) | copy-start | bytes 10616836
  97.7 2.3 %collective-permute-start.10 = (bf16[512,768]{1,0:T(8,128)(2,1)S(1)}, bf16[512,768]{1,0:T(8,128)(2,1)S(1)}, u32[]{:S(2)}, u32[]{:S(2)}) collective-permute-start(bf16[512,768]{1,0:T(8,128)(2,1)S(1)} %bitcast.64), channel_id=1, source_target_pairs={{0,16},{16,0},{1,17},{17,1},{2,18},{18,2},{3,19},{19,3},{4,20},{20... | collective-permute-start | bytes 2359304 | tf_op jit(solution)/shard_map/ppermute | solution.py:36
  98.1 4.9 %copy-start.4 = (bf16[4,4,144,768]{3,2,1,0:T(8,128)(2,1)S(1)}, bf16[4,4,144,768]{3,2,1,0:T(8,128)(2,1)}, u32[]{:S(2)}) copy-start(bf16[4,4,144,768]{3,2,1,0:T(8,128)(2,1)} %copy-done.3) | copy-start | bytes 10616836
  98.1 8.0 %collective-permute-start.16 = (bf16[288,512]{1,0:T(8,128)(2,1)S(1)}, bf16[288,512]{1,0:T(8,128)(2,1)S(1)}, u32[]{:S(2)}, u32[]{:S(2)}) collective-permute-start(bf16[288,512]{1,0:T(8,128)(2,1)S(1)} %convolution_convert_fusion.4), channel_id=1, source_target_pairs={{0,12},{1,13},{2,14},{3,15},{4,8},{5,9},{6,10},{7,11},{8,4},{9,5},... | collective-permute-start | bytes 884744 | tf_op jit(solution)/shard_map/ppermute | solution.py:32
  99.1 11.0 %collective-permute-start.13 = (bf16[288,512]{1,0:T(8,128)(2,1)S(1)}, bf16[288,512]{1,0:T(8,128)(2,1)S(1)}, u32[]{:S(2)}, u32[]{:S(2)}) collective-permute-start(bf16[288,512]{1,0:T(8,128)(2,1)S(1)} %convolution_convert_fusion.5), channel_id=1, source_target_pairs={{0,4},{1,5},{2,6},{3,7},{4,0},{5,1},{6,2},{7,3},{8,12},{9,13},{10,... | collective-permute-start | bytes 884744 | tf_op jit(solution)/shard_map/ppermute | solution.py:32
  100.9 8.4 %collective-permute-start.15 = (bf16[288,512]{1,0:T(8,128)(2,1)S(1)}, bf16[288,512]{1,0:T(8,128)(2,1)S(1)}, u32[]{:S(2)}, u32[]{:S(2)}) collective-permute-start(bf16[288,512]{1,0:T(8,128)(2,1)S(1)} %convolution_convert_fusion.6), channel_id=1, source_target_pairs={{0,12},{1,13},{2,14},{3,15},{4,8},{5,9},{6,10},{7,11},{8,4},{9,5},... | collective-permute-start | bytes 884744 | tf_op jit(solution)/shard_map/ppermute | solution.py:32
  103.7 12.3 %collective-permute-start.18 = (bf16[288,1024]{1,0:T(8,128)(2,1)S(1)}, bf16[288,1024]{1,0:T(8,128)(2,1)S(1)}, u32[]{:S(2)}, u32[]{:S(2)}) collective-permute-start(bf16[288,1024]{1,0:T(8,128)(2,1)S(1)} %convolution_convert_fusion), channel_id=1, source_target_pairs={{0,12},{1,13},{2,14},{3,15},{4,8},{5,9},{6,10},{7,11},{8,4},{9,5},... | collective-permute-start | bytes 1769480 | tf_op jit(solution)/shard_map/ppermute | solution.py:32
  105.0 6.7 %collective-permute-start.12 = (bf16[288,512]{1,0:T(8,128)(2,1)S(1)}, bf16[288,512]{1,0:T(8,128)(2,1)S(1)}, u32[]{:S(2)}, u32[]{:S(2)}) collective-permute-start(bf16[288,512]{1,0:T(8,128)(2,1)S(1)} %convolution_convert_fusion.7), channel_id=1, source_target_pairs={{0,4},{1,5},{2,6},{3,7},{4,0},{5,1},{6,2},{7,3},{8,12},{9,13},{10,... | collective-permute-start | bytes 884744 | tf_op jit(solution)/shard_map/ppermute | solution.py:32
  106.1 11.9 %collective-permute-start.11 = (bf16[288,1024]{1,0:T(8,128)(2,1)S(1)}, bf16[288,1024]{1,0:T(8,128)(2,1)S(1)}, u32[]{:S(2)}, u32[]{:S(2)}) collective-permute-start(bf16[288,1024]{1,0:T(8,128)(2,1)S(1)} %convolution_convert_fusion.2), channel_id=1, source_target_pairs={{0,4},{1,5},{2,6},{3,7},{4,0},{5,1},{6,2},{7,3},{8,12},{9,13},{10,... | collective-permute-start | bytes 1769480 | tf_op jit(solution)/shard_map/ppermute | solution.py:32
  110.0 14.4 %collective-permute-start.17 = (bf16[288,1024]{1,0:T(8,128)(2,1)S(1)}, bf16[288,1024]{1,0:T(8,128)(2,1)S(1)}, u32[]{:S(2)}, u32[]{:S(2)}) collective-permute-start(bf16[288,1024]{1,0:T(8,128)(2,1)S(1)} %fusion.4), channel_id=1, source_target_pairs={{0,4},{1,5},{2,6},{3,7},{4,0},{5,1},{6,2},{7,3},{8,12},{9,13},{10,... | collective-permute-start | bytes 1769480 | tf_op jit(solution)/shard_map/ppermute | solution.py:32
  112.4 12.0 %collective-permute-start.14 = (bf16[288,1024]{1,0:T(8,128)(2,1)S(1)}, bf16[288,1024]{1,0:T(8,128)(2,1)S(1)}, u32[]{:S(2)}, u32[]{:S(2)}) collective-permute-start(bf16[288,1024]{1,0:T(8,128)(2,1)S(1)} %fusion.3), channel_id=1, source_target_pairs={{0,12},{1,13},{2,14},{3,15},{4,8},{5,9},{6,10},{7,11},{8,4},{9,5},... | collective-permute-start | bytes 1769480 | tf_op jit(solution)/shard_map/ppermute | solution.py:32
  114.7 23.1 %copy-start.1 = (bf16[2304,512]{1,0:T(8,128)(2,1)S(1)}, bf16[2304,512]{1,0:T(8,128)(2,1)}, u32[]{:S(2)}) copy-start(bf16[2304,512]{1,0:T(8,128)(2,1)} %param.8) | copy-start | bytes 7077892
  125.4 8.4 %collective-permute-start.19 = (bf16[144,1024]{1,0:T(8,128)(2,1)S(1)}, bf16[144,1024]{1,0:T(8,128)(2,1)S(1)}, u32[]{:S(2)}, u32[]{:S(2)}) collective-permute-start(bf16[144,1024]{1,0:T(8,128)(2,1)S(1)} %get-tuple-element.31), channel_id=1, source_target_pairs={{0,2},{1,3},{2,0},{3,1},{4,6},{5,7},{6,4},{7,5},{8,10},{9,11},{10,... | collective-permute-start | bytes 884744 | tf_op jit(solution)/shard_map/ppermute | solution.py:32
  126.9 8.3 %collective-permute-start.20 = (bf16[144,1024]{1,0:T(8,128)(2,1)S(1)}, bf16[144,1024]{1,0:T(8,128)(2,1)S(1)}, u32[]{:S(2)}, u32[]{:S(2)}) collective-permute-start(bf16[144,1024]{1,0:T(8,128)(2,1)S(1)} %get-tuple-element.32), channel_id=1, source_target_pairs={{0,1},{1,0},{2,3},{3,2},{4,5},{5,4},{6,7},{7,6},{8,9},{9,8},{10,11... | collective-permute-start | bytes 884744 | tf_op jit(solution)/shard_map/ppermute | solution.py:32
  127.3 9.6 %collective-permute-start.21 = (bf16[144,1024]{1,0:T(8,128)(2,1)S(1)}, bf16[144,1024]{1,0:T(8,128)(2,1)S(1)}, u32[]{:S(2)}, u32[]{:S(2)}) collective-permute-start(bf16[144,1024]{1,0:T(8,128)(2,1)S(1)} %get-tuple-element.33), channel_id=1, source_target_pairs={{0,3},{1,2},{2,1},{3,0},{4,7},{5,6},{6,5},{7,4},{8,11},{9,10},{10,... | collective-permute-start | bytes 884744 | tf_op jit(solution)/shard_map/ppermute | solution.py:32
